TPU v7x, 32 devices: a whole 2x2x4 slice. The times are simulated.
32 devices in a mesh: groups: 2 (over y), rep: 4 (over z), tp: 2 (over x), sub: 2 (over core).
Axes of the slice: x: 2, y: 2, z: 4, core: 2. Of those that a mesh axis runs over, the one named last changes fastest.
Arguments:
- rec_hidden: bfloat16 [8, 512, 5120], P(('groups', 'rep'), ('tp', 'sub')), parts along dimension 0
- dec_hidden: bfloat16 [8, 9, 2, 5120], P(('groups', 'rep')), parts along dimension 0
- norm_gain: float32 [5120], replicated, may hold values from 0.5 to 1.5
- query_gain: float32 [128], replicated, may hold values from 2 to 4
- key_gain: float32 [128], replicated, may hold values from 0.5 to 1.5
- w_query: bfloat16 [5120, 8192], P('rep', ('tp', 'sub')), may hold values from -0.078125 to 0.078125
- w_key: bfloat16 [5120, 1024], P('rep', ('tp', 'sub')), may hold values from -0.078125 to 0.078125
- w_value: bfloat16 [5120, 1024], P('rep', ('tp', 'sub')), may hold values from -0.078125 to 0.078125
- pool_keys: bfloat16 [8, 40, 128, 1024], P(('groups', 'rep'), None, None, ('tp', 'sub')), parts along dimension 0, may hold values from -1.5 to 1.5
- pool_values: bfloat16 [8, 40, 128, 1024], P(('groups', 'rep'), None, None, ('tp', 'sub')), parts along dimension 0, may hold values from -6 to 6
- page_table: int32 [8, 8, 16], P(('groups', 'rep')), parts along dimension 0, may hold values from 0 to 39, as said below
- seq_lengths: int32 [8, 8], P('groups'), parts along dimension 0, may hold values from 0 to 2048, as said below
- listed_slot: int32 [8], P('groups'), parts along dimension 0, may hold values from 0 to 7
Outputs:
- rec_keys: bfloat16 [8, 512, 1024], P(('groups', 'rep'), None, ('tp', 'sub')), parts along dimension 0
- rec_values: bfloat16 [8, 512, 1024], P(('groups', 'rep'), None, ('tp', 'sub')), parts along dimension 0
- decoded: bfloat16 [8, 9, 2, 8192], P(('groups', 'rep'), None, None, ('tp', 'sub')), parts along dimension 0
There are 2 independent parts, one for each index of `groups`. A program takes and returns all parts, laid end to end along the dimension named above; an argument that names none is the same for every part. Nothing has to cross between parts.
Inputs may be any that keep to these rules, and one draw needn't show every extreme that they name: `seq_lengths`: the listed sequence of a replica r < 2 holds more than (14) * 128 tokens, the listed slot of any other replica holds 0; every other sequence holds 1 to 384 tokens. `page_table`: the first ceil(length / 128) entries of a sequence's row name pages of the replica's own pool, distinct over all sequences of the replica; the other entries name arbitrary pages of that pool.
All inputs are finite; a program needn't handle non-finite values.
Results may differ from a plain program's by a relative error of at most 0.0092.
Values may be sent and summed in bfloat16 or wider, within the bound.
No kernel may reach another device: no remote copies, remote signals or barrier semaphores. Data moves between devices by JAX's collectives and lax.ppermute only.
A program may use at most 128 MiB of HBM per device.

v0:
```python
import math

import jax
import jax.numpy as jnp
from jax import lax
from jax.sharding import PartitionSpec as P

EPSILON = 1e-06
ROPE_BASE = 1000000.0


def from_behind(value, axis, steps):
    count = lax.axis_size(axis)
    first, last = (max(0, -steps), min(count, count - steps))
    return lax.ppermute(value, axis, [(source, source + steps) for source in range(first, last)])


def normalize(states, gain):
    values = states.astype(jnp.float32)
    scale = lax.rsqrt(jnp.mean(values * values, axis=-1, keepdims=True) + EPSILON)
    return (values * scale * gain).astype(jnp.bfloat16)


def head_norm(values, gain):
    scale = lax.rsqrt(jnp.mean(values * values, axis=-1, keepdims=True) + EPSILON)
    return values * scale * gain


def rotate(values, positions):
    half_size = values.shape[-1] // 2
    freqs = jnp.exp(
        jnp.arange(half_size, dtype=jnp.float32) * (-2.0 * math.log(ROPE_BASE) / values.shape[-1])
    )
    angles = positions.astype(jnp.float32)[:, None] * freqs[None, :]
    cosine = jnp.cos(angles)[:, None, :]
    sine = jnp.sin(angles)[:, None, :]
    first = values[..., :half_size]
    second = values[..., half_size:]
    return jnp.concatenate(
        [first * cosine - second * sine, second * cosine + first * sine], axis=-1
    )


def keys_values(normed, weight_key, weight_value, key_gain, positions):
    rows = normed.shape[0]
    raw = jnp.dot(normed, weight_key, preferred_element_type=jnp.float32)
    heads = raw.reshape(rows, -1, key_gain.shape[0])
    keys = rotate(head_norm(heads, key_gain), positions).reshape(rows, -1).astype(jnp.bfloat16)
    values = jnp.dot(normed, weight_value, preferred_element_type=jnp.float32).astype(jnp.bfloat16)
    return (keys, values)


def queries_from(projected, query_gain, positions):
    rows = projected.shape[0]
    heads = projected.reshape(rows, -1, query_gain.shape[0])
    rotated = rotate(head_norm(heads, query_gain), positions)
    return (rotated * query_gain.shape[0] ** (-0.5)).reshape(rows, -1).astype(jnp.bfloat16)


def attend(queries, cache_keys, cache_values, new_keys, new_values, base_length, head_size):
    slots, steps, query_cols = queries.shape
    context = cache_keys.shape[1]
    kv_heads = cache_keys.shape[2] // head_size
    groups = query_cols // cache_keys.shape[2]
    grouped = queries.reshape(slots, steps, kv_heads, groups, head_size)
    stored_keys = cache_keys.reshape(slots, context, kv_heads, head_size)
    stored_values = cache_values.reshape(slots, context, kv_heads, head_size)
    fresh_keys = new_keys.reshape(slots, steps, kv_heads, head_size)
    fresh_values = new_values.reshape(slots, steps, kv_heads, head_size)
    old_scores = jnp.einsum(
        "stkgd,sckd->stkgc", grouped, stored_keys, preferred_element_type=jnp.float32
    )
    new_scores = jnp.einsum(
        "stkgd,sukd->stkgu", grouped, fresh_keys, preferred_element_type=jnp.float32
    )
    old_mask = (jnp.arange(context, dtype=jnp.int32)[None, :] < base_length[:, None])[
        :, None, None, None, :
    ]
    step_ids = jnp.arange(steps, dtype=jnp.int32)
    new_mask = (step_ids[None, :] <= step_ids[:, None])[None, :, None, None, :]
    old_exp = jnp.where(old_mask, jnp.exp(old_scores), jnp.float32(0.0))
    new_exp = jnp.where(new_mask, jnp.exp(new_scores), jnp.float32(0.0))
    total = jnp.sum(old_exp, axis=-1, keepdims=True) + jnp.sum(new_exp, axis=-1, keepdims=True)
    old_weights = (old_exp / total).astype(jnp.bfloat16)
    new_weights = (new_exp / total).astype(jnp.bfloat16)
    mixed = jnp.einsum(
        "stkgc,sckd->stkgd", old_weights, stored_values, preferred_element_type=jnp.float32
    )
    mixed = mixed + jnp.einsum(
        "stkgu,sukd->stkgd", new_weights, fresh_values, preferred_element_type=jnp.float32
    )
    return mixed.reshape(slots, steps, kv_heads * groups * head_size)


def body(
    rec_hidden,
    dec_hidden,
    norm_gain,
    query_gain,
    key_gain,
    w_query,
    w_key,
    w_value,
    pool_keys,
    pool_values,
    page_table,
    seq_lengths,
    listed_slot,
):
    replicas = lax.axis_size("rep")
    half_count = replicas // 2
    replica = lax.axis_index("rep")
    partner = (replica + half_count) % replicas
    is_busy = replica < half_count
    head_size = query_gain.shape[0]
    width = w_key.shape[1]
    slots = dec_hidden.shape[1]
    steps = dec_hidden.shape[2]
    seq_count = slots - 1
    context = page_table.shape[2] * pool_keys.shape[2]
    key_rows, value_rows = (
        lax.all_gather(w_key, "rep", axis=0, tiled=True),
        lax.all_gather(w_value, "rep", axis=0, tiled=True),
    )
    tokens = rec_hidden[0]
    piece = lax.all_gather(tokens, ("tp", "sub"), axis=0, tiled=True)
    normed = normalize(piece, norm_gain)
    positions = jnp.arange(piece.shape[0], dtype=jnp.int32)
    keys, values = keys_values(normed, key_rows, value_rows, key_gain, positions)
    joined = jnp.concatenate([keys, values], axis=1)
    rec_k = joined[:, :width]
    rec_v = joined[:, width:]
    hidden = dec_hidden[0].reshape(slots * steps, dec_hidden.shape[3])
    normed_new = normalize(hidden, norm_gain)
    spread = lax.all_to_all(normed_new, "rep", split_axis=1, concat_axis=0, tiled=True)
    projected = lax.psum_scatter(
        jnp.dot(spread, w_query, preferred_element_type=jnp.float32),
        "rep",
        scatter_dimension=0,
        tiled=True,
    )
    slot_ids = jnp.arange(seq_count, dtype=jnp.int32)
    mine = listed_slot[replica]
    theirs = listed_slot[partner]
    at_listed = slot_ids == mine
    moved_length = seq_lengths[partner, theirs]
    slot_length = jnp.where(at_listed, jnp.where(is_busy, 0, moved_length), seq_lengths[replica])
    base_length = jnp.concatenate([slot_length, jnp.full((1,), rec_k.shape[0], jnp.int32)])
    live = jnp.where(at_listed & is_busy, jnp.float32(0.0), jnp.float32(1.0))
    live = jnp.concatenate([live, jnp.ones((1,), jnp.float32)])
    positions_new = (base_length[:, None] + jnp.arange(steps, dtype=jnp.int32)[None, :]).reshape(-1)
    new_k, new_v = keys_values(normed_new, key_rows, value_rows, key_gain, positions_new)
    queries = queries_from(projected, query_gain, positions_new).reshape(slots, steps, -1)
    new_k = new_k.reshape(slots, steps, width)
    new_v = new_v.reshape(slots, steps, width)
    table = page_table[0]
    own_k = pool_keys[0][table].reshape(seq_count, context, width)
    own_v = pool_values[0][table].reshape(seq_count, context, width)
    padding = jnp.zeros((context - rec_k.shape[0], width), jnp.bfloat16)
    rec_slot_k = jnp.concatenate([rec_k, padding])[None]
    rec_slot_v = jnp.concatenate([rec_v, padding])[None]
    take_moved = at_listed & jnp.logical_not(is_busy)
    leaving = table[mine]
    leaving_k = pool_keys[0][leaving].reshape(context, width)
    leaving_v = pool_values[0][leaving].reshape(context, width)
    arrived_k, arrived_v = from_behind((leaving_k, leaving_v), "rep", half_count)
    cache_k = jnp.concatenate(
        [jnp.where(take_moved[:, None, None], arrived_k[None], own_k), rec_slot_k]
    )
    cache_v = jnp.concatenate(
        [jnp.where(take_moved[:, None, None], arrived_v[None], own_v), rec_slot_v]
    )
    mixed = attend(queries, cache_k, cache_v, new_k, new_v, base_length, head_size)
    decoded = (mixed * live[:, None, None]).astype(jnp.bfloat16)
    return (rec_k[None], rec_v[None], decoded[None])


def solution(mesh):
    in_specs = (
        P(("groups", "rep"), ("tp", "sub"), None),
        P(("groups", "rep"), None, None, None),
        P(),
        P(),
        P(),
        P("rep", ("tp", "sub")),
        P("rep", ("tp", "sub")),
        P("rep", ("tp", "sub")),
        P(("groups", "rep"), None, None, ("tp", "sub")),
        P(("groups", "rep"), None, None, ("tp", "sub")),
        P(("groups", "rep"), None, None),
        P("groups", None),
        P("groups"),
    )
    out_specs = (
        P(("groups", "rep"), None, ("tp", "sub")),
        P(("groups", "rep"), None, ("tp", "sub")),
        P(("groups", "rep"), None, None, ("tp", "sub")),
    )
    return jax.shard_map(body, mesh=mesh, in_specs=in_specs, out_specs=out_specs, check_vma=False)
```

profile of v0, /device:TPU:0, one launch (start us, length us, event | category | flops | bytes accessed | tf_op | source)
XLA Modules:
  0.0 328.9 jit_solution(12563098639127312207)
XLA Ops:
  8.7 1.3 fusion.37
  12.7 1.6 gather_fusion
  14.3 2.3 copy.67
  16.6 6.9 %collective-permute-start = (bf16[2048,256]{0,1:T(8,128)(2,1)}, bf16[2048,256]{0,1:T(8,128)(2,1)}, u32[]{:S(2)}, u32[]{:S(2)}) collective-permute-start(bf16[2048,256]{0,1:T(8,128)(2,1)} %copy.67), channel_id=1, source_target_pairs={{0,8},{4,12},{1,9},{5,13},{2,10},{6,14},{3,11},{7,15},{16,24},{20,... | collective-permute-start | bytes 3145736 | tf_op jit(solution)/shard_map/ppermute | solution.py:15
  23.6 3.3 %gather_fusion.2 = bf16[16,128,256]{2,1,0:T(8,128)(2,1)} fusion(bf16[40,128,256]{2,1,0:T(8,128)(2,1)} %bitcast.92, s32[1024]{0:T(1024)S(1)} %pad_clamp_fusion.1), kind=kCustom, calls=%fused_computation.2 | custom fusion | bytes 2097216 | tf_op jit(solution)/shard_map/gather | solution.py:164
  26.9 2.3 copy.70
  29.2 2.3 collective-permute-start.1
  32.8 3.4 %all-to-all-start = ((bf16[18,4,1280]{2,0,1:T(8,128)(2,1)}), bf16[18,4,1280]{2,0,1:T(8,128)(2,1)S(1)}, u32[]{:S(2)}, u32[]{:S(2)}) async-start(bf16[18,4,1280]{2,0,1:T(8,128)(2,1)} %fusion.24), calls=%async_computation | async-start | bytes 491520 | tf_op jit(solution)/shard_map/all_to_all | solution.py:135
  44.1 1.2 and_select_fusion
  45.3 1.2 multiply_cosine_fusion
  46.5 65.4 %all-to-all-done = bf16[18,4,1280]{2,0,1:T(8,128)(2,1)S(1)} async-done(((bf16[18,4,1280]{2,0,1:T(8,128)(2,1)}), bf16[18,4,1280]{2,0,1:T(8,128)(2,1)S(1)}, u32[]{:S(2)}, u32[]{:S(2)}) %all-to-all-start) | async-done | bytes 184352 | tf_op jit(solution)/shard_map/all_to_all | solution.py:135
  112.6 3.6 %fusion.40 = f32[72,2048]{1,0:T(8,128)S(1)} fusion(bf16[72,1280]{1,0:T(8,128)(2,1)} %all_to_all.14, bf16[1280,2048]{1,0:T(8,128)(2,1)} %param.18), kind=kOutput, calls=%fused_computation.94 | convolution fusion | flops 377487360 | bytes 6017024 | tf_op jit(solution)/shard_map/dot_general | solution.py:137
  116.3 104.9 %fusion = f32[24,2048]{1,0:T(8,128)} fusion(f32[72,2048]{1,0:T(8,128)S(1)} %fusion.40), kind=kCustom, calls=%all-reduce-scatter | all-reduce-scatter fusion | flops 196609 | bytes 786944
  221.2 1.6 slice.38
  222.8 2.0 collective-permute-start.2
  224.8 1.2 broadcast_and_fusion
  226.0 6.7 %gather_fusion.1 = bf16[128,128,256]{2,1,0:T(8,128)(2,1)} fusion(bf16[40,128,256]{2,1,0:T(8,128)(2,1)S(1)} %bitcast.91, s32[1024]{0:T(1024)S(1)} %pad_clamp_fusion), kind=kCustom, calls=%fused_computation.1 | custom fusion | bytes 16777728 | tf_op jit(solution)/shard_map/gather | solution.py:158
  232.6 8.3 %gather_fusion.3 = bf16[128,128,256]{2,1,0:T(8,128)(2,1)} fusion(bf16[40,128,256]{2,1,0:T(8,128)(2,1)} %bitcast.93, s32[1024]{0:T(1024)S(1)} %pad_clamp_fusion), kind=kCustom, calls=%fused_computation.3 | custom fusion | bytes 16777728 | tf_op jit(solution)/shard_map/gather | solution.py:157
  241.0 12.6 %reshape.430 = bf16[8,2048,2,128]{3,2,1,0:T(2,128)(2,1)} reshape(bf16[128,128,256]{2,1,0:T(8,128)(2,1)} %gather_fusion.1) | data formatting | bytes 16777216 | tf_op jit(solution)/shard_map/reshape | solution.py:158
  253.7 12.7 %reshape.431 = bf16[8,2048,2,128]{3,2,1,0:T(2,128)(2,1)} reshape(bf16[128,128,256]{2,1,0:T(8,128)(2,1)} %gather_fusion.3) | data formatting | bytes 16777216 | tf_op jit(solution)/shard_map/reshape | solution.py:157
  268.3 1.1 concatenate.45
  270.1 1.6 copy.44
  271.7 1.6 copy.49
  273.4 13.3 %copy_select_fusion.1 = (bf16[8,2048,2,128]{3,1,2,0:T(8,128)(2,1)}, bf16[8,2048,2,128]{3,1,2,0:T(8,128)(2,1)}) fusion(bf16[8,2048,2,128]{3,2,1,0:T(2,128)(2,1)} %reshape.430, pred[8]{0:T(512)(128)(4,1)S(1)} %copy-done.23, bf16[2048,2,128]{2,0,1:T(8,128)(2,1)S(1)} %copy.44, bf16[8,2048,2,128]{3,2,1,0:T(2,128)(2,1)} %reshape.431, ...), kind=kLoop, calls=%fused_computation.16 | loop fusion | flops 8388608 | bytes 35651592 | tf_op jit(solution)/shard_map/jit(_where)/select_n | solution.py:171
  286.7 3.0 copy.55
  290.9 2.4 convolution_convert_fusion
  293.9 3.6 %fusion.1 = f32[512]{0:T(512)S(1)} fusion(bf16[1,512,5120]{2,1,0:T(8,128)(2,1)} %all-gather.9.cloned.1.call-done), kind=kLoop, calls=%fused_computation.6 | loop fusion | flops 7863808 | bytes 5244928 | tf_op jit(solution)/shard_map/reduce_sum | solution.py:20
  297.5 4.4 %multiply_reduce_fusion = (f32[512,2]{0,1:T(2,128)S(1)}, f32[512,256]{0,1:T(8,128)S(1)}) fusion(bf16[5120,256]{1,0:T(8,128)(2,1)S(1)} %copy-done.3, bf16[1,512,5120]{2,1,0:T(8,128)(2,1)} %all-gather.9.cloned.1.call-done, f32[5120]{0:T(1024)S(1)} %copy-done.10, f32[512]{0:T(512)S(1)} %add_rsqrt_fusion.3), kind=kOutput, calls=%fused_computation.33 | convolution fusion | flops 1352924160 | bytes 8415232 | tf_op jit(solution)/shard_map/dot_general | solution.py:46
  303.3 5.2 %fusion.15 = bf16[512,256]{0,1:T(8,128)(2,1)S(1)} fusion(bf16[5120,256]{1,0:T(8,128)(2,1)} %all-gather.7.cloned.1.call-done, bf16[1,512,5120]{2,1,0:T(8,128)(2,1)} %all-gather.9.cloned.1.call-done, f32[5120]{0:T(1024)S(1)} %copy-done.11, f32[512]{0:T(512)S(1)} %add_rsqrt_fusion.3), kind=kOutput, calls=%fused_computation.23 | convolution fusion | flops 1352794112 | bytes 8148992 | tf_op jit(solution)/shard_map/dot_general | solution.py:49
  308.6 1.3 copy.47
  310.0 5.1 %fusion.38 = (f32[9,2,2,8]{3,1,2,0:T(2,128)S(1)}, f32[9,2,2,8,2048]{4,3,1,2,0:T(8,128)S(1)}) fusion(bf16[9,2,2,8,128]{4,3,2,1,0:T(8,128)(2,1)S(1)} %bitcast.108, bf16[1,2048,2,128]{3,1,2,0:T(8,128)(2,1)S(1)} %copy.52, bf16[8,2048,2,128]{3,1,2,0:T(8,128)(2,1)} %get-tuple-element.23, pred[9,2048]{1,0:T(8,128)(4,1)S(1)} %copy-done.16), kind=kOutput, calls=%fused_computation.92 | convolution fusion | flops 171048672 | bytes 11889792 | tf_op jit(solution)/shard_map/stkgd,sckd->stkgc/dot_general | solution.py:70
  315.4 4.4 %fusion.20 = f32[9,2,2,8,128]{4,3,1,2,0:T(8,128)S(1)} fusion(f32[9,2,128,2,8]{2,4,3,1,0:T(8,128)S(1)} %fusion.30, f32[9,2,2,8,2048]{4,3,1,2,0:T(8,128)S(1)} %get-tuple-element.31, f32[9,2,2,8]{3,1,2,0:T(2,128)S(1)} %add.168, bf16[1,2048,2,128]{3,1,2,0:T(8,128)(2,1)S(1)} %copy-done.5, bf16[8,2048,2,128]{3,1,2,0:T(8,128)(2,1)} %get-tuple-element.22), kind=kOutput, calls=%fused_computation.26 | convolution fusion | flops 171085824 | bytes 12092544 | tf_op jit(solution)/shard_map/stkgc,sckd->stkgd/dot_general | solution.py:86
  (125 shorter events, 17.2 us)
Async XLA Ops:
  7.2 5.5 %copy-start = (bf16[1,40,128,256]{3,2,1,0:T(8,128)(2,1)S(1)}, bf16[1,40,128,256]{3,2,1,0:T(8,128)(2,1)}, u32[]{:S(2)}) copy-start(bf16[1,40,128,256]{3,2,1,0:T(8,128)(2,1)} %param.22) | copy-start | bytes 7864324
  7.2 29.8 %copy-start.19 = (s32[1,8,16]{2,1,0:T(8,128)S(1)}, s32[1,8,16]{2,1,0:T(8,128)}, u32[]{:S(2)}) copy-start(s32[1,8,16]{2,1,0:T(8,128)} %param.23) | copy-start | bytes 1540
  7.2 24.2 %copy-start.2 = (bf16[1,9,2,5120]{3,2,1,0:T(2,128)(2,1)S(1)}, bf16[1,9,2,5120]{3,2,1,0:T(2,128)(2,1)}, u32[]{:S(2)}) copy-start(bf16[1,9,2,5120]{3,2,1,0:T(2,128)(2,1)} %param.14) | copy-start | bytes 552964
  7.2 24.8 %copy-start.9 = (f32[5120]{0:T(1024)S(1)}, f32[5120]{0:T(1024)}, u32[]{:S(2)}) copy-start(f32[5120]{0:T(1024)} %param.15) | copy-start | bytes 61444
  7.2 31.9 %copy-start.25 = (s32[4,8]{1,0:T(4,128)S(1)}, s32[4,8]{1,0:T(4,128)}, u32[]{:S(2)}) copy-start(s32[4,8]{1,0:T(4,128)} %param.24) | copy-start | bytes 388
  7.2 279.5 %all-gather.5.cloned.1.call-start = ((), (), s32[]{:S(2)}) async-start(), calls=%async_computation.1 | async-start | bytes 3276800 | tf_op jit(solution)/shard_map/all_gather | solution.py:122
  8.0 282.9 %all-gather.7.cloned.1.call-start = ((), (), s32[]{:S(2)}) async-start(), calls=%async_computation.2 | async-start | bytes 3276800 | tf_op jit(solution)/shard_map/all_gather | solution.py:123
  16.6 253.4 %collective-permute-start = (bf16[2048,256]{0,1:T(8,128)(2,1)}, bf16[2048,256]{0,1:T(8,128)(2,1)}, u32[]{:S(2)}, u32[]{:S(2)}) collective-permute-start(bf16[2048,256]{0,1:T(8,128)(2,1)} %copy.67), channel_id=1, source_target_pairs={{0,8},{4,12},{1,9},{5,13},{2,10},{6,14},{3,11},{7,15},{16,24},{20,... | collective-permute-start | bytes 3145736 | tf_op jit(solution)/shard_map/ppermute | solution.py:15
  29.2 242.6 %collective-permute-start.1 = (bf16[2048,256]{0,1:T(8,128)(2,1)}, bf16[2048,256]{0,1:T(8,128)(2,1)}, u32[]{:S(2)}, u32[]{:S(2)}) collective-permute-start(bf16[2048,256]{0,1:T(8,128)(2,1)} %copy.70), channel_id=1, source_target_pairs={{0,8},{4,12},{1,9},{5,13},{2,10},{6,14},{3,11},{7,15},{16,24},{20,... | collective-permute-start | bytes 3145736 | tf_op jit(solution)/shard_map/ppermute | solution.py:15
  32.0 79.9 %copy-start.17 = (f32[18]{0:T(128)}, f32[18]{0:T(128)S(1)}, u32[]{:S(2)}) copy-start(f32[18]{0:T(128)S(1)} %rsqrt.47) | copy-start | bytes 220
  32.8 79.1 %all-to-all-start = ((bf16[18,4,1280]{2,0,1:T(8,128)(2,1)}), bf16[18,4,1280]{2,0,1:T(8,128)(2,1)S(1)}, u32[]{:S(2)}, u32[]{:S(2)}) async-start(bf16[18,4,1280]{2,0,1:T(8,128)(2,1)} %fusion.24), calls=%async_computation | async-start | bytes 491520 | tf_op jit(solution)/shard_map/all_to_all | solution.py:135
  36.2 257.7 %all-gather.9.cloned.1.call-start = ((), (), s32[]{:S(2)}) async-start(), calls=%async_computation.3 | async-start | bytes 6553600 | tf_op jit(solution)/shard_map/all_gather | solution.py:126
  222.8 45.5 %collective-permute-start.2 = (f32[18,2048]{1,0:T(8,128)}, f32[18,2048]{1,0:T(8,128)}, u32[]{:S(2)}, u32[]{:S(2)}) collective-permute-start(f32[18,2048]{1,0:T(8,128)} %slice.38), channel_id=1, source_target_pairs={{0,4},{4,8},{8,12},{1,5},{5,9},{9,13},{2,6},{6,10},{10,14},{3,7},{... | collective-permute-start | bytes 442376
  253.6 12.7 %copy-start.6 = (bf16[1,9,2,5120]{3,2,1,0:T(2,128)(2,1)S(1)}, bf16[1,9,2,5120]{3,2,1,0:T(2,128)(2,1)}, u32[]{:S(2)}) copy-start(bf16[1,9,2,5120]{3,2,1,0:T(2,128)(2,1)} %multiply_convert_fusion.1) | copy-start | bytes 552964
  253.6 12.8 %copy-start.24 = (u32[32]{0:T(128)S(1)}, u32[32]{0:T(128)}, u32[]{:S(2)}) copy-start(u32[32]{0:T(128)} %constant.72) | copy-start | bytes 388
  253.6 14.0 %copy-start.26 = (f32[8]{0:T(128)S(1)}, f32[8]{0:T(128)}, u32[]{:S(2)}) copy-start(f32[8]{0:T(128)} %and_select_fusion) | copy-start | bytes 100
  253.6 14.7 %copy-start.4 = (f32[24,2048]{1,0:T(8,128)S(1)}, f32[24,2048]{1,0:T(8,128)}, u32[]{:S(2)}) copy-start(f32[24,2048]{1,0:T(8,128)} %fusion) | copy-start | bytes 589828
  253.6 16.1 %copy-start.21 = (f32[128]{0:T(128)S(1)}, f32[128]{0:T(128)}, u32[]{:S(2)}) copy-start(f32[128]{0:T(128)} %param.16) | copy-start | bytes 1540
  253.6 16.2 %copy-start.12 = (f32[18,64]{1,0:T(8,128)S(1)}, f32[18,64]{1,0:T(8,128)}, u32[]{:S(2)}) copy-start(f32[18,64]{1,0:T(8,128)} %get-tuple-element.21) | copy-start | bytes 13828
  253.7 19.7 %copy-start.23 = (pred[8]{0:T(512)(128)(4,1)S(1)}, pred[8]{0:T(512)(128)(4,1)}, u32[]{:S(2)}) copy-start(pred[8]{0:T(512)(128)(4,1)} %broadcast_and_fusion) | copy-start | bytes 28
  270.0 23.3 %copy-start.14 = (bf16[18,16,128]{2,1,0:T(8,128)(2,1)}, bf16[18,16,128]{2,1,0:T(8,128)(2,1)S(1)}, u32[]{:S(2)}) copy-start(bf16[18,16,128]{2,1,0:T(8,128)(2,1)S(1)} %fusion.27) | copy-start | bytes 221188
  273.4 17.3 %copy-start.20 = (f32[128]{0:T(128)S(1)}, f32[128]{0:T(128)}, u32[]{:S(2)}) copy-start(f32[128]{0:T(128)} %param.17) | copy-start | bytes 1540
  273.4 17.3 %copy-start.13 = (f32[18,64]{1,0:T(8,128)S(1)}, f32[18,64]{1,0:T(8,128)}, u32[]{:S(2)}) copy-start(f32[18,64]{1,0:T(8,128)} %get-tuple-element.21) | copy-start | bytes 13828
  273.4 17.5 %copy-start.10 = (f32[5120]{0:T(1024)S(1)}, f32[5120]{0:T(1024)}, u32[]{:S(2)}) copy-start(f32[5120]{0:T(1024)} %param.15) | copy-start | bytes 61444
  273.4 17.5 %copy-start.18 = (f32[18]{0:T(128)S(1)}, f32[18]{0:T(128)}, u32[]{:S(2)}) copy-start(f32[18]{0:T(128)} %copy-done.17) | copy-start | bytes 220
  286.7 6.7 %copy-start.27 = (pred[2,2]{1,0:T(4,128)(4,1)S(1)}, pred[2,2]{1,0:T(4,128)(4,1)}, u32[]{:S(2)}) copy-start(pred[2,2]{1,0:T(4,128)(4,1)} %iota_compare_fusion.1) | copy-start | bytes 16
  290.6 6.9 %copy-start.3 = (bf16[5120,256]{1,0:T(8,128)(2,1)S(1)}, bf16[5120,256]{1,0:T(8,128)(2,1)}, u32[]{:S(2)}) copy-start(bf16[5120,256]{1,0:T(8,128)(2,1)} %all-gather.5.cloned.1.call-done) | copy-start | bytes 7864324
  297.5 5.7 %copy-start.11 = (f32[5120]{0:T(1024)S(1)}, f32[5120]{0:T(1024)}, u32[]{:S(2)}) copy-start(f32[5120]{0:T(1024)} %param.15) | copy-start | bytes 61444
  303.3 6.7 %copy-start.15 = (bf16[18,16,128]{2,1,0:T(8,128)(2,1)S(1)}, bf16[18,16,128]{2,1,0:T(8,128)(2,1)}, u32[]{:S(2)}) copy-start(bf16[18,16,128]{2,1,0:T(8,128)(2,1)} %copy-done.14) | copy-start | bytes 221188
  303.3 6.7 %copy-start.16 = (pred[9,2048]{1,0:T(8,128)(4,1)S(1)}, pred[9,2048]{1,0:T(8,128)(4,1)}, u32[]{:S(2)}) copy-start(pred[9,2048]{1,0:T(8,128)(4,1)} %iota_compare_fusion) | copy-start | bytes 55300
  315.3 7.0 %copy-start.1 = (bf16[1,40,128,256]{3,2,1,0:T(8,128)(2,1)S(1)}, bf16[1,40,128,256]{3,2,1,0:T(8,128)(2,1)}, u32[]{:S(2)}) copy-start(bf16[1,40,128,256]{3,2,1,0:T(8,128)(2,1)} %param.22) | copy-start | bytes 7864324
  315.4 6.2 %copy-start.22 = (f32[9]{0:T(128)S(1)}, f32[9]{0:T(128)}, u32[]{:S(2)}) copy-start(f32[9]{0:T(128)} %pad_maximum_fusion.1) | copy-start | bytes 112
  (3 other events, 14.6 us)
Sparse Core Ops, SparseCore 0:
  9.6 93.1 all-gather.4
  104.4 83.8 all-gather.6
  189.9 55.2 all-gather.8
where the time goes:
time: 330 us; the launch traced here: 329 us
  blocking collectives  105 us (32%)
  waiting for transfers between devices  67.5 us (20%)
  local copies, waits for them, and re-layouts  67 us (20%)
  other arithmetic  28.4 us (9%)
  matrix products  26.8 us (8%)
  between operations  19.6 us (6%)
  starting transfers between devices  14.7 us (4%)
    unnamed x1, blocking collectives  105 us
    all_to_all x1, waiting for transfers between devices, body(): lax.all_to_all(normed_new, 'rep', split_axis=1, concat_axis=0, tiled=True)  65.4 us
    select_n x1, other arithmetic, body(): jnp.where(take_moved[:, None, None], arrived_v[None], own_v)  13.3 us
    reshape x1, local copies, waits for them, and re-layouts, body(): own_k = pool_keys[0][table].reshape(seq_count, context, width)  12.7 us
    reshape x1, local copies, waits for them, and re-layouts, body(): own_v = pool_values[0][table].reshape(seq_count, context, width)  12.6 us
    ppermute x2, starting transfers between devices, from_behind(): lax.ppermute(value, axis, [(source, source + steps) for source in range(f...  9.22 us
    gather x1, local copies, waits for them, and re-layouts, body(): own_k = pool_keys[0][table].reshape(seq_count, context, width)  8.32 us
    dot_general x2, matrix products, keys_values(): jnp.dot(normed, weight_value, preferred_element_type=jnp.float32)  7.64 us
  transfers between devices with their start and end apart: 7, of which 1 were waited for; matrix products, arithmetic and copies ran while one was open for 60% of the time, Pallas kernels for 0%

commit v1 on v0

v1 whole, which is shorter than its diff:
```python
import functools
import math

import jax
import jax.numpy as jnp
from jax import lax
from jax.experimental import pallas as pl
from jax.experimental.pallas import tpu as pltpu
from jax.sharding import PartitionSpec as P

EPSILON = 1e-06
ROPE_BASE = 1000000.0
KEEP_PAGES = 3
VMEM_BYTES = 56 * 2**20
F32 = jnp.float32
BF16 = jnp.bfloat16

WHOLE = pl.BlockSpec(memory_space=pltpu.VMEM)
SCALAR = pl.BlockSpec(memory_space=pltpu.SMEM)


def call(kernel, outs, ins, scalars, scratch=(), flops=0, **grid):
    bytes_accessed = sum(math.prod(a.shape) * a.dtype.itemsize for a in list(ins) + list(outs))
    return pl.pallas_call(
        kernel,
        out_shape=tuple(outs),
        in_specs=[SCALAR] * len(scalars) + [WHOLE] * len(ins),
        out_specs=tuple([WHOLE] * len(outs)),
        scratch_shapes=list(scratch),
        compiler_params=pltpu.CompilerParams(vmem_limit_bytes=VMEM_BYTES),
        cost_estimate=pl.CostEstimate(flops=flops, bytes_accessed=bytes_accessed, transcendentals=0),
    )(*scalars, *ins)


def shaped(shape, dtype):
    return jax.ShapeDtypeStruct(shape, dtype)


def dot(a, b):
    return jnp.dot(a, b, preferred_element_type=F32)


def dot_rows(a, b):
    return lax.dot_general(a, b, (((1,), (1,)), ((), ())), preferred_element_type=F32)


def xor_permute(value, axis, distance):
    count = lax.axis_size(axis)
    return lax.ppermute(value, axis, [(i, i ^ distance) for i in range(count)])


def head_scale(values):
    return lax.rsqrt(jnp.mean(values * values, axis=-1, keepdims=True) + EPSILON)


def rotate_rows(values, cosine, sine):
    return values * cosine + pltpu.roll(values, values.shape[-1] // 2, values.ndim - 1) * sine


def rope_tables(positions, head_size):
    half_size = head_size // 2
    freqs = jnp.exp(jnp.arange(half_size, dtype=F32) * (-2.0 * math.log(ROPE_BASE) / head_size))
    angles = positions.astype(F32)[:, None] * freqs[None, :]
    cosine, sine = jnp.cos(angles), jnp.sin(angles)
    return jnp.concatenate([cosine, cosine], axis=1), jnp.concatenate([-sine, sine], axis=1)


def normalize(states, gain):
    values = states.astype(F32)
    return (values * head_scale(values) * gain).astype(BF16)


def norm_spread_kernel(x_ref, gain_ref, *outs):
    replica = lax.axis_index("rep")
    width = outs[0].shape[1]
    values = x_ref[...].astype(F32)
    scale = head_scale(values)
    for k, out in enumerate(outs):
        at = pl.multiple_of((replica ^ k) * width, 128)
        part = x_ref[:, pl.ds(at, width)].astype(F32)
        out[...] = (part * scale * gain_ref[:, pl.ds(at, width)]).astype(BF16)


def project_kernel(count, slots, steps, listed_ref, *refs):
    rows = refs[:count]
    wq_ref, wk_ref, wv_ref = refs[count : count + 3]
    outs = refs[count + 3 : 2 * count + 3]
    stacked = refs[2 * count + 3]
    replica = lax.axis_index("rep")
    half = count // 2
    step = pl.program_id(0)
    per = slots * steps

    @pl.when(step == 0)
    def _():
        for k in range(count):
            own = rows[k][...].astype(F32)
            other = rows[k ^ half][...].astype(F32)
            busy = (replica ^ k) < half
            mine = listed_ref[replica ^ k]
            theirs = listed_ref[replica ^ k ^ half]
            ids = lax.broadcasted_iota(jnp.int32, (per, 1), 0)
            for t in range(steps):
                moved = jnp.sum(jnp.where(ids == theirs * steps + t, other, 0.0), axis=0, keepdims=True)
                own = jnp.where((ids == mine * steps + t) & busy, moved, own)
            stacked[k, :per, :] = own.astype(BF16)

    lhs = stacked[...].reshape(-1, stacked.shape[2])
    pad = stacked.shape[1]
    last = pl.num_programs(0) - 1

    @pl.when(step < last)
    def _():
        product = dot(lhs, wq_ref[...])
        for k in range(count):
            outs[k][...] = product[k * pad : k * pad + per].astype(outs[k].dtype)

    @pl.when(step == last)
    def _():
        product = jnp.concatenate([dot(lhs, wk_ref[...]), dot(lhs, wv_ref[...])], axis=1)
        for k in range(count):
            outs[k][...] = product[k * pad : k * pad + per].astype(outs[k].dtype)


def project_new(rows, listed, w_query, w_key, w_value, slots, steps):
    count = len(rows)
    per, depth = rows[0].shape
    block = 2 * w_key.shape[1]
    blocks = w_query.shape[1] // block
    pad = -(-per // 16) * 16
    total = w_query.shape[1] + block
    return pl.pallas_call(
        functools.partial(project_kernel, count, slots, steps),
        grid=(blocks + 1,),
        out_shape=tuple(shaped((per, total), F32) for _ in rows),
        in_specs=[SCALAR]
        + [pl.BlockSpec((per, depth), lambda j: (0, 0)) for _ in rows]
        + [
            pl.BlockSpec((depth, block), lambda j: (0, jnp.minimum(j, blocks - 1))),
            pl.BlockSpec(w_key.shape, lambda j: (0, 0)),
            pl.BlockSpec(w_value.shape, lambda j: (0, 0)),
        ],
        out_specs=tuple(pl.BlockSpec((per, block), lambda j: (0, j)) for _ in rows),
        scratch_shapes=[pltpu.VMEM((count, pad, depth), BF16)],
        compiler_params=pltpu.CompilerParams(vmem_limit_bytes=VMEM_BYTES),
        cost_estimate=pl.CostEstimate(
            flops=2 * count * per * depth * total, bytes_accessed=2 * depth * total, transcendentals=0
        ),
    )(listed, *rows, w_query, w_key, w_value)


def spread_heads(rows, kv_heads):
    heads = kv_heads * 8
    ids = lax.broadcasted_iota(jnp.int32, (rows.shape[0], 1), 0) % heads // 8
    return jnp.concatenate([jnp.where(ids == k, rows, 0.0) for k in range(kv_heads)], axis=1)


def own_head(wide, kv_heads):
    size = wide.shape[1] // kv_heads
    heads = kv_heads * 8
    ids = lax.broadcasted_iota(jnp.int32, (wide.shape[0], 1), 0) % heads // 8
    total = wide[:, :size]
    for k in range(1, kv_heads):
        total = jnp.where(ids == k, wide[:, k * size : (k + 1) * size], total)
    return total


def attend_kernel(parts, seq_count, steps, table_ref, lengths_ref, listed_ref, *refs):
    sums = refs[:parts]
    (cos_ref, sin_ref, qgain_ref, kgain_ref, keys_ref, values_ref) = refs[parts : parts + 6]
    num_ref, den_ref, moved_ref, last_ref = refs[parts + 6 : parts + 10]
    q3, k3, v3 = refs[parts + 10 :]
    replica = lax.axis_index("rep")
    half = lax.axis_size("rep") // 2
    size = qgain_ref.shape[1]
    width = keys_ref.shape[2]
    page = keys_ref.shape[1]
    kv_heads = width // size
    heads = kv_heads * 8
    slots = seq_count + 1

    def total(at):
        value = sums[0][:, at : at + size].astype(F32)
        for other in sums[1:]:
            value = value + other[:, at : at + size].astype(F32)
        return value

    cosine, sine = cos_ref[...], sin_ref[...]
    for h in range(heads):
        x = total(h * size)
        x = rotate_rows(x * head_scale(x) * qgain_ref[...], cosine, sine) * size**-0.5
        q3[:, h, :] = x.astype(BF16).astype(F32)
    for h in range(kv_heads):
        x = total((heads + h) * size)
        x = rotate_rows(x * head_scale(x) * kgain_ref[...], cosine, sine).astype(BF16).astype(F32)
        k3[:, h * 8 : h * 8 + 8, :] = jnp.broadcast_to(x[:, None, :], (x.shape[0], 8, size))
        v = total((heads + kv_heads + h) * size).astype(BF16).astype(F32)
        v3[:, h * 8 : h * 8 + 8, :] = jnp.broadcast_to(v[:, None, :], (x.shape[0], 8, size))

    def old_terms(rows, page_of, length, pages, first):
        num, den = None, None
        for i in range(pages):
            at = first + i
            scores = dot_rows(rows, keys_ref[page_of(at)])
            ids = lax.broadcasted_iota(jnp.int32, scores.shape, 1) + at * page
            weights = jnp.where(ids < length, jnp.exp(scores), 0.0)
            part = jnp.sum(weights, axis=-1, keepdims=True)
            mixed = dot(weights.astype(BF16), values_ref[page_of(at)])
            num = mixed if num is None else num + mixed
            den = part if den is None else den + part
        return num, den

    def rows_of(slot):
        return q3[pl.ds(slot * steps, steps)].reshape(steps * heads, size)

    for slot in range(slots):
        q = q3[slot * steps : (slot + 1) * steps]
        k = k3[slot * steps : (slot + 1) * steps]
        v = v3[slot * steps : (slot + 1) * steps]
        nums, dens = [], []
        for t in range(steps):
            num, den = None, None
            for u in range(t + 1):
                e = jnp.exp(jnp.sum(q[t] * k[u], axis=-1, keepdims=True))
                num = e * v[u] if num is None else num + e * v[u]
                den = e if den is None else den + e
            nums.append(num)
            dens.append(den)
        num, den = jnp.concatenate(nums, axis=0), jnp.concatenate(dens, axis=0)
        rows = spread_heads(rows_of(slot), kv_heads).astype(BF16)
        if slot < seq_count:
            old_num, old_den = old_terms(
                rows, lambda at: table_ref[slot, at], lengths_ref[replica, slot], KEEP_PAGES, 0
            )
            num = num + own_head(old_num, kv_heads)
            den = den + old_den
        else:
            last_ref[...] = rows
        num_ref[slot * steps : (slot + 1) * steps] = num.reshape(steps, heads, size)
        den_ref[slot * steps : (slot + 1) * steps] = jnp.broadcast_to(den, num.shape).reshape(
            steps, heads, size
        )

    moved_ref[...] = jnp.zeros_like(moved_ref)

    @pl.when(replica < half)
    def _():
        slot = listed_ref[replica]
        length = lengths_ref[replica, slot]
        rows = spread_heads(rows_of(slot), kv_heads).astype(BF16)
        pages = table_ref.shape[1]
        at_once = 4

        def turn(i, carry):
            num, den = old_terms(rows, lambda at: table_ref[slot, at], length, at_once, i * at_once)
            return carry[0] + num, carry[1] + den

        num, den = lax.fori_loop(
            0,
            pages // at_once,
            turn,
            (jnp.zeros((steps * heads, width), F32), jnp.zeros((steps * heads, 1), F32)),
        )
        num = own_head(num, kv_heads)
        moved_ref[0] = num
        moved_ref[1] = jnp.broadcast_to(den, num.shape)


def norm_blocks_kernel(x_ref, gain_ref, out_ref):
    width = out_ref.shape[2]
    values = x_ref[...].astype(F32)
    scale = head_scale(values)
    for k, at in enumerate(half_blocks()):
        at = pl.multiple_of(at * width, 128)
        part = x_ref[:, pl.ds(at, width)].astype(F32)
        out_ref[k] = (part * scale * gain_ref[:, pl.ds(at, width)]).astype(BF16)


def half_blocks():
    replica, group = lax.axis_index("rep"), lax.axis_index("groups")
    second = jnp.where(replica < 2, 2, 1)
    third = jnp.where(replica < 2, 3, 0)
    order = [2 * replica, 2 * replica + 1]
    for source in (replica ^ 1, second, third):
        order += [2 * source + group, 2 * source + 1 - group]
    return order


def first_kernel(*refs):
    xs = refs[:4]
    wk_ref, wv_ref, a_ref, ya_ref, b_ref, c_ref, yb_ref, yc_ref, acc_ref = refs[4:]
    replica = lax.axis_index("rep")
    middle = (replica == 1) | (replica == 2)
    width = wk_ref.shape[1]
    depth = a_ref.shape[0]

    def block(k):
        return jnp.concatenate([x[k] for x in xs], axis=0)

    keys, values = None, None
    for k in range(2):
        x = block(k)
        more_k = dot(x, wk_ref[k * depth : (k + 1) * depth])
        more_v = dot(x, wv_ref[k * depth : (k + 1) * depth])
        keys = more_k if keys is None else keys + more_k
        values = more_v if values is None else values + more_v
    acc_ref[:, :width] = keys
    acc_ref[:, width:] = values
    acc_ref[...] += dot(block(2), a_ref[...])
    acc_ref[...] += dot(block(3), ya_ref[...])

    @pl.when(middle)
    def _():
        acc_ref[...] += dot(block(4), b_ref[...])
        acc_ref[...] += dot(block(5), yb_ref[...])

    @pl.when(jnp.logical_not(middle))
    def _():
        acc_ref[...] += dot(block(4), c_ref[...])
        acc_ref[...] += dot(block(5), yc_ref[...])


def tail_kernel(far, steps, listed_ref, *refs):
    if far:
        xs, (d_ref, e_ref, yd_ref, ye_ref) = refs[:4], refs[4:8]
        refs = refs[8:]
    acc_ref, cos_ref, sin_ref, kgain_ref, rows_ref, num_ref, den_ref, moved_ref = refs[:8]
    keys_ref, values_ref, out_ref, o3 = refs[8:12]
    replica = lax.axis_index("rep")
    half = lax.axis_size("rep") // 2
    tokens, width = keys_ref.shape
    size = kgain_ref.shape[1]
    kv_heads = width // size
    heads = kv_heads * 8
    slots = num_ref.shape[0] // steps

    if far:
        fresh = refs[12]
        middle = (replica == 1) | (replica == 2)

        def block(k):
            return jnp.concatenate([x[k] for x in xs], axis=0)

        @pl.when(middle)
        def _():
            fresh[...] = acc_ref[...] + dot(block(6), d_ref[...]) + dot(block(7), yd_ref[...])

        @pl.when(jnp.logical_not(middle))
        def _():
            fresh[...] = acc_ref[...] + dot(block(6), e_ref[...]) + dot(block(7), ye_ref[...])

        tp, sub = lax.axis_index("tp"), lax.axis_index("sub")
        places = [tp * 2 + sub, (tp ^ 1) * 2 + sub, tp * 2 + (sub ^ 1), (tp ^ 1) * 2 + (sub ^ 1)]
    else:
        fresh, places = acc_ref, [0]
    chunk = tokens // len(places)
    for i, place in enumerate(places):
        if len(places) > 1:
            place = pl.ds(pl.multiple_of(place * chunk, chunk), chunk)
        else:
            place = pl.ds(0, chunk)
        cosine, sine = cos_ref[place, :], sin_ref[place, :]
        for h in range(kv_heads):
            x = fresh[i * chunk : (i + 1) * chunk, h * size : (h + 1) * size]
            x = rotate_rows(x * head_scale(x) * kgain_ref[...], cosine, sine)
            keys_ref[place, h * size : (h + 1) * size] = x.astype(BF16)
        values_ref[place, :] = fresh[i * chunk : (i + 1) * chunk, width:].astype(BF16)

    weights = jnp.exp(dot_rows(rows_ref[...], keys_ref[...]))
    old_num = own_head(dot(weights.astype(BF16), values_ref[...]), kv_heads)
    old_den = jnp.sum(weights, axis=-1, keepdims=True)
    at = (slots - 1) * steps
    o3[:at] = num_ref[:at] / den_ref[:at]
    o3[at:] = (num_ref[at:] + old_num.reshape(steps, heads, size)) / (
        den_ref[at:] + jnp.broadcast_to(old_den, old_num.shape).reshape(steps, heads, size)
    )
    mine = pl.ds(listed_ref[replica] * steps, steps)
    live = jnp.where(replica < half, 0.0, 1.0)
    o3[mine] = (
        live
        * (num_ref[mine] + moved_ref[0].reshape(steps, heads, size))
        / (den_ref[mine] + moved_ref[1].reshape(steps, heads, size))
    )
    for h in range(heads):
        out_ref[:, h * size : (h + 1) * size] = o3[:, h, :].astype(BF16)


def line_pairs(pairs, axis="rep"):
    return lambda value: lax.ppermute(value, axis, pairs)


def across_groups(value, replicas):
    count = lax.axis_size("rep")
    pairs = [(g * count + r, (1 - g) * count + r) for g in range(2) for r in replicas]
    return lax.ppermute(value, ("groups", "rep"), pairs)


def body(
    rec_hidden,
    dec_hidden,
    norm_gain,
    query_gain,
    key_gain,
    w_query,
    w_key,
    w_value,
    pool_keys,
    pool_values,
    page_table,
    seq_lengths,
    listed_slot,
):
    replicas = lax.axis_size("rep")
    half = replicas // 2
    replica = lax.axis_index("rep")
    partner = (replica + half) % replicas
    head_size = query_gain.shape[0]
    width = w_key.shape[1]
    depth = w_key.shape[0]
    _, slots, steps, features = dec_hidden.shape
    seq_count = slots - 1
    per = slots * steps
    heads = w_query.shape[1] // head_size
    gain = norm_gain[None]
    qgain, kgain = query_gain[None], key_gain[None]
    table = page_table[0]
    tokens = rec_hidden.shape[1] * lax.axis_size("tp") * lax.axis_size("sub")
    near = (
        replicas == 4
        and lax.axis_size("tp") == 2
        and lax.axis_size("sub") == 2
        and lax.axis_size("groups") == 2
    )

    if near:
        group = lax.axis_index("groups")
        rows = depth // 2
        own = jnp.concatenate(
            [lax.dynamic_slice_in_dim(w, group * rows, rows, 0) for w in (w_key, w_value)], axis=1
        )
        from_a = line_pairs([(0, 1), (1, 0), (2, 3), (3, 2)])(own)
        from_b = line_pairs([(1, 2), (2, 1)])(own)

    hidden = dec_hidden[0].reshape(per, features)
    if near:
        spread = call(
            norm_spread_kernel, [shaped((per, depth), BF16)] * replicas, [hidden, gain], []
        )
        spread = [spread[0]] + [xor_permute(spread[k], "rep", k) for k in range(1, replicas)]
        sums = project_new(spread, listed_slot, w_query, w_key, w_value, slots, steps)
        sums = [sums[0]] + [xor_permute(sums[k], "rep", k) for k in range(1, replicas)]
    else:
        spread = lax.all_to_all(
            normalize(hidden, norm_gain), "rep", split_axis=1, concat_axis=0, tiled=True
        ).reshape(replicas, slots, steps, depth)
        moved = jnp.take_along_axis(spread, listed_slot[:, None, None, None], axis=1)
        moved = jnp.roll(moved, half, axis=0)
        ids = jnp.arange(replicas)[:, None]
        swap = (jnp.arange(slots)[None] == listed_slot[:, None]) & (ids < half)
        spread = jnp.where(swap[:, :, None, None], moved, spread).reshape(replicas * per, depth)
        weights = jnp.concatenate([w_query, w_key, w_value], axis=1)
        sums = [
            lax.psum_scatter(
                jnp.dot(spread, weights, preferred_element_type=F32),
                "rep",
                scatter_dimension=0,
                tiled=True,
            )
        ]

    rec_cos, rec_sin = rope_tables(jnp.arange(tokens, dtype=jnp.int32), head_size)
    if near:
        (blocks,) = call(
            norm_blocks_kernel,
            [shaped((2 * replicas, rec_hidden.shape[1], rows), BF16)],
            [rec_hidden[0], gain],
            [],
        )
        across = xor_permute(blocks, "tp", 1)
        xs = [blocks, across, xor_permute(blocks, "sub", 1), xor_permute(across, "sub", 1)]
        from_d = line_pairs([(1, 2), (2, 1)])(from_a)
        from_c = line_pairs([(1, 0), (2, 3)])(from_b)
        over_a = across_groups(from_a, range(4))
        over_b = across_groups(from_b, (1, 2))
        from_e = line_pairs([(1, 0), (2, 3)])(from_d)
        over_c = across_groups(from_c, (0, 3))
        over_d = across_groups(from_d, (1, 2))
        over_e = across_groups(from_e, (0, 3))
        (acc,) = call(
            first_kernel,
            [shaped((tokens, 2 * width), F32)],
            [*xs, w_key, w_value, from_a, over_a, from_b, from_c, over_b, over_c],
            [],
            flops=3 * depth * tokens * width * 4,
        )
        far = [*xs, from_d, from_e, over_d, over_e]
    else:
        normed = lax.all_gather(
            normalize(rec_hidden[0], norm_gain), ("tp", "sub"), axis=0, tiled=True
        )
        acc = jnp.concatenate(
            [
                jnp.dot(
                    normed,
                    lax.all_gather(w, "rep", axis=0, tiled=True),
                    preferred_element_type=F32,
                )
                for w in (w_key, w_value)
            ],
            axis=1,
        )
        far = []

    lengths = seq_lengths[replica]
    arriving = (jnp.arange(seq_count) == listed_slot[replica]) & (replica >= half)
    moved_length = seq_lengths[partner, listed_slot[partner]]
    base = jnp.concatenate(
        [jnp.where(arriving, moved_length, lengths), jnp.full((1,), tokens, jnp.int32)]
    )
    positions = (base[:, None] + jnp.arange(steps, dtype=jnp.int32)[None, :]).reshape(-1)
    cosine, sine = rope_tables(positions, head_size)
    flat = (per, heads, head_size)
    num, den, moved, rows_last = call(
        functools.partial(attend_kernel, len(sums), seq_count, steps),
        [
            shaped(flat, F32),
            shaped(flat, F32),
            shaped((2, steps * heads, head_size), F32),
            shaped((steps * heads, width), BF16),
        ],
        [*sums, cosine, sine, qgain, kgain, pool_keys[0], pool_values[0]],
        [table, seq_lengths, listed_slot],
        scratch=[pltpu.VMEM(flat, F32)] * 3,
    )
    moved = lax.ppermute(moved, "rep", [(i, i + half) for i in range(half)])

    rec_k, rec_v, decoded = call(
        functools.partial(tail_kernel, bool(far), steps),
        [
            shaped((tokens, width), BF16),
            shaped((tokens, width), BF16),
            shaped((per, heads * head_size), BF16),
        ],
        [*far, acc, rec_cos, rec_sin, kgain, rows_last, num, den, moved],
        [listed_slot],
        scratch=[pltpu.VMEM(flat, F32)] + [pltpu.VMEM((tokens, 2 * width), F32)] * bool(far),
        flops=depth * tokens * width * 4,
    )
    return (rec_k[None], rec_v[None], decoded.reshape(1, slots, steps, heads * head_size))


def solution(mesh):
    in_specs = (
        P(("groups", "rep"), ("tp", "sub"), None),
        P(("groups", "rep"), None, None, None),
        P(),
        P(),
        P(),
        P("rep", ("tp", "sub")),
        P("rep", ("tp", "sub")),
        P("rep", ("tp", "sub")),
        P(("groups", "rep"), None, None, ("tp", "sub")),
        P(("groups", "rep"), None, None, ("tp", "sub")),
        P(("groups", "rep"), None, None),
        P("groups", None),
        P("groups"),
    )
    out_specs = (
        P(("groups", "rep"), None, ("tp", "sub")),
        P(("groups", "rep"), None, ("tp", "sub")),
        P(("groups", "rep"), None, None, ("tp", "sub")),
    )
    return jax.shard_map(body, mesh=mesh, in_specs=in_specs, out_specs=out_specs, check_vma=False)
```

time: 330 us -> 130 us (0.39)
  blocking collectives: 105 us -> 0 us
  local copies, waits for them, and re-layouts: 67 us -> 6.21 us
  Pallas kernels: 0 us -> 33.4 us
  matrix products: 26.8 us -> 0 us
  other arithmetic: 28.4 us -> 4.35 us
  starting transfers between devices: 14.7 us -> 31.8 us
  between operations: 19.6 us -> 2.93 us
  waiting for transfers between devices: 67.5 us -> 51.1 us
    unnamed x1 -> x0, blocking collectives: 105 us -> none
    all_to_all x1 -> x0, waiting for transfers between devices: 65.4 us -> none  [body(): lax.all_to_all(normed_new, 'rep', split_axis=1, concat_axis=0, tiled=True)]
    ppermute x2 -> x20, waiting for transfers between devices: 0.01 us -> 51.1 us  [the longest x9 35.7 us: xor_permute(): return lax.ppermute(value, axis, [(i, i ^ distance) for i in range(count)])]
    pallas_call x0 -> x6, Pallas kernels: none -> 33.4 us  [the longest x5 27.3 us: call(): pl.pallas_call(kernel, out_shape=tuple(outs), in_specs=[SCALAR] * len(sca...]
    reshape x5 -> x1, local copies, waits for them, and re-layouts: 29.9 us -> 1.59 us  [body(): decoded.reshape(1, slots, steps, heads * head_size)]
    dot_general x9 -> x0, matrix products: 26.8 us -> none  [the longest x2 7.64 us: keys_values(): jnp.dot(normed, weight_value, preferred_element_type=jnp.float32)]
    ppermute x2 -> x20, starting transfers between devices: 9.22 us -> 31.8 us  [the longest x9 12.7 us: xor_permute(): return lax.ppermute(value, axis, [(i, i ^ distance) for i in range(count)])]
    gather x4 -> x0, local copies, waits for them, and re-layouts: 20 us -> none  [the longest x1 8.32 us: body(): own_k = pool_keys[0][table].reshape(seq_count, context, width)]
  transfers between devices with their start and end apart: 7 -> 20, of which waited for: 1 -> 7; matrix products, arithmetic and copies ran while one was open for 60% -> 5% of each run, Pallas kernels for 0% -> 18%
where the time goes in v1:
time: 130 us
  waiting for transfers between devices  51.1 us (39%)
  Pallas kernels  33.4 us (26%)
  starting transfers between devices  31.8 us (24%)
  local copies, waits for them, and re-layouts  6.21 us (5%)
  other arithmetic  4.35 us (3%)
  between operations  2.93 us (2%)
    ppermute x9, waiting for transfers between devices, xor_permute(): return lax.ppermute(value, axis, [(i, i ^ distance) for i in range(count)])  35.7 us
    pallas_call x5, Pallas kernels, call(): pl.pallas_call(kernel, out_shape=tuple(outs), in_specs=[SCALAR] * len(sca...  27.3 us
    ppermute x5, waiting for transfers between devices, across_groups(): return lax.ppermute(value, ('groups', 'rep'), pairs)  13.8 us
    ppermute x9, starting transfers between devices, xor_permute(): return lax.ppermute(value, axis, [(i, i ^ distance) for i in range(count)])  12.7 us
    ppermute x5, starting transfers between devices, line_pairs(): return lambda value: lax.ppermute(value, axis, pairs)  9.2 us
    ppermute x5, starting transfers between devices, across_groups(): return lax.ppermute(value, ('groups', 'rep'), pairs)  8.57 us
    pallas_call x1, Pallas kernels, project_new(): pl.pallas_call(functools.partial(project_kernel, count, slots, steps), gr...  6.07 us
  transfers between devices with their start and end apart: 20, of which 7 were waited for; matrix products, arithmetic and copies ran while one was open for 5% of the time, Pallas kernels for 18%

profile of v1, /device:TPU:0, one launch (start us, length us, event | category | flops | bytes accessed | tf_op | source)
XLA Modules:
  0.0 129.8 jit_solution(12630538679653186483)
XLA Ops:
  0.7 3.2 %shard_map.148.refs_0_ = bf16[8,128,640]{2,1,0:T(8,128)(2,1)} custom-call(bf16[128,5120]{1,0:T(8,128)(2,1)} %bitcast.18, f32[1,5120]{1,0:T(1,128)} %bitcast.19), custom_call_target="tpu_custom_call" | custom-call | bytes 2641920 | tf_op jit(solution)/shard_map/pallas_call | solution.py:24
  3.9 2.9 %collective-permute-start = (bf16[8,128,640]{2,1,0:T(8,128)(2,1)}, bf16[8,128,640]{2,1,0:T(8,128)(2,1)S(1)}, u32[]{:S(2)}, u32[]{:S(2)}) collective-permute-start(bf16[8,128,640]{2,1,0:T(8,128)(2,1)} %shard_map.148.refs_0_), channel_id=1, source_target_pairs={{0,2},{2,0},{1,3},{3,1},{4,6},{6,4},{5,7},{7,5},{8,10},{10,8},{9,1... | collective-permute-start | bytes 3932168 | tf_op jit(solution)/shard_map/ppermute | solution.py:49
  7.6 4.4 %collective-permute-start.3 = (bf16[640,512]{1,0:T(8,128)(2,1)S(1)}, bf16[640,512]{1,0:T(8,128)(2,1)}, u32[]{:S(2)}, u32[]{:S(2)}) collective-permute-start(bf16[640,512]{1,0:T(8,128)(2,1)S(1)} %pad_maximum_fusion), channel_id=1, source_target_pairs={{0,4},{4,0},{8,12},{12,8},{1,5},{5,1},{9,13},{13,9},{2,6},{6,2},{1... | collective-permute-start | bytes 1966088 | tf_op jit(solution)/shard_map/ppermute | solution.py:389
  12.8 1.8 %shard_map.150 = (bf16[18,1280]{1,0:T(8,128)(2,1)}, bf16[18,1280]{1,0:T(8,128)(2,1)}, bf16[18,1280]{1,0:T(8,128)(2,1)}, bf16[18,1280]{1,0:T(8,128)(2,1)}) custom-call(bf16[18,5120]{1,0:T(8,128)(2,1)} %reshape_squeeze.3.x_ref, f32[1,5120]{1,0:T(1,128)} %bitcast.20), custom_call_target="tpu_custom_call" | custom-call | bytes 389120 | tf_op jit(solution)/shard_map/pallas_call | solution.py:24
  14.7 1.9 %collective-permute-start.14 = (bf16[18,1280]{1,0:T(8,128)(2,1)}, bf16[18,1280]{1,0:T(8,128)(2,1)S(1)}, u32[]{:S(2)}, u32[]{:S(2)}) collective-permute-start(bf16[18,1280]{1,0:T(8,128)(2,1)} %get-tuple-element.20), channel_id=1, source_target_pairs={{0,8},{4,12},{8,0},{12,4},{1,9},{5,13},{9,1},{13,5},{2,10},{6,14},... | collective-permute-start | bytes 138248 | tf_op jit(solution)/shard_map/ppermute | solution.py:49
  16.6 12.3 %collective-permute-done.13.refs_1_ = bf16[18,1280]{1,0:T(8,128)(2,1)S(1)} collective-permute-done((bf16[18,1280]{1,0:T(8,128)(2,1)}, bf16[18,1280]{1,0:T(8,128)(2,1)S(1)}, u32[]{:S(2)}, u32[]{:S(2)}) %collective-permute-start.13) | collective-permute-done | bytes 46112 | tf_op jit(solution)/shard_map/ppermute | solution.py:49
  28.9 1.2 collective-permute-start.15
  30.1 1.3 collective-permute-start.10
  31.4 1.5 %collective-permute-start.4 = (bf16[640,512]{1,0:T(8,128)(2,1)}, bf16[640,512]{1,0:T(8,128)(2,1)}, u32[]{:S(2)}, u32[]{:S(2)}) collective-permute-start(bf16[640,512]{1,0:T(8,128)(2,1)} %collective-permute-done.3.refs_6_), channel_id=1, source_target_pairs={{4,8},{8,4},{5,9},{9,5},{6,10},{10,6},{7,11},{11,7},{20,24},{24,20... | collective-permute-start | bytes 1966088 | tf_op jit(solution)/shard_map/ppermute | solution.py:389
  32.9 2.3 %collective-permute-done.15.refs_3_ = bf16[18,1280]{1,0:T(8,128)(2,1)S(1)} collective-permute-done((bf16[18,1280]{1,0:T(8,128)(2,1)}, bf16[18,1280]{1,0:T(8,128)(2,1)S(1)}, u32[]{:S(2)}, u32[]{:S(2)}) %collective-permute-start.15) | collective-permute-done | bytes 46112 | tf_op jit(solution)/shard_map/ppermute | solution.py:49
  35.9 6.1 %shard_map.151 = (f32[18,2560]{1,0:T(8,128)}, f32[18,2560]{1,0:T(8,128)}, f32[18,2560]{1,0:T(8,128)}, f32[18,2560]{1,0:T(8,128)}) custom-call(s32[4]{0:T(128)} %listed_ref.5, bf16[18,1280]{1,0:T(8,128)(2,1)} %get-tuple-element.18.refs_0_, bf16[18,1280]{1,0:T(8,128)(2,1)} %copy-done.10, bf16[18,1280]{1,0:T(8,128)(2,1)} %copy-done.11, ...), custom_call_target="tpu_custom_call" | custom-call | flops 471859200 | bytes 6553600 | tf_op jit(solution)/shard_map/pallas_call | solution.py:132
  41.9 3.4 %collective-permute-start.16 = (f32[18,2560]{1,0:T(8,128)}, f32[18,2560]{1,0:T(8,128)S(1)}, u32[]{:S(2)}, u32[]{:S(2)}) collective-permute-start(f32[18,2560]{1,0:T(8,128)} %get-tuple-element.23), channel_id=1, source_target_pairs={{0,4},{4,0},{8,12},{12,8},{1,5},{5,1},{9,13},{13,9},{2,6},{6,2},{1... | collective-permute-start | bytes 552968 | tf_op jit(solution)/shard_map/ppermute | solution.py:49
  45.3 8.3 %collective-permute-done.16.refs_1_ = f32[18,2560]{1,0:T(8,128)S(1)} collective-permute-done((f32[18,2560]{1,0:T(8,128)}, f32[18,2560]{1,0:T(8,128)S(1)}, u32[]{:S(2)}, u32[]{:S(2)}) %collective-permute-start.16) | collective-permute-done | bytes 184352 | tf_op jit(solution)/shard_map/ppermute | solution.py:49
  53.7 2.7 %collective-permute-start.18 = (f32[18,2560]{1,0:T(8,128)}, f32[18,2560]{1,0:T(8,128)}, u32[]{:S(2)}, u32[]{:S(2)}) collective-permute-start(f32[18,2560]{1,0:T(8,128)} %get-tuple-element.25), channel_id=1, source_target_pairs={{0,12},{4,8},{8,4},{12,0},{1,13},{5,9},{9,5},{13,1},{2,14},{6,10},... | collective-permute-start | bytes 552968 | tf_op jit(solution)/shard_map/ppermute | solution.py:49
  56.4 12.8 %collective-permute-done.17.refs_2_ = f32[18,2560]{1,0:T(8,128)} collective-permute-done((f32[18,2560]{1,0:T(8,128)}, f32[18,2560]{1,0:T(8,128)}, u32[]{:S(2)}, u32[]{:S(2)}) %collective-permute-start.17) | collective-permute-done | bytes 184352 | tf_op jit(solution)/shard_map/ppermute | solution.py:49
  69.2 1.5 %collective-permute-start.11 = (bf16[640,512]{1,0:T(8,128)(2,1)S(1)}, bf16[640,512]{1,0:T(8,128)(2,1)}, u32[]{:S(2)}, u32[]{:S(2)}) collective-permute-start(bf16[640,512]{1,0:T(8,128)(2,1)S(1)} %collective-permute-done.9.refs_8_), channel_id=1, source_target_pairs={{4,20},{8,24},{20,4},{24,8},{5,21},{9,25},{21,5},{25,9},{6,22},{10... | collective-permute-start | bytes 1966088 | tf_op jit(solution)/shard_map/ppermute | solution.py:395
  74.6 1.3 %and_select_fusion = s32[8]{0:T(128)S(1)} fusion(pred[]{:T(512)S(6)} %ge.3, s32[4,8]{1,0:T(4,128)S(1)} %copy-done.15, s32[]{:T(128)S(6)} %select_n.27, s32[]{:T(128)} %bitcast.6, s32[]{:T(128)} %bitcast.4), kind=kLoop, calls=%fused_computation.13 | loop fusion | flops 24 | bytes 77 | tf_op jit(solution)/shard_map/jit(_where)/select_n | solution.py:518
  76.1 1.5 %collective-permute-start.8 = (bf16[640,512]{1,0:T(8,128)(2,1)}, bf16[640,512]{1,0:T(8,128)(2,1)}, u32[]{:S(2)}, u32[]{:S(2)}) collective-permute-start(bf16[640,512]{1,0:T(8,128)(2,1)} %collective-permute-done.3.refs_6_), channel_id=1, source_target_pairs={{0,16},{4,20},{8,24},{12,28},{16,0},{20,4},{24,8},{28,12},{1,17},{... | collective-permute-start | bytes 1966088 | tf_op jit(solution)/shard_map/ppermute | solution.py:395
  77.6 1.3 collective-permute-start.5
  79.1 2.4 %collective-permute-start.12 = (bf16[640,512]{1,0:T(8,128)(2,1)}, bf16[640,512]{1,0:T(8,128)(2,1)S(1)}, u32[]{:S(2)}, u32[]{:S(2)}) collective-permute-start(bf16[640,512]{1,0:T(8,128)(2,1)} %collective-permute-done.10.refs_9_), channel_id=1, source_target_pairs={{0,16},{12,28},{16,0},{28,12},{1,17},{13,29},{17,1},{29,13},{2,18}... | collective-permute-start | bytes 1966088 | tf_op jit(solution)/shard_map/ppermute | solution.py:395
  82.3 11.7 %collective-permute-done.8.refs_7_ = bf16[640,512]{1,0:T(8,128)(2,1)} collective-permute-done((bf16[640,512]{1,0:T(8,128)(2,1)}, bf16[640,512]{1,0:T(8,128)(2,1)}, u32[]{:S(2)}, u32[]{:S(2)}) %collective-permute-start.8) | collective-permute-done | bytes 655392 | tf_op jit(solution)/shard_map/ppermute | solution.py:395
  94.7 1.6 %collective-permute-done.5.refs_5_ = bf16[640,512]{1,0:T(8,128)(2,1)} collective-permute-done((bf16[640,512]{1,0:T(8,128)(2,1)}, bf16[640,512]{1,0:T(8,128)(2,1)}, u32[]{:S(2)}, u32[]{:S(2)}) %collective-permute-start.5) | collective-permute-done | bytes 655392 | tf_op jit(solution)/shard_map/ppermute | solution.py:389
  96.2 2.4 %collective-permute-start.7 = (bf16[640,512]{1,0:T(8,128)(2,1)}, bf16[640,512]{1,0:T(8,128)(2,1)S(1)}, u32[]{:S(2)}, u32[]{:S(2)}) collective-permute-start(bf16[640,512]{1,0:T(8,128)(2,1)} %collective-permute-done.5.refs_5_), channel_id=1, source_target_pairs={{0,16},{12,28},{16,0},{28,12},{1,17},{13,29},{17,1},{29,13},{2,18}... | collective-permute-start | bytes 1966088 | tf_op jit(solution)/shard_map/ppermute | solution.py:395
  98.7 1.0 fusion
  99.7 1.0 pad_maximum_fusion.1
  100.7 8.4 %shard_map.152 = (f32[18,16,128]{2,1,0:T(8,128)}, f32[18,16,128]{2,1,0:T(8,128)}, f32[2,32,128]{2,1,0:T(8,128)}, bf16[32,256]{1,0:T(8,128)(2,1)}) custom-call(s32[8,16]{1,0:T(8,128)} %bitcast.21, s32[4,8]{1,0:T(4,128)} %lengths_ref.1, s32[4]{0:T(128)} %listed_ref.5, f32[18,2560]{1,0:T(8,128)} %get-tuple-element.22.refs_0_, f32[18,2560]{1,0:T(8,128)} %copy-done.8, ...), custom_call_target="tpu_custom_call" | custom-call | bytes 6343680 | tf_op jit(solution)/shard_map/pallas_call | solution.py:24
  109.1 1.3 collective-permute-start.19
  111.2 7.7 %shard_map.149.refs_8_ = f32[512,512]{1,0:T(8,128)} custom-call(bf16[8,128,640]{2,1,0:T(8,128)(2,1)} %shard_map.148.refs_0_, bf16[8,128,640]{2,1,0:T(8,128)(2,1)} %copy-done.1, bf16[8,128,640]{2,1,0:T(8,128)(2,1)} %collective-permute-done.1.refs_2_, bf16[8,128,640]{2,1,0:T(8,128)(2,1)} %collective-permute-done.2.refs_3_, bf16[1280,256]{1,0:T(8,128)(2,1)} %refs_5_.3, ...), custom_call_target="tpu_custom_call" | custom-call | flops 2013265920 | bytes 11534336 | tf_op jit(solution)/shard_map/pallas_call | solution.py:24
  119.0 2.1 %collective-permute-done.7.refs_7_ = bf16[640,512]{1,0:T(8,128)(2,1)S(1)} collective-permute-done((bf16[640,512]{1,0:T(8,128)(2,1)}, bf16[640,512]{1,0:T(8,128)(2,1)S(1)}, u32[]{:S(2)}, u32[]{:S(2)}) %collective-permute-start.7) | collective-permute-done | bytes 655392 | tf_op jit(solution)/shard_map/ppermute | solution.py:395
  121.1 0.9 copy-done.7
  122.0 6.2 %shard_map.153 = (bf16[512,256]{1,0:T(8,128)(2,1)}, bf16[512,256]{1,0:T(8,128)(2,1)}, bf16[18,2048]{1,0:T(8,128)(2,1)}) custom-call(s32[4]{0:T(128)} %listed_ref.5, bf16[8,128,640]{2,1,0:T(8,128)(2,1)} %shard_map.148.refs_0_, bf16[8,128,640]{2,1,0:T(8,128)(2,1)} %copy-done.1, bf16[8,128,640]{2,1,0:T(8,128)(2,1)} %collective-permute-done.1.refs_2_, ...), custom_call_target="tpu_custom_call" | custom-call | flops 671088640 | bytes 10379776 | tf_op jit(solution)/shard_map/pallas_call | solution.py:24
  128.2 1.6 %reshape.34 = bf16[1,9,2,2048]{3,2,1,0:T(2,128)(2,1)} reshape(bf16[18,2048]{1,0:T(8,128)(2,1)} %get-tuple-element.32) | data formatting | bytes 147456 | tf_op jit(solution)/shard_map/reshape | solution.py:549
  (62 shorter events, 6.7 us)
Async XLA Ops:
  0.6 6.2 %copy-start.2 = (bf16[1280,256]{1,0:T(8,128)(2,1)S(1)}, bf16[1280,256]{1,0:T(8,128)(2,1)}, u32[]{:S(2)}) copy-start(bf16[1280,256]{1,0:T(8,128)(2,1)} %refs_6_.1) | copy-start | bytes 1966084
  0.6 6.2 %copy-start.3 = (bf16[1280,256]{1,0:T(8,128)(2,1)S(1)}, bf16[1280,256]{1,0:T(8,128)(2,1)}, u32[]{:S(2)}) copy-start(bf16[1280,256]{1,0:T(8,128)(2,1)} %refs_5_.3) | copy-start | bytes 1966084
  3.9 70.2 %collective-permute-start = (bf16[8,128,640]{2,1,0:T(8,128)(2,1)}, bf16[8,128,640]{2,1,0:T(8,128)(2,1)S(1)}, u32[]{:S(2)}, u32[]{:S(2)}) collective-permute-start(bf16[8,128,640]{2,1,0:T(8,128)(2,1)} %shard_map.148.refs_0_), channel_id=1, source_target_pairs={{0,2},{2,0},{1,3},{3,1},{4,6},{6,4},{5,7},{7,5},{8,10},{10,8},{9,1... | collective-permute-start | bytes 3932168 | tf_op jit(solution)/shard_map/ppermute | solution.py:49
  6.8 5.2 %copy-start.9 = (bf16[1,9,2,5120]{3,2,1,0:T(2,128)(2,1)S(1)}, bf16[1,9,2,5120]{3,2,1,0:T(2,128)(2,1)}, u32[]{:S(2)}) copy-start(bf16[1,9,2,5120]{3,2,1,0:T(2,128)(2,1)} %param.14) | copy-start | bytes 552964
  6.9 23.2 %collective-permute-start.9 = (bf16[640,512]{1,0:T(8,128)(2,1)S(1)}, bf16[640,512]{1,0:T(8,128)(2,1)S(1)}, u32[]{:S(2)}, u32[]{:S(2)}) collective-permute-start(bf16[640,512]{1,0:T(8,128)(2,1)S(1)} %pad_maximum_fusion), channel_id=1, source_target_pairs={{4,8},{8,4},{5,9},{9,5},{6,10},{10,6},{7,11},{11,7},{20,24},{24,20... | collective-permute-start | bytes 1966088 | tf_op jit(solution)/shard_map/ppermute | solution.py:389
  7.6 23.8 %collective-permute-start.3 = (bf16[640,512]{1,0:T(8,128)(2,1)S(1)}, bf16[640,512]{1,0:T(8,128)(2,1)}, u32[]{:S(2)}, u32[]{:S(2)}) collective-permute-start(bf16[640,512]{1,0:T(8,128)(2,1)S(1)} %pad_maximum_fusion), channel_id=1, source_target_pairs={{0,4},{4,0},{8,12},{12,8},{1,5},{5,1},{9,13},{13,9},{2,6},{6,2},{1... | collective-permute-start | bytes 1966088 | tf_op jit(solution)/shard_map/ppermute | solution.py:389
  14.7 14.2 %collective-permute-start.13 = (bf16[18,1280]{1,0:T(8,128)(2,1)}, bf16[18,1280]{1,0:T(8,128)(2,1)S(1)}, u32[]{:S(2)}, u32[]{:S(2)}) collective-permute-start(bf16[18,1280]{1,0:T(8,128)(2,1)} %get-tuple-element.19), channel_id=1, source_target_pairs={{0,4},{4,0},{8,12},{12,8},{1,5},{5,1},{9,13},{13,9},{2,6},{6,2},{1... | collective-permute-start | bytes 138248 | tf_op jit(solution)/shard_map/ppermute | solution.py:49
  14.7 18.3 %collective-permute-start.14 = (bf16[18,1280]{1,0:T(8,128)(2,1)}, bf16[18,1280]{1,0:T(8,128)(2,1)S(1)}, u32[]{:S(2)}, u32[]{:S(2)}) collective-permute-start(bf16[18,1280]{1,0:T(8,128)(2,1)} %get-tuple-element.20), channel_id=1, source_target_pairs={{0,8},{4,12},{8,0},{12,4},{1,9},{5,13},{9,1},{13,5},{2,10},{6,14},... | collective-permute-start | bytes 138248 | tf_op jit(solution)/shard_map/ppermute | solution.py:49
  28.9 6.3 %copy-start.10 = (bf16[18,1280]{1,0:T(8,128)(2,1)}, bf16[18,1280]{1,0:T(8,128)(2,1)S(1)}, u32[]{:S(2)}) copy-start(bf16[18,1280]{1,0:T(8,128)(2,1)S(1)} %collective-permute-done.13.refs_1_) | copy-start | bytes 138244
  28.9 6.3 %collective-permute-start.15 = (bf16[18,1280]{1,0:T(8,128)(2,1)}, bf16[18,1280]{1,0:T(8,128)(2,1)S(1)}, u32[]{:S(2)}, u32[]{:S(2)}) collective-permute-start(bf16[18,1280]{1,0:T(8,128)(2,1)} %get-tuple-element.21), channel_id=1, source_target_pairs={{0,12},{4,8},{8,4},{12,0},{1,13},{5,9},{9,5},{13,1},{2,14},{6,10},... | collective-permute-start | bytes 138248 | tf_op jit(solution)/shard_map/ppermute | solution.py:49
  30.1 39.0 %copy-start.4 = (bf16[640,512]{1,0:T(8,128)(2,1)}, bf16[640,512]{1,0:T(8,128)(2,1)S(1)}, u32[]{:S(2)}) copy-start(bf16[640,512]{1,0:T(8,128)(2,1)S(1)} %collective-permute-done.9.refs_8_) | copy-start | bytes 1966084
  30.1 45.9 %collective-permute-start.10 = (bf16[640,512]{1,0:T(8,128)(2,1)S(1)}, bf16[640,512]{1,0:T(8,128)(2,1)}, u32[]{:S(2)}, u32[]{:S(2)}) collective-permute-start(bf16[640,512]{1,0:T(8,128)(2,1)S(1)} %collective-permute-done.9.refs_8_), channel_id=1, source_target_pairs={{4,0},{8,12},{5,1},{9,13},{6,2},{10,14},{7,3},{11,15},{20,16},{24,... | collective-permute-start | bytes 1966088 | tf_op jit(solution)/shard_map/ppermute | solution.py:389
  31.4 46.2 %collective-permute-start.4 = (bf16[640,512]{1,0:T(8,128)(2,1)}, bf16[640,512]{1,0:T(8,128)(2,1)}, u32[]{:S(2)}, u32[]{:S(2)}) collective-permute-start(bf16[640,512]{1,0:T(8,128)(2,1)} %collective-permute-done.3.refs_6_), channel_id=1, source_target_pairs={{4,8},{8,4},{5,9},{9,5},{6,10},{10,6},{7,11},{11,7},{20,24},{24,20... | collective-permute-start | bytes 1966088 | tf_op jit(solution)/shard_map/ppermute | solution.py:389
  32.9 2.3 %copy-start.11 = (bf16[18,1280]{1,0:T(8,128)(2,1)}, bf16[18,1280]{1,0:T(8,128)(2,1)S(1)}, u32[]{:S(2)}) copy-start(bf16[18,1280]{1,0:T(8,128)(2,1)S(1)} %collective-permute-done.14.refs_2_) | copy-start | bytes 138244
  35.8 34.9 %copy-start.14 = (s32[4]{0:T(128)S(1)}, s32[4]{0:T(128)}, u32[]{:S(2)}) copy-start(s32[4]{0:T(128)} %listed_ref.5) | copy-start | bytes 52
  35.8 37.6 %copy-start.15 = (s32[4,8]{1,0:T(4,128)S(1)}, s32[4,8]{1,0:T(4,128)}, u32[]{:S(2)}) copy-start(s32[4,8]{1,0:T(4,128)} %lengths_ref.1) | copy-start | bytes 388
  35.8 38.3 %copy-start = (bf16[8,128,640]{2,1,0:T(8,128)(2,1)S(1)}, bf16[8,128,640]{2,1,0:T(8,128)(2,1)}, u32[]{:S(2)}) copy-start(bf16[8,128,640]{2,1,0:T(8,128)(2,1)} %shard_map.148.refs_0_) | copy-start | bytes 3932164
  41.9 11.8 %collective-permute-start.16 = (f32[18,2560]{1,0:T(8,128)}, f32[18,2560]{1,0:T(8,128)S(1)}, u32[]{:S(2)}, u32[]{:S(2)}) collective-permute-start(f32[18,2560]{1,0:T(8,128)} %get-tuple-element.23), channel_id=1, source_target_pairs={{0,4},{4,0},{8,12},{12,8},{1,5},{5,1},{9,13},{13,9},{2,6},{6,2},{1... | collective-permute-start | bytes 552968 | tf_op jit(solution)/shard_map/ppermute | solution.py:49
  45.3 23.8 %collective-permute-start.17 = (f32[18,2560]{1,0:T(8,128)}, f32[18,2560]{1,0:T(8,128)}, u32[]{:S(2)}, u32[]{:S(2)}) collective-permute-start(f32[18,2560]{1,0:T(8,128)} %get-tuple-element.24), channel_id=1, source_target_pairs={{0,8},{4,12},{8,0},{12,4},{1,9},{5,13},{9,1},{13,5},{2,10},{6,14},... | collective-permute-start | bytes 552968 | tf_op jit(solution)/shard_map/ppermute | solution.py:49
  53.7 47.0 %copy-start.8 = (f32[18,2560]{1,0:T(8,128)}, f32[18,2560]{1,0:T(8,128)S(1)}, u32[]{:S(2)}) copy-start(f32[18,2560]{1,0:T(8,128)S(1)} %collective-permute-done.16.refs_1_) | copy-start | bytes 552964
  53.7 20.4 %collective-permute-start.18 = (f32[18,2560]{1,0:T(8,128)}, f32[18,2560]{1,0:T(8,128)}, u32[]{:S(2)}, u32[]{:S(2)}) collective-permute-start(f32[18,2560]{1,0:T(8,128)} %get-tuple-element.25), channel_id=1, source_target_pairs={{0,12},{4,8},{8,4},{12,0},{1,13},{5,9},{9,5},{13,1},{2,14},{6,10},... | collective-permute-start | bytes 552968 | tf_op jit(solution)/shard_map/ppermute | solution.py:49
  69.2 9.9 %collective-permute-start.11 = (bf16[640,512]{1,0:T(8,128)(2,1)S(1)}, bf16[640,512]{1,0:T(8,128)(2,1)}, u32[]{:S(2)}, u32[]{:S(2)}) collective-permute-start(bf16[640,512]{1,0:T(8,128)(2,1)S(1)} %collective-permute-done.9.refs_8_), channel_id=1, source_target_pairs={{4,20},{8,24},{20,4},{24,8},{5,21},{9,25},{21,5},{25,9},{6,22},{10... | collective-permute-start | bytes 1966088 | tf_op jit(solution)/shard_map/ppermute | solution.py:395
  74.1 34.9 %collective-permute-start.1 = (bf16[8,128,640]{2,1,0:T(8,128)(2,1)S(1)}, bf16[8,128,640]{2,1,0:T(8,128)(2,1)}, u32[]{:S(2)}, u32[]{:S(2)}) collective-permute-start(bf16[8,128,640]{2,1,0:T(8,128)(2,1)S(1)} %copy-done), channel_id=1, source_target_pairs={{0,1},{1,0},{2,3},{3,2},{4,5},{5,4},{6,7},{7,6},{8,9},{9,8},{10,11... | collective-permute-start | bytes 3932168 | tf_op jit(solution)/shard_map/ppermute | solution.py:49
  74.1 34.9 %copy-start.1 = (bf16[8,128,640]{2,1,0:T(8,128)(2,1)}, bf16[8,128,640]{2,1,0:T(8,128)(2,1)S(1)}, u32[]{:S(2)}) copy-start(bf16[8,128,640]{2,1,0:T(8,128)(2,1)S(1)} %collective-permute-done.refs_1_) | copy-start | bytes 3932164
  74.1 36.2 %collective-permute-start.2 = (bf16[8,128,640]{2,1,0:T(8,128)(2,1)S(1)}, bf16[8,128,640]{2,1,0:T(8,128)(2,1)}, u32[]{:S(2)}, u32[]{:S(2)}) collective-permute-start(bf16[8,128,640]{2,1,0:T(8,128)(2,1)S(1)} %collective-permute-done.refs_1_), channel_id=1, source_target_pairs={{0,1},{1,0},{2,3},{3,2},{4,5},{5,4},{6,7},{7,6},{8,9},{9,8},{10,11... | collective-permute-start | bytes 3932168 | tf_op jit(solution)/shard_map/ppermute | solution.py:49
  76.1 17.9 %collective-permute-start.8 = (bf16[640,512]{1,0:T(8,128)(2,1)}, bf16[640,512]{1,0:T(8,128)(2,1)}, u32[]{:S(2)}, u32[]{:S(2)}) collective-permute-start(bf16[640,512]{1,0:T(8,128)(2,1)} %collective-permute-done.3.refs_6_), channel_id=1, source_target_pairs={{0,16},{4,20},{8,24},{12,28},{16,0},{20,4},{24,8},{28,12},{1,17},{... | collective-permute-start | bytes 1966088 | tf_op jit(solution)/shard_map/ppermute | solution.py:395
  77.6 18.6 %collective-permute-start.5 = (bf16[640,512]{1,0:T(8,128)(2,1)}, bf16[640,512]{1,0:T(8,128)(2,1)}, u32[]{:S(2)}, u32[]{:S(2)}) collective-permute-start(bf16[640,512]{1,0:T(8,128)(2,1)} %collective-permute-done.4.refs_4_), channel_id=1, source_target_pairs={{4,0},{8,12},{5,1},{9,13},{6,2},{10,14},{7,3},{11,15},{20,16},{24,... | collective-permute-start | bytes 1966088 | tf_op jit(solution)/shard_map/ppermute | solution.py:389
  79.1 31.3 %collective-permute-start.12 = (bf16[640,512]{1,0:T(8,128)(2,1)}, bf16[640,512]{1,0:T(8,128)(2,1)S(1)}, u32[]{:S(2)}, u32[]{:S(2)}) collective-permute-start(bf16[640,512]{1,0:T(8,128)(2,1)} %collective-permute-done.10.refs_9_), channel_id=1, source_target_pairs={{0,16},{12,28},{16,0},{28,12},{1,17},{13,29},{17,1},{29,13},{2,18}... | collective-permute-start | bytes 1966088 | tf_op jit(solution)/shard_map/ppermute | solution.py:395
  94.0 25.0 %collective-permute-start.6 = (bf16[640,512]{1,0:T(8,128)(2,1)}, bf16[640,512]{1,0:T(8,128)(2,1)S(1)}, u32[]{:S(2)}, u32[]{:S(2)}) collective-permute-start(bf16[640,512]{1,0:T(8,128)(2,1)} %collective-permute-done.4.refs_4_), channel_id=1, source_target_pairs={{4,20},{8,24},{20,4},{24,8},{5,21},{9,25},{21,5},{25,9},{6,22},{10... | collective-permute-start | bytes 1966088 | tf_op jit(solution)/shard_map/ppermute | solution.py:395
  96.2 24.9 %collective-permute-start.7 = (bf16[640,512]{1,0:T(8,128)(2,1)}, bf16[640,512]{1,0:T(8,128)(2,1)S(1)}, u32[]{:S(2)}, u32[]{:S(2)}) collective-permute-start(bf16[640,512]{1,0:T(8,128)(2,1)} %collective-permute-done.5.refs_5_), channel_id=1, source_target_pairs={{0,16},{12,28},{16,0},{28,12},{1,17},{13,29},{17,1},{29,13},{2,18}... | collective-permute-start | bytes 1966088 | tf_op jit(solution)/shard_map/ppermute | solution.py:395
  109.1 9.9 %collective-permute-start.19 = (f32[2,32,128]{2,1,0:T(8,128)}, f32[2,32,128]{2,1,0:T(8,128)S(1)}, u32[]{:S(2)}, u32[]{:S(2)}) collective-permute-start(f32[2,32,128]{2,1,0:T(8,128)} %get-tuple-element.29), channel_id=1, source_target_pairs={{0,8},{4,12},{1,9},{5,13},{2,10},{6,14},{3,11},{7,15},{16,24},{20,... | collective-permute-start | bytes 98312 | tf_op jit(solution)/shard_map/ppermute | solution.py:535
  118.9 2.2 %copy-start.13 = (f32[2,32,128]{2,1,0:T(8,128)}, f32[2,32,128]{2,1,0:T(8,128)S(1)}, u32[]{:S(2)}) copy-start(f32[2,32,128]{2,1,0:T(8,128)S(1)} %collective-permute-done.19.refs_15_) | copy-start | bytes 98308
  (4 other events, 4.5 us)

commit v2 on v1

--- a/solution.py
+++ b/solution.py
@@ -3,6 +3,7 @@
 
 import jax
 import jax.numpy as jnp
+import numpy as np
 from jax import lax
 from jax.experimental import pallas as pl
 from jax.experimental.pallas import tpu as pltpu
@@ -11,7 +12,7 @@
 EPSILON = 1e-06
 ROPE_BASE = 1000000.0
 KEEP_PAGES = 3
-VMEM_BYTES = 56 * 2**20
+VMEM_BYTES = 16 * 2**20
 F32 = jnp.float32
 BF16 = jnp.bfloat16
 
@@ -19,7 +20,7 @@
 SCALAR = pl.BlockSpec(memory_space=pltpu.SMEM)
 
 
-def call(kernel, outs, ins, scalars, scratch=(), flops=0, **grid):
+def call(kernel, outs, ins, scalars, scratch=(), flops=0):
     bytes_accessed = sum(math.prod(a.shape) * a.dtype.itemsize for a in list(ins) + list(outs))
     return pl.pallas_call(
         kernel,
@@ -29,7 +30,7 @@
         scratch_shapes=list(scratch),
         compiler_params=pltpu.CompilerParams(vmem_limit_bytes=VMEM_BYTES),
         cost_estimate=pl.CostEstimate(flops=flops, bytes_accessed=bytes_accessed, transcendentals=0),
-    )(*scalars, *ins)
+    )(*scalars, *[pltpu.with_memory_space_constraint(a, pltpu.VMEM) for a in ins])
 
 
 def shaped(shape, dtype):
@@ -57,12 +58,17 @@
     return values * cosine + pltpu.roll(values, values.shape[-1] // 2, values.ndim - 1) * sine
 
 
-def rope_tables(positions, head_size):
-    half_size = head_size // 2
-    freqs = jnp.exp(jnp.arange(half_size, dtype=F32) * (-2.0 * math.log(ROPE_BASE) / head_size))
-    angles = positions.astype(F32)[:, None] * freqs[None, :]
-    cosine, sine = jnp.cos(angles), jnp.sin(angles)
-    return jnp.concatenate([cosine, cosine], axis=1), jnp.concatenate([-sine, sine], axis=1)
+def rope_freqs(head_size):
+    half = np.arange(head_size // 2, dtype=np.float32)
+    freqs = np.exp(half * np.float32(-2.0 * math.log(ROPE_BASE) / head_size)).astype(np.float32)
+    return np.concatenate([freqs, freqs])[None]
+
+
+def rope_tables(count, head_size):
+    angles = np.arange(count, dtype=np.float32)[:, None] * rope_freqs(head_size)
+    signs = np.where(np.arange(head_size) < head_size // 2, -1.0, 1.0)
+    cosine, sine = np.cos(angles.astype(np.float64)), np.sin(angles.astype(np.float64)) * signs
+    return jnp.asarray(cosine, F32), jnp.asarray(sine, F32)
 
 
 def normalize(states, gain):
@@ -72,81 +78,62 @@
 
 def norm_spread_kernel(x_ref, gain_ref, *outs):
     replica = lax.axis_index("rep")
+    slots, steps, _ = x_ref.shape
     width = outs[0].shape[1]
-    values = x_ref[...].astype(F32)
-    scale = head_scale(values)
-    for k, out in enumerate(outs):
-        at = pl.multiple_of((replica ^ k) * width, 128)
-        part = x_ref[:, pl.ds(at, width)].astype(F32)
-        out[...] = (part * scale * gain_ref[:, pl.ds(at, width)]).astype(BF16)
-
-
-def project_kernel(count, slots, steps, listed_ref, *refs):
+    for slot in range(slots):
+        values = x_ref[slot].astype(F32)
+        scale = head_scale(values)
+        for k, out in enumerate(outs):
+            at = pl.multiple_of((replica ^ k) * width, 128)
+            part = x_ref[slot, :, pl.ds(at, width)].astype(F32)
+            out[slot * steps : (slot + 1) * steps, :] = (
+                part * scale * gain_ref[:, pl.ds(at, width)]
+            ).astype(BF16)
+
+
+def project_kernel(count, steps, listed_ref, *refs):
     rows = refs[:count]
-    wq_ref, wk_ref, wv_ref = refs[count : count + 3]
-    outs = refs[count + 3 : 2 * count + 3]
-    stacked = refs[2 * count + 3]
+    wq_ref, wk_ref, wv_ref, own_ref = refs[count : count + 4]
+    sent_refs, stacked = refs[count + 4 : -1], refs[-1]
     replica = lax.axis_index("rep")
     half = count // 2
-    step = pl.program_id(0)
-    per = slots * steps
-
-    @pl.when(step == 0)
-    def _():
-        for k in range(count):
-            own = rows[k][...].astype(F32)
-            other = rows[k ^ half][...].astype(F32)
-            busy = (replica ^ k) < half
-            mine = listed_ref[replica ^ k]
-            theirs = listed_ref[replica ^ k ^ half]
-            ids = lax.broadcasted_iota(jnp.int32, (per, 1), 0)
-            for t in range(steps):
-                moved = jnp.sum(jnp.where(ids == theirs * steps + t, other, 0.0), axis=0, keepdims=True)
-                own = jnp.where((ids == mine * steps + t) & busy, moved, own)
-            stacked[k, :per, :] = own.astype(BF16)
-
+    per = rows[0].shape[0]
+    pad = stacked.shape[1]
+    ids = lax.broadcasted_iota(jnp.int32, (per, 1), 0)
+    for k in range(count):
+        own = rows[k][...].astype(F32)
+        other = rows[k ^ half][...].astype(F32)
+        busy = (replica ^ k) < half
+        for t in range(steps):
+            from_row = ids == listed_ref[replica ^ k ^ half] * steps + t
+            moved = jnp.sum(jnp.where(from_row, other, 0.0), axis=0, keepdims=True)
+            own = jnp.where((ids == listed_ref[replica ^ k] * steps + t) & busy, moved, own)
+        stacked[k, :per, :] = own.astype(BF16)
     lhs = stacked[...].reshape(-1, stacked.shape[2])
-    pad = stacked.shape[1]
-    last = pl.num_programs(0) - 1
-
-    @pl.when(step < last)
-    def _():
-        product = dot(lhs, wq_ref[...])
-        for k in range(count):
-            outs[k][...] = product[k * pad : k * pad + per].astype(outs[k].dtype)
-
-    @pl.when(step == last)
-    def _():
-        product = jnp.concatenate([dot(lhs, wk_ref[...]), dot(lhs, wv_ref[...])], axis=1)
-        for k in range(count):
-            outs[k][...] = product[k * pad : k * pad + per].astype(outs[k].dtype)
-
-
-def project_new(rows, listed, w_query, w_key, w_value, slots, steps):
+    width = wk_ref.shape[1]
+    at = 0
+    for w_ref, pieces in ((wq_ref, wq_ref.shape[1] // width), (wk_ref, 1), (wv_ref, 1)):
+        for piece in range(pieces):
+            product = dot(lhs, w_ref[:, piece * width : (piece + 1) * width])
+            own_ref[:, at : at + width] = product[:per]
+            for k in range(1, count):
+                sent_refs[k - 1][:, at : at + width] = product[k * pad : k * pad + per].astype(BF16)
+            at += width
+
+
+def project_new(rows, listed, w_query, w_key, w_value, steps):
     count = len(rows)
     per, depth = rows[0].shape
-    block = 2 * w_key.shape[1]
-    blocks = w_query.shape[1] // block
     pad = -(-per // 16) * 16
-    total = w_query.shape[1] + block
-    return pl.pallas_call(
-        functools.partial(project_kernel, count, slots, steps),
-        grid=(blocks + 1,),
-        out_shape=tuple(shaped((per, total), F32) for _ in rows),
-        in_specs=[SCALAR]
-        + [pl.BlockSpec((per, depth), lambda j: (0, 0)) for _ in rows]
-        + [
-            pl.BlockSpec((depth, block), lambda j: (0, jnp.minimum(j, blocks - 1))),
-            pl.BlockSpec(w_key.shape, lambda j: (0, 0)),
-            pl.BlockSpec(w_value.shape, lambda j: (0, 0)),
-        ],
-        out_specs=tuple(pl.BlockSpec((per, block), lambda j: (0, j)) for _ in rows),
-        scratch_shapes=[pltpu.VMEM((count, pad, depth), BF16)],
-        compiler_params=pltpu.CompilerParams(vmem_limit_bytes=VMEM_BYTES),
-        cost_estimate=pl.CostEstimate(
-            flops=2 * count * per * depth * total, bytes_accessed=2 * depth * total, transcendentals=0
-        ),
-    )(listed, *rows, w_query, w_key, w_value)
+    total = w_query.shape[1] + 2 * w_key.shape[1]
+    return call(
+        functools.partial(project_kernel, count, steps),
+        [pltpu.VMEM((per, total), F32)] + [pltpu.VMEM((per, total), BF16)] * (count - 1),
+        [*rows, w_query, w_key, w_value],
+        [listed],
+        scratch=[pltpu.VMEM((count, pad, depth), BF16)],
+        flops=2 * count * per * depth * total,
+    )
 
 
 def spread_heads(rows, kv_heads):
@@ -165,11 +152,10 @@
     return total
 
 
-def attend_kernel(parts, seq_count, steps, table_ref, lengths_ref, listed_ref, *refs):
+def attend_kernel(parts, seq_count, steps, tokens, table_ref, lengths_ref, listed_ref, *refs):
     sums = refs[:parts]
-    (cos_ref, sin_ref, qgain_ref, kgain_ref, keys_ref, values_ref) = refs[parts : parts + 6]
-    num_ref, den_ref, moved_ref, last_ref = refs[parts + 6 : parts + 10]
-    q3, k3, v3 = refs[parts + 10 :]
+    freqs_ref, qgain_ref, kgain_ref, keys_ref, values_ref = refs[parts : parts + 5]
+    num_ref, den_ref, moved_ref, last_ref, q3, k3, v3 = refs[parts + 5 :]
     replica = lax.axis_index("rep")
     half = lax.axis_size("rep") // 2
     size = qgain_ref.shape[1]
@@ -178,6 +164,7 @@
     kv_heads = width // size
     heads = kv_heads * 8
     slots = seq_count + 1
+    per = slots * steps
 
     def total(at):
         value = sums[0][:, at : at + size].astype(F32)
@@ -185,7 +172,20 @@
             value = value + other[:, at : at + size].astype(F32)
         return value
 
-    cosine, sine = cos_ref[...], sin_ref[...]
+    partner = jnp.where(replica < half, replica, replica - half)
+    arrived = lengths_ref[partner, listed_ref[partner]]
+    ids = lax.broadcasted_iota(jnp.int32, (per, 1), 0)
+    positions = ids % steps
+    for slot in range(slots):
+        base = tokens
+        if slot < seq_count:
+            base = jnp.where(listed_ref[replica] == slot, arrived, lengths_ref[replica, slot])
+        positions = positions + jnp.where(ids // steps == slot, base, 0)
+    angles = positions.astype(F32) * freqs_ref[...]
+    lanes = lax.broadcasted_iota(jnp.int32, (per, size), 1)
+    cosine, sine = jnp.cos(angles), jnp.sin(angles)
+    sine = jnp.where(lanes < size // 2, -sine, sine)
+
     for h in range(heads):
         x = total(h * size)
         x = rotate_rows(x * head_scale(x) * qgain_ref[...], cosine, sine) * size**-0.5
@@ -382,7 +382,10 @@
         / (den_ref[mine] + moved_ref[1].reshape(steps, heads, size))
     )
     for h in range(heads):
-        out_ref[:, h * size : (h + 1) * size] = o3[:, h, :].astype(BF16)
+        for slot in range(slots):
+            out_ref[slot, :, h * size : (h + 1) * size] = o3[
+                slot * steps : (slot + 1) * steps, h, :
+            ].astype(BF16)
 
 
 def line_pairs(pairs, axis="rep"):
@@ -413,7 +416,6 @@
     replicas = lax.axis_size("rep")
     half = replicas // 2
     replica = lax.axis_index("rep")
-    partner = (replica + half) % replicas
     head_size = query_gain.shape[0]
     width = w_key.shape[1]
     depth = w_key.shape[0]
@@ -438,20 +440,30 @@
         own = jnp.concatenate(
             [lax.dynamic_slice_in_dim(w, group * rows, rows, 0) for w in (w_key, w_value)], axis=1
         )
+
+    if near:
+        spread = call(
+            norm_spread_kernel, [pltpu.VMEM((per, depth), BF16)] * replicas, [dec_hidden[0], gain], []
+        )
+        rec_hidden, *spread = lax.optimization_barrier((rec_hidden, *spread))
+        (blocks,) = call(
+            norm_blocks_kernel,
+            [pltpu.VMEM((2 * replicas, rec_hidden.shape[1], rows), BF16)],
+            [rec_hidden[0], gain],
+            [],
+        )
+        spread = [spread[0]] + [xor_permute(spread[k], "rep", k) for k in range(1, replicas)]
+        own, *spread = lax.optimization_barrier((own, *spread))
         from_a = line_pairs([(0, 1), (1, 0), (2, 3), (3, 2)])(own)
         from_b = line_pairs([(1, 2), (2, 1)])(own)
-
-    hidden = dec_hidden[0].reshape(per, features)
-    if near:
-        spread = call(
-            norm_spread_kernel, [shaped((per, depth), BF16)] * replicas, [hidden, gain], []
-        )
-        spread = [spread[0]] + [xor_permute(spread[k], "rep", k) for k in range(1, replicas)]
-        sums = project_new(spread, listed_slot, w_query, w_key, w_value, slots, steps)
-        sums = [sums[0]] + [xor_permute(sums[k], "rep", k) for k in range(1, replicas)]
+        own_sums, *sent = project_new(spread, listed_slot, w_query, w_key, w_value, steps)
+        sums = [xor_permute(sent[k - 1], "rep", k) for k in range(1, replicas)]
+        from_a, from_b, _ = lax.optimization_barrier((from_a, from_b, sent[0]))
+        late_a, blocks, *sums = lax.optimization_barrier((from_a, blocks, *sums))
+        sums = [own_sums, *sums]
     else:
         spread = lax.all_to_all(
-            normalize(hidden, norm_gain), "rep", split_axis=1, concat_axis=0, tiled=True
+            normalize(dec_hidden[0].reshape(per, features), norm_gain), "rep", split_axis=1, concat_axis=0, tiled=True
         ).reshape(replicas, slots, steps, depth)
         moved = jnp.take_along_axis(spread, listed_slot[:, None, None, None], axis=1)
         moved = jnp.roll(moved, half, axis=0)
@@ -468,32 +480,12 @@
             )
         ]
 
-    rec_cos, rec_sin = rope_tables(jnp.arange(tokens, dtype=jnp.int32), head_size)
+    rec_cos, rec_sin = rope_tables(tokens, head_size)
     if near:
-        (blocks,) = call(
-            norm_blocks_kernel,
-            [shaped((2 * replicas, rec_hidden.shape[1], rows), BF16)],
-            [rec_hidden[0], gain],
-            [],
-        )
         across = xor_permute(blocks, "tp", 1)
-        xs = [blocks, across, xor_permute(blocks, "sub", 1), xor_permute(across, "sub", 1)]
         from_d = line_pairs([(1, 2), (2, 1)])(from_a)
         from_c = line_pairs([(1, 0), (2, 3)])(from_b)
-        over_a = across_groups(from_a, range(4))
-        over_b = across_groups(from_b, (1, 2))
-        from_e = line_pairs([(1, 0), (2, 3)])(from_d)
-        over_c = across_groups(from_c, (0, 3))
-        over_d = across_groups(from_d, (1, 2))
-        over_e = across_groups(from_e, (0, 3))
-        (acc,) = call(
-            first_kernel,
-            [shaped((tokens, 2 * width), F32)],
-            [*xs, w_key, w_value, from_a, over_a, from_b, from_c, over_b, over_c],
-            [],
-            flops=3 * depth * tokens * width * 4,
-        )
-        far = [*xs, from_d, from_e, over_d, over_e]
+        over_a = across_groups(late_a, range(4))
     else:
         normed = lax.all_gather(
             normalize(rec_hidden[0], norm_gain), ("tp", "sub"), axis=0, tiled=True
@@ -509,29 +501,43 @@
             ],
             axis=1,
         )
-        far = []
-
-    lengths = seq_lengths[replica]
-    arriving = (jnp.arange(seq_count) == listed_slot[replica]) & (replica >= half)
-    moved_length = seq_lengths[partner, listed_slot[partner]]
-    base = jnp.concatenate(
-        [jnp.where(arriving, moved_length, lengths), jnp.full((1,), tokens, jnp.int32)]
-    )
-    positions = (base[:, None] + jnp.arange(steps, dtype=jnp.int32)[None, :]).reshape(-1)
-    cosine, sine = rope_tables(positions, head_size)
+
     flat = (per, heads, head_size)
     num, den, moved, rows_last = call(
-        functools.partial(attend_kernel, len(sums), seq_count, steps),
+        functools.partial(attend_kernel, len(sums), seq_count, steps, tokens),
         [
-            shaped(flat, F32),
-            shaped(flat, F32),
-            shaped((2, steps * heads, head_size), F32),
-            shaped((steps * heads, width), BF16),
+            pltpu.VMEM(flat, F32),
+            pltpu.VMEM(flat, F32),
+            pltpu.VMEM((2, steps * heads, head_size), F32),
+            pltpu.VMEM((steps * heads, width), BF16),
         ],
-        [*sums, cosine, sine, qgain, kgain, pool_keys[0], pool_values[0]],
+        [*sums, jnp.asarray(rope_freqs(head_size)), qgain, kgain, pool_keys[0], pool_values[0]],
         [table, seq_lengths, listed_slot],
         scratch=[pltpu.VMEM(flat, F32)] * 3,
     )
+    far = []
+    if near:
+        from_b, from_c, from_d, num, den, moved, rows_last = lax.optimization_barrier(
+            (from_b, from_c, from_d, num, den, moved, rows_last)
+        )
+        from_e = line_pairs([(1, 0), (2, 3)])(from_d)
+        over_b = across_groups(from_b, (1, 2))
+        over_c = across_groups(from_c, (0, 3))
+        beside = xor_permute(blocks, "sub", 1)
+        across, beside, from_d, from_e, over_a, over_b, over_c, moved = lax.optimization_barrier(
+            (across, beside, from_d, from_e, over_a, over_b, over_c, moved)
+        )
+        over_d = across_groups(from_d, (1, 2))
+        over_e = across_groups(from_e, (0, 3))
+        xs = [blocks, across, beside, xor_permute(across, "sub", 1)]
+        (acc,) = call(
+            first_kernel,
+            [pltpu.VMEM((tokens, 2 * width), F32)],
+            [*xs, w_key, w_value, from_a, over_a, from_b, from_c, over_b, over_c],
+            [],
+            flops=3 * depth * tokens * width * 4,
+        )
+        far = [*xs, from_d, from_e, over_d, over_e]
     moved = lax.ppermute(moved, "rep", [(i, i + half) for i in range(half)])
 
     rec_k, rec_v, decoded = call(
@@ -539,14 +545,14 @@
         [
             shaped((tokens, width), BF16),
             shaped((tokens, width), BF16),
-            shaped((per, heads * head_size), BF16),
+            shaped((slots, steps, heads * head_size), BF16),
         ],
         [*far, acc, rec_cos, rec_sin, kgain, rows_last, num, den, moved],
         [listed_slot],
         scratch=[pltpu.VMEM(flat, F32)] + [pltpu.VMEM((tokens, 2 * width), F32)] * bool(far),
         flops=depth * tokens * width * 4,
     )
-    return (rec_k[None], rec_v[None], decoded.reshape(1, slots, steps, heads * head_size))
+    return (rec_k[None], rec_v[None], decoded[None])
 
 
 def solution(mesh):

time: 130 us -> 96 us (0.74)
  Pallas kernels: 33.4 us -> 13.8 us
  waiting for transfers between devices: 51.1 us -> 46 us
  other arithmetic: 4.35 us -> 0.05 us
  starting transfers between devices: 31.8 us -> 29.3 us
  between operations: 2.93 us -> 0.99 us
    ppermute x9, waiting for transfers between devices: 35.7 us -> 13.7 us  [xor_permute(): return lax.ppermute(value, axis, [(i, i ^ distance) for i in range(count)])]
    ppermute x5, waiting for transfers between devices: 1.57 us -> 20.1 us  [line_pairs(): return lambda value: lax.ppermute(value, axis, pairs)]
    pallas_call x5 -> x6, Pallas kernels: 27.3 us -> 13.8 us  [call(): pl.pallas_call(kernel, out_shape=tuple(outs), in_specs=[SCALAR] * len(sca...]
    pallas_call x1 -> x0, Pallas kernels: 6.07 us -> none  [project_new(): pl.pallas_call(functools.partial(project_kernel, count, slots, steps), gr...]
    ppermute x5, starting transfers between devices: 9.2 us -> 4.1 us  [line_pairs(): return lambda value: lax.ppermute(value, axis, pairs)]
    unnamed x32 -> x34, local copies, waits for them, and re-layouts: 2.39 us -> 4.2 us
    concatenate x3 -> x0, other arithmetic: 1.76 us -> none  [the longest x2 1.69 us: rope_tables(): jnp.concatenate([cosine, cosine], axis=1)]
    ppermute x5, waiting for transfers between devices: 13.8 us -> 12.2 us  [across_groups(): return lax.ppermute(value, ('groups', 'rep'), pairs)]
  transfers between devices with their start and end apart: 20 -> 20, of which waited for: 7 -> 9; matrix products, arithmetic and copies ran while one was open for 5% -> 1% of each run, Pallas kernels for 18% -> 11%
where the time goes in v2:
time: 96 us; the launch traced here: 95.6 us
  waiting for transfers between devices  46 us (48%)
  starting transfers between devices  29.3 us (31%)
  Pallas kernels  13.8 us (14%)
  local copies, waits for them, and re-layouts  5.42 us (6%)
  between operations  0.99 us (1%)
    ppermute x5, waiting for transfers between devices, line_pairs(): return lambda value: lax.ppermute(value, axis, pairs)  20.1 us
    pallas_call x6, Pallas kernels, call(): pl.pallas_call(kernel, out_shape=tuple(outs), in_specs=[SCALAR] * len(sca...  13.8 us
    ppermute x9, waiting for transfers between devices, xor_permute(): return lax.ppermute(value, axis, [(i, i ^ distance) for i in range(count)])  13.7 us
    ppermute x9, starting transfers between devices, xor_permute(): return lax.ppermute(value, axis, [(i, i ^ distance) for i in range(count)])  13.5 us
    ppermute x5, waiting for transfers between devices, across_groups(): return lax.ppermute(value, ('groups', 'rep'), pairs)  12.2 us
    ppermute x5, starting transfers between devices, across_groups(): return lax.ppermute(value, ('groups', 'rep'), pairs)  8.74 us
    unnamed x34, local copies, waits for them, and re-layouts  4.2 us
    ppermute x5, starting transfers between devices, line_pairs(): return lambda value: lax.ppermute(value, axis, pairs)  4.1 us
  transfers between devices with their start and end apart: 20, of which 9 were waited for; matrix products, arithmetic and copies ran while one was open for 1% of the time, Pallas kernels for 11%

profile of v2, /device:TPU:0, one launch (start us, length us, event | category | flops | bytes accessed | tf_op | source)
XLA Modules:
  0.0 95.6 jit_solution(3472938463351318957)
XLA Ops:
  0.6 0.9 copy-done.8
  1.6 0.7 copy-done.9
  2.7 3.1 %collective-permute-start = (bf16[18,1280]{1,0:T(8,128)(2,1)S(1)}, bf16[18,1280]{1,0:T(8,128)(2,1)S(1)}, u32[]{:S(2)}, u32[]{:S(2)}) collective-permute-start(bf16[18,1280]{1,0:T(8,128)(2,1)S(1)} %get-tuple-element.55), channel_id=1, source_target_pairs={{0,4},{4,0},{8,12},{12,8},{1,5},{5,1},{9,13},{13,9},{2,6},{6,2},{1... | collective-permute-start | bytes 138248 | tf_op jit(solution)/shard_map/ppermute | solution.py:50
  5.8 2.6 %collective-permute-start.1 = (bf16[18,1280]{1,0:T(8,128)(2,1)S(1)}, bf16[18,1280]{1,0:T(8,128)(2,1)S(1)}, u32[]{:S(2)}, u32[]{:S(2)}) collective-permute-start(bf16[18,1280]{1,0:T(8,128)(2,1)S(1)} %get-tuple-element.56), channel_id=1, source_target_pairs={{0,8},{4,12},{8,0},{12,4},{1,9},{5,13},{9,1},{13,5},{2,10},{6,14},... | collective-permute-start | bytes 138248 | tf_op jit(solution)/shard_map/ppermute | solution.py:50
  8.4 1.2 %constant_dynamic-slice_fusion = (bf16[640,256]{1,0:T(8,128)(2,1)S(1)}, bf16[640,256]{1,0:T(8,128)(2,1)S(1)}) fusion(bf16[1280,256]{1,0:T(8,128)(2,1)} %refs_5_.3, s32[]{:T(128)S(6)} %select_n.4, bf16[1280,256]{1,0:T(8,128)(2,1)} %refs_4_.4), kind=kLoop, calls=%fused_computation.1 | loop fusion | bytes 1310724 | tf_op jit(solution)/shard_map/dynamic_slice | solution.py:441
  9.7 2.4 %collective-permute-done.1.refs_2_ = bf16[18,1280]{1,0:T(8,128)(2,1)S(1)} collective-permute-done((bf16[18,1280]{1,0:T(8,128)(2,1)S(1)}, bf16[18,1280]{1,0:T(8,128)(2,1)S(1)}, u32[]{:S(2)}, u32[]{:S(2)}) %collective-permute-start.1) | collective-permute-done | bytes 46112 | tf_op jit(solution)/shard_map/ppermute | solution.py:50
  12.1 2.3 %collective-permute-done.2.refs_3_ = bf16[18,1280]{1,0:T(8,128)(2,1)S(1)} collective-permute-done((bf16[18,1280]{1,0:T(8,128)(2,1)S(1)}, bf16[18,1280]{1,0:T(8,128)(2,1)S(1)}, u32[]{:S(2)}, u32[]{:S(2)}) %collective-permute-start.2) | collective-permute-done | bytes 46112 | tf_op jit(solution)/shard_map/ppermute | solution.py:50
  14.4 0.7 collective-permute-start.4
  15.1 2.5 %copy-done = bf16[1280,2048]{1,0:T(8,128)(2,1)S(1)} copy-done((bf16[1280,2048]{1,0:T(8,128)(2,1)S(1)}, bf16[1280,2048]{1,0:T(8,128)(2,1)}, u32[]{:S(2)}) %copy-start) | copy-done | bytes 5242904
  17.6 1.7 %shard_map.176 = (f32[18,2560]{1,0:T(8,128)S(1)}, bf16[18,2560]{1,0:T(8,128)(2,1)S(1)}, bf16[18,2560]{1,0:T(8,128)(2,1)S(1)}, bf16[18,2560]{1,0:T(8,128)(2,1)S(1)}) custom-call(s32[4]{0:T(128)S(1)} %copy-done.11, bf16[18,1280]{1,0:T(8,128)(2,1)S(1)} %get-tuple-element.59.refs_0_, bf16[18,1280]{1,0:T(8,128)(2,1)S(1)} %collective-permute-done.refs_1_, ...), custom_call_target="tpu_custom_call" | custom-call | flops 471859200 | bytes 7198720 | tf_op jit(solution)/shard_map/pallas_call | solution.py:25
  19.3 3.9 %collective-permute-start.5 = (bf16[18,2560]{1,0:T(8,128)(2,1)S(1)}, bf16[18,2560]{1,0:T(8,128)(2,1)S(1)}, u32[]{:S(2)}, u32[]{:S(2)}) collective-permute-start(bf16[18,2560]{1,0:T(8,128)(2,1)S(1)} %get-tuple-element.63), channel_id=1, source_target_pairs={{0,4},{4,0},{8,12},{12,8},{1,5},{5,1},{9,13},{13,9},{2,6},{6,2},{1... | collective-permute-start | bytes 276488 | tf_op jit(solution)/shard_map/ppermute | solution.py:50
  23.2 0.9 collective-permute-start.6
  24.1 1.5 %collective-permute-start.7 = (bf16[18,2560]{1,0:T(8,128)(2,1)S(1)}, bf16[18,2560]{1,0:T(8,128)(2,1)S(1)}, u32[]{:S(2)}, u32[]{:S(2)}) collective-permute-start(bf16[18,2560]{1,0:T(8,128)(2,1)S(1)} %get-tuple-element.67), channel_id=1, source_target_pairs={{0,12},{4,8},{8,4},{12,0},{1,13},{5,9},{9,5},{13,1},{2,14},{6,10},... | collective-permute-start | bytes 276488 | tf_op jit(solution)/shard_map/ppermute | solution.py:50
  25.7 5.8 %collective-permute-done.3.refs_6_ = bf16[640,512]{1,0:T(8,128)(2,1)S(1)} collective-permute-done((bf16[640,512]{1,0:T(8,128)(2,1)S(1)}, bf16[640,512]{1,0:T(8,128)(2,1)S(1)}, u32[]{:S(2)}, u32[]{:S(2)}) %collective-permute-start.3) | collective-permute-done | bytes 655392 | tf_op jit(solution)/shard_map/ppermute | solution.py:392
  31.5 1.3 %collective-permute-start.10 = (bf16[640,512]{1,0:T(8,128)(2,1)S(1)}, bf16[640,512]{1,0:T(8,128)(2,1)S(1)}, u32[]{:S(2)}, u32[]{:S(2)}) collective-permute-start(bf16[640,512]{1,0:T(8,128)(2,1)S(1)} %collective-permute-done.4.refs_8_), channel_id=1, source_target_pairs={{4,0},{8,12},{5,1},{9,13},{6,2},{10,14},{7,3},{11,15},{20,16},{24,... | collective-permute-start | bytes 1966088 | tf_op jit(solution)/shard_map/ppermute | solution.py:392
  32.8 0.7 collective-permute-start.11
  33.6 0.7 shard_map.177.refs_0_
  34.8 8.5 %collective-permute-done.6.refs_2_ = bf16[18,2560]{1,0:T(8,128)(2,1)S(1)} collective-permute-done((bf16[18,2560]{1,0:T(8,128)(2,1)S(1)}, bf16[18,2560]{1,0:T(8,128)(2,1)S(1)}, u32[]{:S(2)}, u32[]{:S(2)}) %collective-permute-start.6) | collective-permute-done | bytes 92192 | tf_op jit(solution)/shard_map/ppermute | solution.py:50
  43.3 1.5 %collective-permute-start.13 = (bf16[640,512]{1,0:T(8,128)(2,1)S(1)}, bf16[640,512]{1,0:T(8,128)(2,1)S(1)}, u32[]{:S(2)}, u32[]{:S(2)}) collective-permute-start(bf16[640,512]{1,0:T(8,128)(2,1)S(1)} %collective-permute-done.3.refs_6_), channel_id=1, source_target_pairs={{0,16},{4,20},{8,24},{12,28},{16,0},{20,4},{24,8},{28,12},{1,17},{... | collective-permute-start | bytes 1966088 | tf_op jit(solution)/shard_map/ppermute | solution.py:398
  44.8 1.5 %collective-permute-start.8 = (bf16[8,128,640]{2,1,0:T(8,128)(2,1)S(1)}, bf16[8,128,640]{2,1,0:T(8,128)(2,1)S(1)}, u32[]{:S(2)}, u32[]{:S(2)}) collective-permute-start(bf16[8,128,640]{2,1,0:T(8,128)(2,1)S(1)} %shard_map.177.refs_0_), channel_id=1, source_target_pairs={{0,2},{2,0},{1,3},{3,1},{4,6},{6,4},{5,7},{7,5},{8,10},{10,8},{9,1... | collective-permute-start | bytes 3932168 | tf_op jit(solution)/shard_map/ppermute | solution.py:50
  46.4 5.2 %shard_map.178 = (f32[18,16,128]{2,1,0:T(8,128)S(1)}, f32[18,16,128]{2,1,0:T(8,128)S(1)}, f32[2,32,128]{2,1,0:T(8,128)S(1)}, bf16[32,256]{1,0:T(8,128)(2,1)S(1)}) custom-call(s32[8,16]{1,0:T(8,128)S(1)} %bitcast.17, s32[4,8]{1,0:T(4,128)S(1)} %copy-done.13, s32[4]{0:T(128)S(1)} %copy-done.11, f32[18,2560]{1,0:T(8,128)S(1)} %get-tuple-element.70.refs_0_, ...), custom_call_target="tpu_custom_call" | custom-call | bytes 6049280 | tf_op jit(solution)/shard_map/pallas_call | solution.py:25
  51.6 1.4 %collective-permute-start.12 = (bf16[640,512]{1,0:T(8,128)(2,1)S(1)}, bf16[640,512]{1,0:T(8,128)(2,1)S(1)}, u32[]{:S(2)}, u32[]{:S(2)}) collective-permute-start(bf16[640,512]{1,0:T(8,128)(2,1)S(1)} %collective-permute-done.11.refs_4_), channel_id=1, source_target_pairs={{4,0},{8,12},{5,1},{9,13},{6,2},{10,14},{7,3},{11,15},{20,16},{24,... | collective-permute-start | bytes 1966088 | tf_op jit(solution)/shard_map/ppermute | solution.py:392
  53.1 0.7 collective-permute-start.14
  53.9 3.4 %collective-permute-start.15 = (bf16[640,512]{1,0:T(8,128)(2,1)S(1)}, bf16[640,512]{1,0:T(8,128)(2,1)S(1)}, u32[]{:S(2)}, u32[]{:S(2)}) collective-permute-start(bf16[640,512]{1,0:T(8,128)(2,1)S(1)} %collective-permute-done.10.refs_9_), channel_id=1, source_target_pairs={{0,16},{12,28},{16,0},{28,12},{1,17},{13,29},{17,1},{29,13},{2,18}... | collective-permute-start | bytes 1966088 | tf_op jit(solution)/shard_map/ppermute | solution.py:398
  57.3 14.3 %collective-permute-done.12.refs_5_ = bf16[640,512]{1,0:T(8,128)(2,1)S(1)} collective-permute-done((bf16[640,512]{1,0:T(8,128)(2,1)S(1)}, bf16[640,512]{1,0:T(8,128)(2,1)S(1)}, u32[]{:S(2)}, u32[]{:S(2)}) %collective-permute-start.12) | collective-permute-done | bytes 655392 | tf_op jit(solution)/shard_map/ppermute | solution.py:392
  71.6 1.2 %collective-permute-done.15.refs_11_ = bf16[640,512]{1,0:T(8,128)(2,1)S(1)} collective-permute-done((bf16[640,512]{1,0:T(8,128)(2,1)S(1)}, bf16[640,512]{1,0:T(8,128)(2,1)S(1)}, u32[]{:S(2)}, u32[]{:S(2)}) %collective-permute-start.15) | collective-permute-done | bytes 655392 | tf_op jit(solution)/shard_map/ppermute | solution.py:398
  72.8 0.7 collective-permute-start.17
  73.5 2.4 %collective-permute-start.18 = (bf16[640,512]{1,0:T(8,128)(2,1)S(1)}, bf16[640,512]{1,0:T(8,128)(2,1)S(1)}, u32[]{:S(2)}, u32[]{:S(2)}) collective-permute-start(bf16[640,512]{1,0:T(8,128)(2,1)S(1)} %collective-permute-done.12.refs_5_), channel_id=1, source_target_pairs={{0,16},{12,28},{16,0},{28,12},{1,17},{13,29},{17,1},{29,13},{2,18}... | collective-permute-start | bytes 1966088 | tf_op jit(solution)/shard_map/ppermute | solution.py:398
  76.0 2.9 %collective-permute-start.19 = (f32[2,32,128]{2,1,0:T(8,128)S(1)}, f32[2,32,128]{2,1,0:T(8,128)S(1)}, u32[]{:S(2)}, u32[]{:S(2)}) collective-permute-start(f32[2,32,128]{2,1,0:T(8,128)S(1)} %get-tuple-element.93), channel_id=1, source_target_pairs={{0,8},{4,12},{1,9},{5,13},{2,10},{6,14},{3,11},{7,15},{16,24},{20,... | collective-permute-start | bytes 98312 | tf_op jit(solution)/shard_map/ppermute | solution.py:541
  78.9 2.8 %shard_map.179.refs_8_ = f32[512,512]{1,0:T(8,128)S(1)} custom-call(bf16[8,128,640]{2,1,0:T(8,128)(2,1)S(1)} %shard_map.177.refs_0_, bf16[8,128,640]{2,1,0:T(8,128)(2,1)S(1)} %collective-permute-done.8.refs_1_, bf16[8,128,640]{2,1,0:T(8,128)(2,1)S(1)} %collective-permute-done.9.refs_2_, bf16[8,128,640]{2,1,0:T(8,128)(2,1)S(1)} %collective-permute-done.16.refs_3_, ...), custom_call_target="tpu_custom_call" | custom-call | flops 2013265920 | bytes 11534336 | tf_op jit(solution)/shard_map/pallas_call | solution.py:25
  81.7 10.9 %collective-permute-done.18.refs_7_ = bf16[640,512]{1,0:T(8,128)(2,1)S(1)} collective-permute-done((bf16[640,512]{1,0:T(8,128)(2,1)S(1)}, bf16[640,512]{1,0:T(8,128)(2,1)S(1)}, u32[]{:S(2)}, u32[]{:S(2)}) %collective-permute-start.18) | collective-permute-done | bytes 655392 | tf_op jit(solution)/shard_map/ppermute | solution.py:398
  92.6 3.0 %shard_map.180 = (bf16[512,256]{1,0:T(8,128)(2,1)}, bf16[512,256]{1,0:T(8,128)(2,1)}, bf16[9,2,2048]{2,1,0:T(2,128)(2,1)}) custom-call(s32[4]{0:T(128)S(1)} %copy-done.11, bf16[8,128,640]{2,1,0:T(8,128)(2,1)S(1)} %shard_map.177.refs_0_, bf16[8,128,640]{2,1,0:T(8,128)(2,1)S(1)} %collective-permute-done.8.refs_1_, ...), custom_call_target="tpu_custom_call" | custom-call | flops 671088640 | bytes 10379776 | tf_op jit(solution)/shard_map/pallas_call | solution.py:25
  (50 shorter events, 1.2 us)
Async XLA Ops:
  2.7 7.0 %collective-permute-start = (bf16[18,1280]{1,0:T(8,128)(2,1)S(1)}, bf16[18,1280]{1,0:T(8,128)(2,1)S(1)}, u32[]{:S(2)}, u32[]{:S(2)}) collective-permute-start(bf16[18,1280]{1,0:T(8,128)(2,1)S(1)} %get-tuple-element.55), channel_id=1, source_target_pairs={{0,4},{4,0},{8,12},{12,8},{1,5},{5,1},{9,13},{13,9},{2,6},{6,2},{1... | collective-permute-start | bytes 138248 | tf_op jit(solution)/shard_map/ppermute | solution.py:50
  5.8 6.3 %collective-permute-start.1 = (bf16[18,1280]{1,0:T(8,128)(2,1)S(1)}, bf16[18,1280]{1,0:T(8,128)(2,1)S(1)}, u32[]{:S(2)}, u32[]{:S(2)}) collective-permute-start(bf16[18,1280]{1,0:T(8,128)(2,1)S(1)} %get-tuple-element.56), channel_id=1, source_target_pairs={{0,8},{4,12},{8,0},{12,4},{1,9},{5,13},{9,1},{13,5},{2,10},{6,14},... | collective-permute-start | bytes 138248 | tf_op jit(solution)/shard_map/ppermute | solution.py:50
  8.3 6.0 %collective-permute-start.2 = (bf16[18,1280]{1,0:T(8,128)(2,1)S(1)}, bf16[18,1280]{1,0:T(8,128)(2,1)S(1)}, u32[]{:S(2)}, u32[]{:S(2)}) collective-permute-start(bf16[18,1280]{1,0:T(8,128)(2,1)S(1)} %get-tuple-element.57), channel_id=1, source_target_pairs={{0,12},{4,8},{8,4},{12,0},{1,13},{5,9},{9,5},{13,1},{2,14},{6,10},... | collective-permute-start | bytes 138248 | tf_op jit(solution)/shard_map/ppermute | solution.py:50
  8.3 6.7 %copy-start.11 = (s32[4]{0:T(128)S(1)}, s32[4]{0:T(128)}, u32[]{:S(2)}) copy-start(s32[4]{0:T(128)} %listed_ref.5) | copy-start | bytes 52
  9.6 23.9 %copy-start.5 = (bf16[1,128,5120]{2,1,0:T(8,128)(2,1)S(1)}, bf16[1,128,5120]{2,1,0:T(8,128)(2,1)}, u32[]{:S(2)}) copy-start(bf16[1,128,5120]{2,1,0:T(8,128)(2,1)} %param.16) | copy-start | bytes 3932164
  14.4 17.1 %collective-permute-start.3 = (bf16[640,512]{1,0:T(8,128)(2,1)S(1)}, bf16[640,512]{1,0:T(8,128)(2,1)S(1)}, u32[]{:S(2)}, u32[]{:S(2)}) collective-permute-start(bf16[640,512]{1,0:T(8,128)(2,1)S(1)} %pad_maximum_fusion), channel_id=1, source_target_pairs={{0,4},{4,0},{8,12},{12,8},{1,5},{5,1},{9,13},{13,9},{2,6},{6,2},{1... | collective-permute-start | bytes 1966088 | tf_op jit(solution)/shard_map/ppermute | solution.py:392
  14.4 17.1 %collective-permute-start.4 = (bf16[640,512]{1,0:T(8,128)(2,1)S(1)}, bf16[640,512]{1,0:T(8,128)(2,1)S(1)}, u32[]{:S(2)}, u32[]{:S(2)}) collective-permute-start(bf16[640,512]{1,0:T(8,128)(2,1)S(1)} %pad_maximum_fusion), channel_id=1, source_target_pairs={{4,8},{8,4},{5,9},{9,5},{6,10},{10,6},{7,11},{11,7},{20,24},{24,20... | collective-permute-start | bytes 1966088 | tf_op jit(solution)/shard_map/ppermute | solution.py:392
  17.6 15.9 %copy-start.10 = (f32[5120]{0:T(1024)S(1)}, f32[5120]{0:T(1024)}, u32[]{:S(2)}) copy-start(f32[5120]{0:T(1024)} %param.18) | copy-start | bytes 61444
  17.6 28.7 %copy-start.4 = (bf16[1,40,128,256]{3,2,1,0:T(8,128)(2,1)S(1)}, bf16[1,40,128,256]{3,2,1,0:T(8,128)(2,1)}, u32[]{:S(2)}) copy-start(bf16[1,40,128,256]{3,2,1,0:T(8,128)(2,1)} %param.25) | copy-start | bytes 7864324
  19.3 15.5 %collective-permute-start.5 = (bf16[18,2560]{1,0:T(8,128)(2,1)S(1)}, bf16[18,2560]{1,0:T(8,128)(2,1)S(1)}, u32[]{:S(2)}, u32[]{:S(2)}) collective-permute-start(bf16[18,2560]{1,0:T(8,128)(2,1)S(1)} %get-tuple-element.63), channel_id=1, source_target_pairs={{0,4},{4,0},{8,12},{12,8},{1,5},{5,1},{9,13},{13,9},{2,6},{6,2},{1... | collective-permute-start | bytes 276488 | tf_op jit(solution)/shard_map/ppermute | solution.py:50
  23.2 20.1 %collective-permute-start.6 = (bf16[18,2560]{1,0:T(8,128)(2,1)S(1)}, bf16[18,2560]{1,0:T(8,128)(2,1)S(1)}, u32[]{:S(2)}, u32[]{:S(2)}) collective-permute-start(bf16[18,2560]{1,0:T(8,128)(2,1)S(1)} %get-tuple-element.66), channel_id=1, source_target_pairs={{0,8},{4,12},{8,0},{12,4},{1,9},{5,13},{9,1},{13,5},{2,10},{6,14},... | collective-permute-start | bytes 276488 | tf_op jit(solution)/shard_map/ppermute | solution.py:50
  24.1 19.1 %collective-permute-start.7 = (bf16[18,2560]{1,0:T(8,128)(2,1)S(1)}, bf16[18,2560]{1,0:T(8,128)(2,1)S(1)}, u32[]{:S(2)}, u32[]{:S(2)}) collective-permute-start(bf16[18,2560]{1,0:T(8,128)(2,1)S(1)} %get-tuple-element.67), channel_id=1, source_target_pairs={{0,12},{4,8},{8,4},{12,0},{1,13},{5,9},{9,5},{13,1},{2,14},{6,10},... | collective-permute-start | bytes 276488 | tf_op jit(solution)/shard_map/ppermute | solution.py:50
  31.5 20.1 %collective-permute-start.10 = (bf16[640,512]{1,0:T(8,128)(2,1)S(1)}, bf16[640,512]{1,0:T(8,128)(2,1)S(1)}, u32[]{:S(2)}, u32[]{:S(2)}) collective-permute-start(bf16[640,512]{1,0:T(8,128)(2,1)S(1)} %collective-permute-done.4.refs_8_), channel_id=1, source_target_pairs={{4,0},{8,12},{5,1},{9,13},{6,2},{10,14},{7,3},{11,15},{20,16},{24,... | collective-permute-start | bytes 1966088 | tf_op jit(solution)/shard_map/ppermute | solution.py:392
  32.8 18.8 %collective-permute-start.11 = (bf16[640,512]{1,0:T(8,128)(2,1)S(1)}, bf16[640,512]{1,0:T(8,128)(2,1)S(1)}, u32[]{:S(2)}, u32[]{:S(2)}) collective-permute-start(bf16[640,512]{1,0:T(8,128)(2,1)S(1)} %collective-permute-done.3.refs_6_), channel_id=1, source_target_pairs={{4,8},{8,4},{5,9},{9,5},{6,10},{10,6},{7,11},{11,7},{20,24},{24,20... | collective-permute-start | bytes 1966088 | tf_op jit(solution)/shard_map/ppermute | solution.py:392
  33.5 12.8 %copy-start.3 = (bf16[1,40,128,256]{3,2,1,0:T(8,128)(2,1)S(1)}, bf16[1,40,128,256]{3,2,1,0:T(8,128)(2,1)}, u32[]{:S(2)}) copy-start(bf16[1,40,128,256]{3,2,1,0:T(8,128)(2,1)} %param.24) | copy-start | bytes 7864324
  33.5 12.8 %copy-start.12 = (s32[1,8,16]{2,1,0:T(8,128)S(1)}, s32[1,8,16]{2,1,0:T(8,128)}, u32[]{:S(2)}) copy-start(s32[1,8,16]{2,1,0:T(8,128)} %param.26) | copy-start | bytes 1540
  33.5 12.8 %copy-start.13 = (s32[4,8]{1,0:T(4,128)S(1)}, s32[4,8]{1,0:T(4,128)}, u32[]{:S(2)}) copy-start(s32[4,8]{1,0:T(4,128)} %lengths_ref.1) | copy-start | bytes 388
  33.5 12.8 %copy-start.14 = (f32[128]{0:T(128)S(1)}, f32[128]{0:T(128)}, u32[]{:S(2)}) copy-start(f32[128]{0:T(128)} %param.20) | copy-start | bytes 1540
  33.5 12.8 %copy-start.15 = (f32[128]{0:T(128)S(1)}, f32[128]{0:T(128)}, u32[]{:S(2)}) copy-start(f32[128]{0:T(128)} %param.19) | copy-start | bytes 1540
  33.5 12.8 %copy-start.16 = (f32[1,128]{1,0:T(1,128)S(1)}, f32[1,128]{1,0:T(1,128)}, u32[]{:S(2)}) copy-start(f32[1,128]{1,0:T(1,128)} %constant.20.clone.refs_4_) | copy-start | bytes 1540
  43.3 10.6 %collective-permute-start.13 = (bf16[640,512]{1,0:T(8,128)(2,1)S(1)}, bf16[640,512]{1,0:T(8,128)(2,1)S(1)}, u32[]{:S(2)}, u32[]{:S(2)}) collective-permute-start(bf16[640,512]{1,0:T(8,128)(2,1)S(1)} %collective-permute-done.3.refs_6_), channel_id=1, source_target_pairs={{0,16},{4,20},{8,24},{12,28},{16,0},{20,4},{24,8},{28,12},{1,17},{... | collective-permute-start | bytes 1966088 | tf_op jit(solution)/shard_map/ppermute | solution.py:398
  44.8 28.0 %collective-permute-start.8 = (bf16[8,128,640]{2,1,0:T(8,128)(2,1)S(1)}, bf16[8,128,640]{2,1,0:T(8,128)(2,1)S(1)}, u32[]{:S(2)}, u32[]{:S(2)}) collective-permute-start(bf16[8,128,640]{2,1,0:T(8,128)(2,1)S(1)} %shard_map.177.refs_0_), channel_id=1, source_target_pairs={{0,2},{2,0},{1,3},{3,1},{4,6},{6,4},{5,7},{7,5},{8,10},{10,8},{9,1... | collective-permute-start | bytes 3932168 | tf_op jit(solution)/shard_map/ppermute | solution.py:50
  46.3 26.5 %collective-permute-start.9 = (bf16[8,128,640]{2,1,0:T(8,128)(2,1)S(1)}, bf16[8,128,640]{2,1,0:T(8,128)(2,1)S(1)}, u32[]{:S(2)}, u32[]{:S(2)}) collective-permute-start(bf16[8,128,640]{2,1,0:T(8,128)(2,1)S(1)} %shard_map.177.refs_0_), channel_id=1, source_target_pairs={{0,1},{1,0},{2,3},{3,2},{4,5},{5,4},{6,7},{7,6},{8,9},{9,8},{10,11... | collective-permute-start | bytes 3932168 | tf_op jit(solution)/shard_map/ppermute | solution.py:50
  51.6 41.0 %copy-start.6 = (f32[512,128]{1,0:T(8,128)S(1)}, f32[512,128]{1,0:T(8,128)}, u32[]{:S(2)}) copy-start(f32[512,128]{1,0:T(8,128)} %constant.18.clone.refs_9_) | copy-start | bytes 786436
  51.6 41.0 %copy-start.7 = (f32[512,128]{1,0:T(8,128)S(1)}, f32[512,128]{1,0:T(8,128)}, u32[]{:S(2)}) copy-start(f32[512,128]{1,0:T(8,128)} %constant.19.clone.refs_10_) | copy-start | bytes 786436
  51.6 20.0 %collective-permute-start.12 = (bf16[640,512]{1,0:T(8,128)(2,1)S(1)}, bf16[640,512]{1,0:T(8,128)(2,1)S(1)}, u32[]{:S(2)}, u32[]{:S(2)}) collective-permute-start(bf16[640,512]{1,0:T(8,128)(2,1)S(1)} %collective-permute-done.11.refs_4_), channel_id=1, source_target_pairs={{4,0},{8,12},{5,1},{9,13},{6,2},{10,14},{7,3},{11,15},{20,16},{24,... | collective-permute-start | bytes 1966088 | tf_op jit(solution)/shard_map/ppermute | solution.py:392
  53.1 18.6 %collective-permute-start.14 = (bf16[640,512]{1,0:T(8,128)(2,1)S(1)}, bf16[640,512]{1,0:T(8,128)(2,1)S(1)}, u32[]{:S(2)}, u32[]{:S(2)}) collective-permute-start(bf16[640,512]{1,0:T(8,128)(2,1)S(1)} %collective-permute-done.4.refs_8_), channel_id=1, source_target_pairs={{4,20},{8,24},{20,4},{24,8},{5,21},{9,25},{21,5},{25,9},{6,22},{10... | collective-permute-start | bytes 1966088 | tf_op jit(solution)/shard_map/ppermute | solution.py:398
  53.9 19.0 %collective-permute-start.15 = (bf16[640,512]{1,0:T(8,128)(2,1)S(1)}, bf16[640,512]{1,0:T(8,128)(2,1)S(1)}, u32[]{:S(2)}, u32[]{:S(2)}) collective-permute-start(bf16[640,512]{1,0:T(8,128)(2,1)S(1)} %collective-permute-done.10.refs_9_), channel_id=1, source_target_pairs={{0,16},{12,28},{16,0},{28,12},{1,17},{13,29},{17,1},{29,13},{2,18}... | collective-permute-start | bytes 1966088 | tf_op jit(solution)/shard_map/ppermute | solution.py:398
  72.8 6.1 %collective-permute-start.16 = (bf16[8,128,640]{2,1,0:T(8,128)(2,1)S(1)}, bf16[8,128,640]{2,1,0:T(8,128)(2,1)S(1)}, u32[]{:S(2)}, u32[]{:S(2)}) collective-permute-start(bf16[8,128,640]{2,1,0:T(8,128)(2,1)S(1)} %collective-permute-done.8.refs_1_), channel_id=1, source_target_pairs={{0,1},{1,0},{2,3},{3,2},{4,5},{5,4},{6,7},{7,6},{8,9},{9,8},{10,11... | collective-permute-start | bytes 3932168 | tf_op jit(solution)/shard_map/ppermute | solution.py:50
  72.8 8.8 %collective-permute-start.17 = (bf16[640,512]{1,0:T(8,128)(2,1)S(1)}, bf16[640,512]{1,0:T(8,128)(2,1)S(1)}, u32[]{:S(2)}, u32[]{:S(2)}) collective-permute-start(bf16[640,512]{1,0:T(8,128)(2,1)S(1)} %collective-permute-done.11.refs_4_), channel_id=1, source_target_pairs={{4,20},{8,24},{20,4},{24,8},{5,21},{9,25},{21,5},{25,9},{6,22},{10... | collective-permute-start | bytes 1966088 | tf_op jit(solution)/shard_map/ppermute | solution.py:398
  73.5 19.0 %collective-permute-start.18 = (bf16[640,512]{1,0:T(8,128)(2,1)S(1)}, bf16[640,512]{1,0:T(8,128)(2,1)S(1)}, u32[]{:S(2)}, u32[]{:S(2)}) collective-permute-start(bf16[640,512]{1,0:T(8,128)(2,1)S(1)} %collective-permute-done.12.refs_5_), channel_id=1, source_target_pairs={{0,16},{12,28},{16,0},{28,12},{1,17},{13,29},{17,1},{29,13},{2,18}... | collective-permute-start | bytes 1966088 | tf_op jit(solution)/shard_map/ppermute | solution.py:398
  76.0 5.7 %collective-permute-start.19 = (f32[2,32,128]{2,1,0:T(8,128)S(1)}, f32[2,32,128]{2,1,0:T(8,128)S(1)}, u32[]{:S(2)}, u32[]{:S(2)}) collective-permute-start(f32[2,32,128]{2,1,0:T(8,128)S(1)} %get-tuple-element.93), channel_id=1, source_target_pairs={{0,8},{4,12},{1,9},{5,13},{2,10},{6,14},{3,11},{7,15},{16,24},{20,... | collective-permute-start | bytes 98312 | tf_op jit(solution)/shard_map/ppermute | solution.py:541
  (5 other events, 17.6 us)

commit v3 on v2

--- a/solution.py
+++ b/solution.py
@@ -94,7 +94,7 @@
 def project_kernel(count, steps, listed_ref, *refs):
     rows = refs[:count]
     wq_ref, wk_ref, wv_ref, own_ref = refs[count : count + 4]
-    sent_refs, stacked = refs[count + 4 : -1], refs[-1]
+    pair_ref, far_ref, stacked = refs[count + 4 :]
     replica = lax.axis_index("rep")
     half = count // 2
     per = rows[0].shape[0]
@@ -116,8 +116,9 @@
         for piece in range(pieces):
             product = dot(lhs, w_ref[:, piece * width : (piece + 1) * width])
             own_ref[:, at : at + width] = product[:per]
-            for k in range(1, count):
-                sent_refs[k - 1][:, at : at + width] = product[k * pad : k * pad + per].astype(BF16)
+            for i, k in enumerate((1, 3)):
+                pair_ref[i, :, at : at + width] = product[k * pad : k * pad + per].astype(BF16)
+            far_ref[:, at : at + width] = product[2 * pad : 2 * pad + per]
             at += width
 
 
@@ -128,7 +129,11 @@
     total = w_query.shape[1] + 2 * w_key.shape[1]
     return call(
         functools.partial(project_kernel, count, steps),
-        [pltpu.VMEM((per, total), F32)] + [pltpu.VMEM((per, total), BF16)] * (count - 1),
+        [
+            pltpu.VMEM((per, total), F32),
+            pltpu.VMEM((2, per, total), BF16),
+            pltpu.VMEM((per, total), F32),
+        ],
         [*rows, w_query, w_key, w_value],
         [listed],
         scratch=[pltpu.VMEM((count, pad, depth), BF16)],
@@ -152,15 +157,29 @@
     return total
 
 
-def attend_kernel(parts, seq_count, steps, tokens, table_ref, lengths_ref, listed_ref, *refs):
+def old_terms(rows, keys_ref, values_ref, page_of, length, pages, first):
+    page = keys_ref.shape[1]
+    num, den = None, None
+    for i in range(pages):
+        at = first + i
+        scores = dot_rows(rows, keys_ref[page_of(at)])
+        ids = lax.broadcasted_iota(jnp.int32, scores.shape, 1) + at * page
+        weights = jnp.where(ids < length, jnp.exp(scores), 0.0)
+        part = jnp.sum(weights, axis=-1, keepdims=True)
+        mixed = dot(weights.astype(BF16), values_ref[page_of(at)])
+        num = mixed if num is None else num + mixed
+        den = part if den is None else den + part
+    return num, den
+
+
+def queries_kernel(parts, seq_count, steps, tokens, table_ref, lengths_ref, listed_ref, *refs):
     sums = refs[:parts]
     freqs_ref, qgain_ref, kgain_ref, keys_ref, values_ref = refs[parts : parts + 5]
-    num_ref, den_ref, moved_ref, last_ref, q3, k3, v3 = refs[parts + 5 :]
+    q3, k3, v3, moved_ref = refs[parts + 5 :]
     replica = lax.axis_index("rep")
     half = lax.axis_size("rep") // 2
     size = qgain_ref.shape[1]
     width = keys_ref.shape[2]
-    page = keys_ref.shape[1]
     kv_heads = width // size
     heads = kv_heads * 8
     slots = seq_count + 1
@@ -169,7 +188,8 @@
     def total(at):
         value = sums[0][:, at : at + size].astype(F32)
         for other in sums[1:]:
-            value = value + other[:, at : at + size].astype(F32)
+            part = other[0] if len(other.shape) == 3 else other[...]
+            value = value + part[:, at : at + size].astype(F32)
         return value
 
     partner = jnp.where(replica < half, replica, replica - half)
@@ -193,27 +213,32 @@
     for h in range(kv_heads):
         x = total((heads + h) * size)
         x = rotate_rows(x * head_scale(x) * kgain_ref[...], cosine, sine).astype(BF16).astype(F32)
-        k3[:, h * 8 : h * 8 + 8, :] = jnp.broadcast_to(x[:, None, :], (x.shape[0], 8, size))
+        k3[:, h * 8 : h * 8 + 8, :] = jnp.broadcast_to(x[:, None, :], (per, 8, size))
         v = total((heads + kv_heads + h) * size).astype(BF16).astype(F32)
-        v3[:, h * 8 : h * 8 + 8, :] = jnp.broadcast_to(v[:, None, :], (x.shape[0], 8, size))
-
-    def old_terms(rows, page_of, length, pages, first):
-        num, den = None, None
-        for i in range(pages):
-            at = first + i
-            scores = dot_rows(rows, keys_ref[page_of(at)])
-            ids = lax.broadcasted_iota(jnp.int32, scores.shape, 1) + at * page
-            weights = jnp.where(ids < length, jnp.exp(scores), 0.0)
-            part = jnp.sum(weights, axis=-1, keepdims=True)
-            mixed = dot(weights.astype(BF16), values_ref[page_of(at)])
-            num = mixed if num is None else num + mixed
-            den = part if den is None else den + part
-        return num, den
-
-    def rows_of(slot):
-        return q3[pl.ds(slot * steps, steps)].reshape(steps * heads, size)
-
-    for slot in range(slots):
+        v3[:, h * 8 : h * 8 + 8, :] = jnp.broadcast_to(v[:, None, :], (per, 8, size))
+
+    moved_ref[...] = jnp.zeros_like(moved_ref)
+
+    @pl.when(replica < half)
+    def _():
+        slot = listed_ref[replica]
+        length = lengths_ref[replica, slot]
+        rows = q3[pl.ds(slot * steps, steps)].reshape(steps * heads, size)
+        rows = spread_heads(rows, kv_heads).astype(BF16)
+        num, den = old_terms(
+            rows, keys_ref, values_ref, lambda at: table_ref[slot, at], length, table_ref.shape[1], 0
+        )
+        num = own_head(num, kv_heads)
+        moved_ref[0] = num
+        moved_ref[1] = jnp.broadcast_to(den, num.shape)
+
+
+def attend_kernel(seq_count, steps, table_ref, lengths_ref, *refs):
+    q3, k3, v3, keys_ref, values_ref, num_ref, den_ref, last_ref = refs
+    replica = lax.axis_index("rep")
+    heads, size = q3.shape[1:]
+    kv_heads = keys_ref.shape[2] // size
+    for slot in range(seq_count + 1):
         q = q3[slot * steps : (slot + 1) * steps]
         k = k3[slot * steps : (slot + 1) * steps]
         v = v3[slot * steps : (slot + 1) * steps]
@@ -227,10 +252,16 @@
             nums.append(num)
             dens.append(den)
         num, den = jnp.concatenate(nums, axis=0), jnp.concatenate(dens, axis=0)
-        rows = spread_heads(rows_of(slot), kv_heads).astype(BF16)
+        rows = spread_heads(q.reshape(steps * heads, size), kv_heads).astype(BF16)
         if slot < seq_count:
             old_num, old_den = old_terms(
-                rows, lambda at: table_ref[slot, at], lengths_ref[replica, slot], KEEP_PAGES, 0
+                rows,
+                keys_ref,
+                values_ref,
+                lambda at: table_ref[slot, at],
+                lengths_ref[replica, slot],
+                KEEP_PAGES,
+                0,
             )
             num = num + own_head(old_num, kv_heads)
             den = den + old_den
@@ -241,30 +272,6 @@
             steps, heads, size
         )
 
-    moved_ref[...] = jnp.zeros_like(moved_ref)
-
-    @pl.when(replica < half)
-    def _():
-        slot = listed_ref[replica]
-        length = lengths_ref[replica, slot]
-        rows = spread_heads(rows_of(slot), kv_heads).astype(BF16)
-        pages = table_ref.shape[1]
-        at_once = 4
-
-        def turn(i, carry):
-            num, den = old_terms(rows, lambda at: table_ref[slot, at], length, at_once, i * at_once)
-            return carry[0] + num, carry[1] + den
-
-        num, den = lax.fori_loop(
-            0,
-            pages // at_once,
-            turn,
-            (jnp.zeros((steps * heads, width), F32), jnp.zeros((steps * heads, 1), F32)),
-        )
-        num = own_head(num, kv_heads)
-        moved_ref[0] = num
-        moved_ref[1] = jnp.broadcast_to(den, num.shape)
-
 
 def norm_blocks_kernel(x_ref, gain_ref, out_ref):
     width = out_ref.shape[2]
@@ -287,8 +294,8 @@
 
 
 def first_kernel(*refs):
-    xs = refs[:4]
-    wk_ref, wv_ref, a_ref, ya_ref, b_ref, c_ref, yb_ref, yc_ref, acc_ref = refs[4:]
+    xs, (wk_ref, wv_ref), (a_ref, ya_ref, b_ref, c_ref, yb_ref, yc_ref) = refs[:4], refs[4:6], refs[6:12]
+    acc_ref = refs[12]
     replica = lax.axis_index("rep")
     middle = (replica == 1) | (replica == 2)
     width = wk_ref.shape[1]
@@ -299,31 +306,27 @@
 
     keys, values = None, None
     for k in range(2):
-        x = block(k)
-        more_k = dot(x, wk_ref[k * depth : (k + 1) * depth])
-        more_v = dot(x, wv_ref[k * depth : (k + 1) * depth])
+        more_k = dot(block(k), wk_ref[k * depth : (k + 1) * depth])
+        more_v = dot(block(k), wv_ref[k * depth : (k + 1) * depth])
         keys = more_k if keys is None else keys + more_k
         values = more_v if values is None else values + more_v
-    acc_ref[:, :width] = keys
-    acc_ref[:, width:] = values
-    acc_ref[...] += dot(block(2), a_ref[...])
-    acc_ref[...] += dot(block(3), ya_ref[...])
+    both = dot(block(2), a_ref[...]) + dot(block(3), ya_ref[...])
+    acc_ref[:, :width] = keys + both[:, :width]
+    acc_ref[:, width:] = values + both[:, width:]
 
     @pl.when(middle)
     def _():
-        acc_ref[...] += dot(block(4), b_ref[...])
-        acc_ref[...] += dot(block(5), yb_ref[...])
+        acc_ref[...] += dot(block(4), b_ref[...]) + dot(block(5), yb_ref[...])
 
     @pl.when(jnp.logical_not(middle))
     def _():
-        acc_ref[...] += dot(block(4), c_ref[...])
-        acc_ref[...] += dot(block(5), yc_ref[...])
+        acc_ref[...] += dot(block(4), c_ref[...]) + dot(block(5), yc_ref[...])
 
 
 def tail_kernel(far, steps, listed_ref, *refs):
     if far:
-        xs, (d_ref, e_ref, yd_ref, ye_ref) = refs[:4], refs[4:8]
-        refs = refs[8:]
+        xs, (d_ref, yd_ref, ek_ref, ev_ref, yek_ref, yev_ref) = refs[:4], refs[4:10]
+        refs = refs[10:]
     acc_ref, cos_ref, sin_ref, kgain_ref, rows_ref, num_ref, den_ref, moved_ref = refs[:8]
     keys_ref, values_ref, out_ref, o3 = refs[8:12]
     replica = lax.axis_index("rep")
@@ -347,7 +350,7 @@
 
         @pl.when(jnp.logical_not(middle))
         def _():
-            fresh[...] = acc_ref[...] + dot(block(6), e_ref[...]) + dot(block(7), ye_ref[...])
+            fresh[...] = acc_ref[...] + dot(block(6), ek_ref[...]) + dot(block(7), yek_ref[...])
 
         tp, sub = lax.axis_index("tp"), lax.axis_index("sub")
         places = [tp * 2 + sub, (tp ^ 1) * 2 + sub, tp * 2 + (sub ^ 1), (tp ^ 1) * 2 + (sub ^ 1)]
@@ -388,6 +391,10 @@
             ].astype(BF16)
 
 
+def after(value, *others):
+    return lax.optimization_barrier((value, *others))[0]
+
+
 def line_pairs(pairs, axis="rep"):
     return lambda value: lax.ppermute(value, axis, pairs)
 
@@ -395,6 +402,12 @@
 def across_groups(value, replicas):
     count = lax.axis_size("rep")
     pairs = [(g * count + r, (1 - g) * count + r) for g in range(2) for r in replicas]
+    return lax.ppermute(value, ("groups", "rep"), pairs)
+
+
+def diagonal(value, pairs):
+    count = lax.axis_size("rep")
+    pairs = [(count * g + a, count * (1 - g) + b) for g in range(2) for a, b in pairs]
     return lax.ppermute(value, ("groups", "rep"), pairs)
 
 
@@ -434,33 +447,74 @@
         and lax.axis_size("groups") == 2
     )
 
+    rec_cos, rec_sin = rope_tables(tokens, head_size)
+    flat = (per, heads, head_size)
+    keys, values = pool_keys[0], pool_values[0]
+
+    def queries(*sums):
+        return call(
+            functools.partial(queries_kernel, len(sums), seq_count, steps, tokens),
+            [pltpu.VMEM(flat, F32)] * 3 + [pltpu.VMEM((2, steps * heads, head_size), F32)],
+            [*sums, jnp.asarray(rope_freqs(head_size)), qgain, kgain, keys, values],
+            [table, seq_lengths, listed_slot],
+        )
+
+    def attend(q3, k3, v3):
+        return call(
+            functools.partial(attend_kernel, seq_count, steps),
+            [pltpu.VMEM(flat, F32)] * 2 + [pltpu.VMEM((steps * heads, width), BF16)],
+            [q3, k3, v3, keys, values],
+            [table, seq_lengths],
+        )
+
     if near:
         group = lax.axis_index("groups")
+        middle = (replica == 1) | (replica == 2)
         rows = depth // 2
         own = jnp.concatenate(
             [lax.dynamic_slice_in_dim(w, group * rows, rows, 0) for w in (w_key, w_value)], axis=1
         )
-
-    if near:
         spread = call(
-            norm_spread_kernel, [pltpu.VMEM((per, depth), BF16)] * replicas, [dec_hidden[0], gain], []
-        )
-        rec_hidden, *spread = lax.optimization_barrier((rec_hidden, *spread))
+            norm_spread_kernel, [pltpu.VMEM((per, depth), BF16)] * 4, [dec_hidden[0], gain], []
+        )
         (blocks,) = call(
             norm_blocks_kernel,
             [pltpu.VMEM((2 * replicas, rec_hidden.shape[1], rows), BF16)],
             [rec_hidden[0], gain],
             [],
         )
-        spread = [spread[0]] + [xor_permute(spread[k], "rep", k) for k in range(1, replicas)]
-        own, *spread = lax.optimization_barrier((own, *spread))
-        from_a = line_pairs([(0, 1), (1, 0), (2, 3), (3, 2)])(own)
-        from_b = line_pairs([(1, 2), (2, 1)])(own)
-        own_sums, *sent = project_new(spread, listed_slot, w_query, w_key, w_value, steps)
-        sums = [xor_permute(sent[k - 1], "rep", k) for k in range(1, replicas)]
-        from_a, from_b, _ = lax.optimization_barrier((from_a, from_b, sent[0]))
-        late_a, blocks, *sums = lax.optimization_barrier((from_a, blocks, *sums))
-        sums = [own_sums, *sums]
+        s1 = xor_permute(spread[1], "rep", 1)
+        s2 = xor_permute(spread[2], "rep", 2)
+        s3 = xor_permute(spread[3], "rep", 3)
+        from_a = line_pairs([(0, 1), (1, 0), (2, 3), (3, 2)])(after(own, s1, s2, s3))
+        from_b = line_pairs([(1, 2), (2, 1)])(after(own, s1, s2, s3))
+        across = xor_permute(after(blocks, s1, s2, s3), "tp", 1)
+        own_sums, pair, far_sums = project_new(
+            [spread[0], s1, s2, s3], listed_slot, w_query, w_key, w_value, steps
+        )
+        from_d = line_pairs([(1, 2), (2, 1)])(after(from_a, from_b, far_sums))
+        from_c = line_pairs([(1, 0), (2, 3)])(after(from_b, from_a, far_sums))
+        beside = xor_permute(after(blocks, from_d, from_c), "sub", 1)
+        over_c = across_groups(from_c, (0, 3))
+        pair_in = xor_permute(pair, "rep", 1)
+        over_a = across_groups(after(from_a, pair_in), range(4))
+        over_b = across_groups(after(from_b, pair_in), (1, 2))
+        r2 = xor_permute((far_sums + pair_in[1].astype(F32)).astype(BF16), "rep", 2)
+        from_e = line_pairs([(1, 0), (2, 3)])(after(from_d, from_c, r2))
+        over_e = across_groups(after(from_e, across, over_a, over_b, over_c), (0, 3))
+        over_d = across_groups(after(from_d, from_e, over_a, over_b, over_c), (1, 2))
+        corner = xor_permute(after(across, from_e, over_a, over_b, over_c), "sub", 1)
+        (acc,) = call(
+            first_kernel,
+            [pltpu.VMEM((tokens, 2 * width), F32)],
+            [blocks, across, beside, corner, w_key, w_value, from_a, over_a, from_b, from_c, over_b, over_c],
+            [],
+            flops=3 * depth * tokens * width * 4,
+        )
+        q3, k3, v3, moved = queries(own_sums, pair_in, r2)
+        returned = lax.ppermute(after(moved, from_e), "rep", [(i, i + half) for i in range(half)])
+        num, den, rows_last = attend(q3, k3, v3)
+        far = [blocks, across, beside, corner, from_d, over_d, from_e, from_e, over_e, over_e]
     else:
         spread = lax.all_to_all(
             normalize(dec_hidden[0].reshape(per, features), norm_gain), "rep", split_axis=1, concat_axis=0, tiled=True
@@ -479,14 +533,6 @@
                 tiled=True,
             )
         ]
-
-    rec_cos, rec_sin = rope_tables(tokens, head_size)
-    if near:
-        across = xor_permute(blocks, "tp", 1)
-        from_d = line_pairs([(1, 2), (2, 1)])(from_a)
-        from_c = line_pairs([(1, 0), (2, 3)])(from_b)
-        over_a = across_groups(late_a, range(4))
-    else:
         normed = lax.all_gather(
             normalize(rec_hidden[0], norm_gain), ("tp", "sub"), axis=0, tiled=True
         )
@@ -501,44 +547,10 @@
             ],
             axis=1,
         )
-
-    flat = (per, heads, head_size)
-    num, den, moved, rows_last = call(
-        functools.partial(attend_kernel, len(sums), seq_count, steps, tokens),
-        [
-            pltpu.VMEM(flat, F32),
-            pltpu.VMEM(flat, F32),
-            pltpu.VMEM((2, steps * heads, head_size), F32),
-            pltpu.VMEM((steps * heads, width), BF16),
-        ],
-        [*sums, jnp.asarray(rope_freqs(head_size)), qgain, kgain, pool_keys[0], pool_values[0]],
-        [table, seq_lengths, listed_slot],
-        scratch=[pltpu.VMEM(flat, F32)] * 3,
-    )
-    far = []
-    if near:
-        from_b, from_c, from_d, num, den, moved, rows_last = lax.optimization_barrier(
-            (from_b, from_c, from_d, num, den, moved, rows_last)
-        )
-        from_e = line_pairs([(1, 0), (2, 3)])(from_d)
-        over_b = across_groups(from_b, (1, 2))
-        over_c = across_groups(from_c, (0, 3))
-        beside = xor_permute(blocks, "sub", 1)
-        across, beside, from_d, from_e, over_a, over_b, over_c, moved = lax.optimization_barrier(
-            (across, beside, from_d, from_e, over_a, over_b, over_c, moved)
-        )
-        over_d = across_groups(from_d, (1, 2))
-        over_e = across_groups(from_e, (0, 3))
-        xs = [blocks, across, beside, xor_permute(across, "sub", 1)]
-        (acc,) = call(
-            first_kernel,
-            [pltpu.VMEM((tokens, 2 * width), F32)],
-            [*xs, w_key, w_value, from_a, over_a, from_b, from_c, over_b, over_c],
-            [],
-            flops=3 * depth * tokens * width * 4,
-        )
-        far = [*xs, from_d, from_e, over_d, over_e]
-    moved = lax.ppermute(moved, "rep", [(i, i + half) for i in range(half)])
+        far = []
+        q3, k3, v3, moved = queries(*sums)
+        returned = lax.ppermute(moved, "rep", [(i, i + half) for i in range(half)])
+        num, den, rows_last = attend(q3, k3, v3)
 
     rec_k, rec_v, decoded = call(
         functools.partial(tail_kernel, bool(far), steps),
@@ -547,7 +559,7 @@
             shaped((tokens, width), BF16),
             shaped((slots, steps, heads * head_size), BF16),
         ],
-        [*far, acc, rec_cos, rec_sin, kgain, rows_last, num, den, moved],
+        [*far, acc, rec_cos, rec_sin, kgain, rows_last, num, den, returned],
         [listed_slot],
         scratch=[pltpu.VMEM(flat, F32)] + [pltpu.VMEM((tokens, 2 * width), F32)] * bool(far),
         flops=depth * tokens * width * 4,

time: 96 us -> 92.9 us (0.968)
  waiting for transfers between devices: 46 us -> 43.1 us
    ppermute x9 -> x8, waiting for transfers between devices: 13.7 us -> 21.4 us  [xor_permute(): return lax.ppermute(value, axis, [(i, i ^ distance) for i in range(count)])]
    ppermute x5, waiting for transfers between devices: 12.2 us -> 6.29 us  [across_groups(): return lax.ppermute(value, ('groups', 'rep'), pairs)]
    ppermute x5, waiting for transfers between devices: 20.1 us -> 15.5 us  [line_pairs(): return lambda value: lax.ppermute(value, axis, pairs)]
    ppermute x1, starting transfers between devices: 2.92 us -> 1.42 us  [body(): lax.ppermute(after(moved, from_e), 'rep', [(i, i + half) for i in range(h...]
    ppermute x5, starting transfers between devices: 8.74 us -> 9.76 us  [across_groups(): return lax.ppermute(value, ('groups', 'rep'), pairs)]
    pallas_call x6 -> x7, Pallas kernels: 13.8 us -> 14.2 us  [call(): pl.pallas_call(kernel, out_shape=tuple(outs), in_specs=[SCALAR] * len(sca...]
    ppermute x9 -> x8, starting transfers between devices: 13.5 us -> 13.6 us  [xor_permute(): return lax.ppermute(value, axis, [(i, i ^ distance) for i in range(count)])]
  transfers between devices with their start and end apart: 20 -> 19, of which waited for: 9 -> 8; matrix products, arithmetic and copies ran while one was open for 1% -> 1% of each run, Pallas kernels for 11% -> 12%
where the time goes in v3:
time: 92.9 us; the launch traced here: 92.5 us
  waiting for transfers between devices  43.1 us (46%)
  starting transfers between devices  28.7 us (31%)
  Pallas kernels  14.2 us (15%)
  local copies, waits for them, and re-layouts  5.41 us (6%)
  between operations  0.99 us (1%)
    ppermute x8, waiting for transfers between devices, xor_permute(): return lax.ppermute(value, axis, [(i, i ^ distance) for i in range(count)])  21.4 us
    ppermute x5, waiting for transfers between devices, line_pairs(): return lambda value: lax.ppermute(value, axis, pairs)  15.5 us
    pallas_call x7, Pallas kernels, call(): pl.pallas_call(kernel, out_shape=tuple(outs), in_specs=[SCALAR] * len(sca...  14.2 us
    ppermute x8, starting transfers between devices, xor_permute(): return lax.ppermute(value, axis, [(i, i ^ distance) for i in range(count)])  13.6 us
    ppermute x5, starting transfers between devices, across_groups(): return lax.ppermute(value, ('groups', 'rep'), pairs)  9.76 us
    ppermute x5, waiting for transfers between devices, across_groups(): return lax.ppermute(value, ('groups', 'rep'), pairs)  6.29 us
    unnamed x34, local copies, waits for them, and re-layouts  4.19 us
    ppermute x5, starting transfers between devices, line_pairs(): return lambda value: lax.ppermute(value, axis, pairs)  3.97 us
  transfers between devices with their start and end apart: 19, of which 8 were waited for; matrix products, arithmetic and copies ran while one was open for 1% of the time, Pallas kernels for 12%

profile of v3, /device:TPU:0, one launch (start us, length us, event | category | flops | bytes accessed | tf_op | source)
XLA Modules:
  0.0 92.5 jit_solution(18330241788588862923)
XLA Ops:
  0.6 0.9 copy-done.8
  1.6 0.7 copy-done.9
  2.7 3.1 %collective-permute-start = (bf16[18,1280]{1,0:T(8,128)(2,1)S(1)}, bf16[18,1280]{1,0:T(8,128)(2,1)S(1)}, u32[]{:S(2)}, u32[]{:S(2)}) collective-permute-start(bf16[18,1280]{1,0:T(8,128)(2,1)S(1)} %get-tuple-element.32), channel_id=1, source_target_pairs={{0,4},{4,0},{8,12},{12,8},{1,5},{5,1},{9,13},{13,9},{2,6},{6,2},{1... | collective-permute-start | bytes 138248 | tf_op jit(solution)/shard_map/ppermute | solution.py:50
  5.8 2.6 %collective-permute-start.1 = (bf16[18,1280]{1,0:T(8,128)(2,1)S(1)}, bf16[18,1280]{1,0:T(8,128)(2,1)S(1)}, u32[]{:S(2)}, u32[]{:S(2)}) collective-permute-start(bf16[18,1280]{1,0:T(8,128)(2,1)S(1)} %get-tuple-element.33), channel_id=1, source_target_pairs={{0,8},{4,12},{8,0},{12,4},{1,9},{5,13},{9,1},{13,5},{2,10},{6,14},... | collective-permute-start | bytes 138248 | tf_op jit(solution)/shard_map/ppermute | solution.py:50
  8.4 1.2 %constant_dynamic-slice_fusion = (bf16[640,256]{1,0:T(8,128)(2,1)S(1)}, bf16[640,256]{1,0:T(8,128)(2,1)S(1)}) fusion(bf16[1280,256]{1,0:T(8,128)(2,1)} %refs_5_.3, s32[]{:T(128)S(6)} %select_n.4, bf16[1280,256]{1,0:T(8,128)(2,1)} %refs_4_.3), kind=kLoop, calls=%fused_computation.4 | loop fusion | bytes 1310724 | tf_op jit(solution)/shard_map/dynamic_slice | solution.py:475
  9.6 2.5 %collective-permute-done.1.refs_2_ = bf16[18,1280]{1,0:T(8,128)(2,1)S(1)} collective-permute-done((bf16[18,1280]{1,0:T(8,128)(2,1)S(1)}, bf16[18,1280]{1,0:T(8,128)(2,1)S(1)}, u32[]{:S(2)}, u32[]{:S(2)}) %collective-permute-start.1) | collective-permute-done | bytes 46112 | tf_op jit(solution)/shard_map/ppermute | solution.py:50
  12.1 2.3 %collective-permute-done.2.refs_3_ = bf16[18,1280]{1,0:T(8,128)(2,1)S(1)} collective-permute-done((bf16[18,1280]{1,0:T(8,128)(2,1)S(1)}, bf16[18,1280]{1,0:T(8,128)(2,1)S(1)}, u32[]{:S(2)}, u32[]{:S(2)}) %collective-permute-start.2) | collective-permute-done | bytes 46112 | tf_op jit(solution)/shard_map/ppermute | solution.py:50
  14.4 0.7 collective-permute-start.5
  15.1 2.5 %copy-done.2 = bf16[1280,2048]{1,0:T(8,128)(2,1)S(1)} copy-done((bf16[1280,2048]{1,0:T(8,128)(2,1)S(1)}, bf16[1280,2048]{1,0:T(8,128)(2,1)}, u32[]{:S(2)}) %copy-start.2) | copy-done | bytes 5242904
  17.6 1.7 %shard_map.177 = (f32[18,2560]{1,0:T(8,128)S(1)}, bf16[2,18,2560]{2,1,0:T(8,128)(2,1)S(1)}, f32[18,2560]{1,0:T(8,128)S(1)}) custom-call(s32[4]{0:T(128)S(1)} %copy-done.13, bf16[18,1280]{1,0:T(8,128)(2,1)S(1)} %get-tuple-element.37.refs_0_, bf16[18,1280]{1,0:T(8,128)(2,1)S(1)} %collective-permute-done.refs_1_, ...), custom_call_target="tpu_custom_call" | custom-call | flops 471859200 | bytes 7290880 | tf_op jit(solution)/shard_map/pallas_call | solution.py:25
  19.3 3.9 %collective-permute-start.9 = (bf16[2,18,2560]{2,1,0:T(8,128)(2,1)S(1)}, bf16[2,18,2560]{2,1,0:T(8,128)(2,1)S(1)}, u32[]{:S(2)}, u32[]{:S(2)}) collective-permute-start(bf16[2,18,2560]{2,1,0:T(8,128)(2,1)S(1)} %get-tuple-element.42), channel_id=1, source_target_pairs={{0,4},{4,0},{8,12},{12,8},{1,5},{5,1},{9,13},{13,9},{2,6},{6,2},{1... | collective-permute-start | bytes 552968 | tf_op jit(solution)/shard_map/ppermute | solution.py:50
  23.3 0.7 shard_map.175.refs_0_
  24.0 1.6 %collective-permute-start.3 = (bf16[8,128,640]{2,1,0:T(8,128)(2,1)S(1)}, bf16[8,128,640]{2,1,0:T(8,128)(2,1)S(1)}, u32[]{:S(2)}, u32[]{:S(2)}) collective-permute-start(bf16[8,128,640]{2,1,0:T(8,128)(2,1)S(1)} %shard_map.175.refs_0_), channel_id=1, source_target_pairs={{0,2},{2,0},{1,3},{3,1},{4,6},{6,4},{5,7},{7,5},{8,10},{10,8},{9,1... | collective-permute-start | bytes 3932168 | tf_op jit(solution)/shard_map/ppermute | solution.py:50
  25.6 6.3 %collective-permute-done.4.refs_6_ = bf16[640,512]{1,0:T(8,128)(2,1)S(1)} collective-permute-done((bf16[640,512]{1,0:T(8,128)(2,1)S(1)}, bf16[640,512]{1,0:T(8,128)(2,1)S(1)}, u32[]{:S(2)}, u32[]{:S(2)}) %collective-permute-start.4) | collective-permute-done | bytes 655392 | tf_op jit(solution)/shard_map/ppermute | solution.py:399
  31.9 1.3 %collective-permute-start.7 = (bf16[640,512]{1,0:T(8,128)(2,1)S(1)}, bf16[640,512]{1,0:T(8,128)(2,1)S(1)}, u32[]{:S(2)}, u32[]{:S(2)}) collective-permute-start(bf16[640,512]{1,0:T(8,128)(2,1)S(1)} %collective-permute-done.5.refs_8_), channel_id=1, source_target_pairs={{4,0},{8,12},{5,1},{9,13},{6,2},{10,14},{7,3},{11,15},{20,16},{24,... | collective-permute-start | bytes 1966088 | tf_op jit(solution)/shard_map/ppermute | solution.py:399
  33.2 0.7 collective-permute-start.6
  33.9 3.1 %collective-permute-done.9.refs_1_ = bf16[2,18,2560]{2,1,0:T(8,128)(2,1)S(1)} collective-permute-done((bf16[2,18,2560]{2,1,0:T(8,128)(2,1)S(1)}, bf16[2,18,2560]{2,1,0:T(8,128)(2,1)S(1)}, u32[]{:S(2)}, u32[]{:S(2)}) %collective-permute-start.9) | collective-permute-done | bytes 184352 | tf_op jit(solution)/shard_map/ppermute | solution.py:50
  37.0 2.4 %collective-permute-start.10 = (bf16[18,2560]{1,0:T(8,128)(2,1)S(1)}, bf16[18,2560]{1,0:T(8,128)(2,1)S(1)}, u32[]{:S(2)}, u32[]{:S(2)}) collective-permute-start(bf16[18,2560]{1,0:T(8,128)(2,1)S(1)} %fusion), channel_id=1, source_target_pairs={{0,8},{4,12},{8,0},{12,4},{1,9},{5,13},{9,1},{13,5},{2,10},{6,14},... | collective-permute-start | bytes 276488 | tf_op jit(solution)/shard_map/ppermute | solution.py:50
  39.3 1.5 %collective-permute-start.12 = (bf16[640,512]{1,0:T(8,128)(2,1)S(1)}, bf16[640,512]{1,0:T(8,128)(2,1)S(1)}, u32[]{:S(2)}, u32[]{:S(2)}) collective-permute-start(bf16[640,512]{1,0:T(8,128)(2,1)S(1)} %collective-permute-done.4.refs_6_), channel_id=1, source_target_pairs={{0,16},{4,20},{8,24},{12,28},{16,0},{20,4},{24,8},{28,12},{1,17},{... | collective-permute-start | bytes 1966088 | tf_op jit(solution)/shard_map/ppermute | solution.py:405
  40.8 13.6 %collective-permute-done.10.refs_2_ = bf16[18,2560]{1,0:T(8,128)(2,1)S(1)} collective-permute-done((bf16[18,2560]{1,0:T(8,128)(2,1)S(1)}, bf16[18,2560]{1,0:T(8,128)(2,1)S(1)}, u32[]{:S(2)}, u32[]{:S(2)}) %collective-permute-start.10) | collective-permute-done | bytes 92192 | tf_op jit(solution)/shard_map/ppermute | solution.py:50
  55.2 1.3 %collective-permute-start.11 = (bf16[640,512]{1,0:T(8,128)(2,1)S(1)}, bf16[640,512]{1,0:T(8,128)(2,1)S(1)}, u32[]{:S(2)}, u32[]{:S(2)}) collective-permute-start(bf16[640,512]{1,0:T(8,128)(2,1)S(1)} %collective-permute-done.6.refs_4_), channel_id=1, source_target_pairs={{4,0},{8,12},{5,1},{9,13},{6,2},{10,14},{7,3},{11,15},{20,16},{24,... | collective-permute-start | bytes 1966088 | tf_op jit(solution)/shard_map/ppermute | solution.py:399
  56.5 3.4 %collective-permute-start.14 = (bf16[640,512]{1,0:T(8,128)(2,1)S(1)}, bf16[640,512]{1,0:T(8,128)(2,1)S(1)}, u32[]{:S(2)}, u32[]{:S(2)}) collective-permute-start(bf16[640,512]{1,0:T(8,128)(2,1)S(1)} %collective-permute-done.7.refs_9_), channel_id=1, source_target_pairs={{0,16},{12,28},{16,0},{28,12},{1,17},{13,29},{17,1},{29,13},{2,18}... | collective-permute-start | bytes 1966088 | tf_op jit(solution)/shard_map/ppermute | solution.py:405
  60.0 9.2 %collective-permute-done.11.refs_6_.refs_7_ = bf16[640,512]{1,0:T(8,128)(2,1)S(1)} collective-permute-done((bf16[640,512]{1,0:T(8,128)(2,1)S(1)}, bf16[640,512]{1,0:T(8,128)(2,1)S(1)}, u32[]{:S(2)}, u32[]{:S(2)}) %collective-permute-start.11) | collective-permute-done | bytes 655392 | tf_op jit(solution)/shard_map/ppermute | solution.py:399
  69.2 1.3 %collective-permute-done.14.refs_11_ = bf16[640,512]{1,0:T(8,128)(2,1)S(1)} collective-permute-done((bf16[640,512]{1,0:T(8,128)(2,1)S(1)}, bf16[640,512]{1,0:T(8,128)(2,1)S(1)}, u32[]{:S(2)}, u32[]{:S(2)}) %collective-permute-start.14) | collective-permute-done | bytes 655392 | tf_op jit(solution)/shard_map/ppermute | solution.py:405
  70.5 3.4 %collective-permute-start.17 = (bf16[640,512]{1,0:T(8,128)(2,1)S(1)}, bf16[640,512]{1,0:T(8,128)(2,1)S(1)}, u32[]{:S(2)}, u32[]{:S(2)}) collective-permute-start(bf16[640,512]{1,0:T(8,128)(2,1)S(1)} %collective-permute-done.11.refs_6_.refs_7_), channel_id=1, source_target_pairs={{0,16},{12,28},{16,0},{28,12},{1,17},{13,29},{17,1},{29,13},{2,18}... | collective-permute-start | bytes 1966088 | tf_op jit(solution)/shard_map/ppermute | solution.py:405
  73.9 0.7 collective-permute-start.16
  74.7 3.0 %shard_map.179 = (f32[18,16,128]{2,1,0:T(8,128)S(1)}, f32[18,16,128]{2,1,0:T(8,128)S(1)}, f32[18,16,128]{2,1,0:T(8,128)S(1)}, f32[2,32,128]{2,1,0:T(8,128)S(1)}) custom-call(s32[8,16]{1,0:T(8,128)S(1)} %bitcast.24, s32[4,8]{1,0:T(4,128)S(1)} %copy-done.12, s32[4]{0:T(128)S(1)} %copy-done.13, f32[18,2560]{1,0:T(8,128)S(1)} %get-tuple-element.49.refs_0_, ...), custom_call_target="tpu_custom_call" | custom-call | bytes 6180352 | tf_op jit(solution)/shard_map/pallas_call | solution.py:25
  77.7 2.6 %shard_map.180 = (f32[18,16,128]{2,1,0:T(8,128)S(1)}, f32[18,16,128]{2,1,0:T(8,128)S(1)}, bf16[32,256]{1,0:T(8,128)(2,1)S(1)}) custom-call(s32[8,16]{1,0:T(8,128)S(1)} %bitcast.25, s32[4,8]{1,0:T(4,128)S(1)} %copy-done.12, f32[18,16,128]{2,1,0:T(8,128)S(1)} %get-tuple-element.50.refs_0_, f32[18,16,128]{2,1,0:T(8,128)S(1)} %get-tuple-element.51.refs_1_, ...), custom_call_target="tpu_custom_call" | custom-call | bytes 5996544 | tf_op jit(solution)/shard_map/pallas_call | solution.py:25
  80.3 1.4 %collective-permute-start.18 = (f32[2,32,128]{2,1,0:T(8,128)S(1)}, f32[2,32,128]{2,1,0:T(8,128)S(1)}, u32[]{:S(2)}, u32[]{:S(2)}) collective-permute-start(f32[2,32,128]{2,1,0:T(8,128)S(1)} %get-tuple-element.57), channel_id=1, source_target_pairs={{0,8},{4,12},{1,9},{5,13},{2,10},{6,14},{3,11},{7,15},{16,24},{20,... | collective-permute-start | bytes 98312 | tf_op jit(solution)/shard_map/ppermute | solution.py:515
  81.7 2.8 %shard_map.178.refs_10_ = f32[512,512]{1,0:T(8,128)S(1)} custom-call(bf16[8,128,640]{2,1,0:T(8,128)(2,1)S(1)} %shard_map.175.refs_0_, bf16[8,128,640]{2,1,0:T(8,128)(2,1)S(1)} %collective-permute-done.3.refs_1_, bf16[8,128,640]{2,1,0:T(8,128)(2,1)S(1)} %collective-permute-done.8.refs_2_, bf16[8,128,640]{2,1,0:T(8,128)(2,1)S(1)} %collective-permute-done.15.refs_3_, ...), custom_call_target="tpu_custom_call" | custom-call | flops 2013265920 | bytes 11534336 | tf_op jit(solution)/shard_map/pallas_call | solution.py:25
  84.5 5.0 %collective-permute-done.17.refs_8_.refs_9_ = bf16[640,512]{1,0:T(8,128)(2,1)S(1)} collective-permute-done((bf16[640,512]{1,0:T(8,128)(2,1)S(1)}, bf16[640,512]{1,0:T(8,128)(2,1)S(1)}, u32[]{:S(2)}, u32[]{:S(2)}) %collective-permute-start.17) | collective-permute-done | bytes 655392 | tf_op jit(solution)/shard_map/ppermute | solution.py:405
  89.5 3.0 %shard_map.181 = (bf16[512,256]{1,0:T(8,128)(2,1)}, bf16[512,256]{1,0:T(8,128)(2,1)}, bf16[9,2,2048]{2,1,0:T(2,128)(2,1)}) custom-call(s32[4]{0:T(128)S(1)} %copy-done.13, bf16[8,128,640]{2,1,0:T(8,128)(2,1)S(1)} %shard_map.175.refs_0_, bf16[8,128,640]{2,1,0:T(8,128)(2,1)S(1)} %collective-permute-done.3.refs_1_, ...), custom_call_target="tpu_custom_call" | custom-call | flops 671088640 | bytes 11690496 | tf_op jit(solution)/shard_map/pallas_call | solution.py:25
  (50 shorter events, 1.3 us)
Async XLA Ops:
  2.7 7.0 %collective-permute-start = (bf16[18,1280]{1,0:T(8,128)(2,1)S(1)}, bf16[18,1280]{1,0:T(8,128)(2,1)S(1)}, u32[]{:S(2)}, u32[]{:S(2)}) collective-permute-start(bf16[18,1280]{1,0:T(8,128)(2,1)S(1)} %get-tuple-element.32), channel_id=1, source_target_pairs={{0,4},{4,0},{8,12},{12,8},{1,5},{5,1},{9,13},{13,9},{2,6},{6,2},{1... | collective-permute-start | bytes 138248 | tf_op jit(solution)/shard_map/ppermute | solution.py:50
  5.8 6.3 %collective-permute-start.1 = (bf16[18,1280]{1,0:T(8,128)(2,1)S(1)}, bf16[18,1280]{1,0:T(8,128)(2,1)S(1)}, u32[]{:S(2)}, u32[]{:S(2)}) collective-permute-start(bf16[18,1280]{1,0:T(8,128)(2,1)S(1)} %get-tuple-element.33), channel_id=1, source_target_pairs={{0,8},{4,12},{8,0},{12,4},{1,9},{5,13},{9,1},{13,5},{2,10},{6,14},... | collective-permute-start | bytes 138248 | tf_op jit(solution)/shard_map/ppermute | solution.py:50
  8.3 6.0 %collective-permute-start.2 = (bf16[18,1280]{1,0:T(8,128)(2,1)S(1)}, bf16[18,1280]{1,0:T(8,128)(2,1)S(1)}, u32[]{:S(2)}, u32[]{:S(2)}) collective-permute-start(bf16[18,1280]{1,0:T(8,128)(2,1)S(1)} %get-tuple-element.34), channel_id=1, source_target_pairs={{0,12},{4,8},{8,4},{12,0},{1,13},{5,9},{9,5},{13,1},{2,14},{6,10},... | collective-permute-start | bytes 138248 | tf_op jit(solution)/shard_map/ppermute | solution.py:50
  8.3 6.7 %copy-start.3 = (bf16[1280,256]{1,0:T(8,128)(2,1)S(1)}, bf16[1280,256]{1,0:T(8,128)(2,1)}, u32[]{:S(2)}) copy-start(bf16[1280,256]{1,0:T(8,128)(2,1)} %refs_5_.3) | copy-start | bytes 1966084
  8.3 6.7 %copy-start.4 = (bf16[1280,256]{1,0:T(8,128)(2,1)S(1)}, bf16[1280,256]{1,0:T(8,128)(2,1)}, u32[]{:S(2)}) copy-start(bf16[1280,256]{1,0:T(8,128)(2,1)} %refs_4_.3) | copy-start | bytes 1966084
  8.3 6.7 %copy-start.13 = (s32[4]{0:T(128)S(1)}, s32[4]{0:T(128)}, u32[]{:S(2)}) copy-start(s32[4]{0:T(128)} %listed_ref.5) | copy-start | bytes 52
  14.4 17.5 %collective-permute-start.4 = (bf16[640,512]{1,0:T(8,128)(2,1)S(1)}, bf16[640,512]{1,0:T(8,128)(2,1)S(1)}, u32[]{:S(2)}, u32[]{:S(2)}) collective-permute-start(bf16[640,512]{1,0:T(8,128)(2,1)S(1)} %pad_maximum_fusion), channel_id=1, source_target_pairs={{0,4},{4,0},{8,12},{12,8},{1,5},{5,1},{9,13},{13,9},{2,6},{6,2},{1... | collective-permute-start | bytes 1966088 | tf_op jit(solution)/shard_map/ppermute | solution.py:399
  14.4 17.5 %collective-permute-start.5 = (bf16[640,512]{1,0:T(8,128)(2,1)S(1)}, bf16[640,512]{1,0:T(8,128)(2,1)S(1)}, u32[]{:S(2)}, u32[]{:S(2)}) collective-permute-start(bf16[640,512]{1,0:T(8,128)(2,1)S(1)} %pad_maximum_fusion), channel_id=1, source_target_pairs={{4,8},{8,4},{5,9},{9,5},{6,10},{10,6},{7,11},{11,7},{20,24},{24,20... | collective-permute-start | bytes 1966088 | tf_op jit(solution)/shard_map/ppermute | solution.py:399
  17.6 5.6 %copy-start.10 = (f32[5120]{0:T(1024)S(1)}, f32[5120]{0:T(1024)}, u32[]{:S(2)}) copy-start(f32[5120]{0:T(1024)} %param.18) | copy-start | bytes 61444
  17.6 57.0 %copy-start.1 = (bf16[1,40,128,256]{3,2,1,0:T(8,128)(2,1)S(1)}, bf16[1,40,128,256]{3,2,1,0:T(8,128)(2,1)}, u32[]{:S(2)}) copy-start(bf16[1,40,128,256]{3,2,1,0:T(8,128)(2,1)} %param.25) | copy-start | bytes 7864324
  19.3 17.6 %collective-permute-start.9 = (bf16[2,18,2560]{2,1,0:T(8,128)(2,1)S(1)}, bf16[2,18,2560]{2,1,0:T(8,128)(2,1)S(1)}, u32[]{:S(2)}, u32[]{:S(2)}) collective-permute-start(bf16[2,18,2560]{2,1,0:T(8,128)(2,1)S(1)} %get-tuple-element.42), channel_id=1, source_target_pairs={{0,4},{4,0},{8,12},{12,8},{1,5},{5,1},{9,13},{13,9},{2,6},{6,2},{1... | collective-permute-start | bytes 552968 | tf_op jit(solution)/shard_map/ppermute | solution.py:50
  23.2 51.4 %copy-start = (bf16[1,40,128,256]{3,2,1,0:T(8,128)(2,1)S(1)}, bf16[1,40,128,256]{3,2,1,0:T(8,128)(2,1)}, u32[]{:S(2)}) copy-start(bf16[1,40,128,256]{3,2,1,0:T(8,128)(2,1)} %param.24) | copy-start | bytes 7864324
  23.2 51.4 %copy-start.11 = (s32[1,8,16]{2,1,0:T(8,128)S(1)}, s32[1,8,16]{2,1,0:T(8,128)}, u32[]{:S(2)}) copy-start(s32[1,8,16]{2,1,0:T(8,128)} %param.26) | copy-start | bytes 1540
  23.2 51.4 %copy-start.12 = (s32[4,8]{1,0:T(4,128)S(1)}, s32[4,8]{1,0:T(4,128)}, u32[]{:S(2)}) copy-start(s32[4,8]{1,0:T(4,128)} %lengths_ref.3) | copy-start | bytes 388
  23.3 51.4 %copy-start.14 = (f32[128]{0:T(128)S(1)}, f32[128]{0:T(128)}, u32[]{:S(2)}) copy-start(f32[128]{0:T(128)} %param.20) | copy-start | bytes 1540
  23.3 51.4 %copy-start.15 = (f32[128]{0:T(128)S(1)}, f32[128]{0:T(128)}, u32[]{:S(2)}) copy-start(f32[128]{0:T(128)} %param.19) | copy-start | bytes 1540
  23.3 51.4 %copy-start.16 = (f32[1,128]{1,0:T(1,128)S(1)}, f32[1,128]{1,0:T(1,128)}, u32[]{:S(2)}) copy-start(f32[1,128]{1,0:T(1,128)} %constant.20.clone.refs_3_) | copy-start | bytes 1540
  24.0 36.0 %collective-permute-start.3 = (bf16[8,128,640]{2,1,0:T(8,128)(2,1)S(1)}, bf16[8,128,640]{2,1,0:T(8,128)(2,1)S(1)}, u32[]{:S(2)}, u32[]{:S(2)}) collective-permute-start(bf16[8,128,640]{2,1,0:T(8,128)(2,1)S(1)} %shard_map.175.refs_0_), channel_id=1, source_target_pairs={{0,2},{2,0},{1,3},{3,1},{4,6},{6,4},{5,7},{7,5},{8,10},{10,8},{9,1... | collective-permute-start | bytes 3932168 | tf_op jit(solution)/shard_map/ppermute | solution.py:50
  31.9 23.3 %collective-permute-start.7 = (bf16[640,512]{1,0:T(8,128)(2,1)S(1)}, bf16[640,512]{1,0:T(8,128)(2,1)S(1)}, u32[]{:S(2)}, u32[]{:S(2)}) collective-permute-start(bf16[640,512]{1,0:T(8,128)(2,1)S(1)} %collective-permute-done.5.refs_8_), channel_id=1, source_target_pairs={{4,0},{8,12},{5,1},{9,13},{6,2},{10,14},{7,3},{11,15},{20,16},{24,... | collective-permute-start | bytes 1966088 | tf_op jit(solution)/shard_map/ppermute | solution.py:399
  33.2 22.0 %collective-permute-start.6 = (bf16[640,512]{1,0:T(8,128)(2,1)S(1)}, bf16[640,512]{1,0:T(8,128)(2,1)S(1)}, u32[]{:S(2)}, u32[]{:S(2)}) collective-permute-start(bf16[640,512]{1,0:T(8,128)(2,1)S(1)} %collective-permute-done.4.refs_6_), channel_id=1, source_target_pairs={{4,8},{8,4},{5,9},{9,5},{6,10},{10,6},{7,11},{11,7},{20,24},{24,20... | collective-permute-start | bytes 1966088 | tf_op jit(solution)/shard_map/ppermute | solution.py:399
  37.0 17.5 %collective-permute-start.10 = (bf16[18,2560]{1,0:T(8,128)(2,1)S(1)}, bf16[18,2560]{1,0:T(8,128)(2,1)S(1)}, u32[]{:S(2)}, u32[]{:S(2)}) collective-permute-start(bf16[18,2560]{1,0:T(8,128)(2,1)S(1)} %fusion), channel_id=1, source_target_pairs={{0,8},{4,12},{8,0},{12,4},{1,9},{5,13},{9,1},{13,5},{2,10},{6,14},... | collective-permute-start | bytes 276488 | tf_op jit(solution)/shard_map/ppermute | solution.py:50
  39.3 20.6 %collective-permute-start.12 = (bf16[640,512]{1,0:T(8,128)(2,1)S(1)}, bf16[640,512]{1,0:T(8,128)(2,1)S(1)}, u32[]{:S(2)}, u32[]{:S(2)}) collective-permute-start(bf16[640,512]{1,0:T(8,128)(2,1)S(1)} %collective-permute-done.4.refs_6_), channel_id=1, source_target_pairs={{0,16},{4,20},{8,24},{12,28},{16,0},{20,4},{24,8},{28,12},{1,17},{... | collective-permute-start | bytes 1966088 | tf_op jit(solution)/shard_map/ppermute | solution.py:405
  54.4 5.5 %collective-permute-start.13 = (bf16[640,512]{1,0:T(8,128)(2,1)S(1)}, bf16[640,512]{1,0:T(8,128)(2,1)S(1)}, u32[]{:S(2)}, u32[]{:S(2)}) collective-permute-start(bf16[640,512]{1,0:T(8,128)(2,1)S(1)} %collective-permute-done.5.refs_8_), channel_id=1, source_target_pairs={{4,20},{8,24},{20,4},{24,8},{5,21},{9,25},{21,5},{25,9},{6,22},{10... | collective-permute-start | bytes 1966088 | tf_op jit(solution)/shard_map/ppermute | solution.py:405
  55.2 14.0 %collective-permute-start.11 = (bf16[640,512]{1,0:T(8,128)(2,1)S(1)}, bf16[640,512]{1,0:T(8,128)(2,1)S(1)}, u32[]{:S(2)}, u32[]{:S(2)}) collective-permute-start(bf16[640,512]{1,0:T(8,128)(2,1)S(1)} %collective-permute-done.6.refs_4_), channel_id=1, source_target_pairs={{4,0},{8,12},{5,1},{9,13},{6,2},{10,14},{7,3},{11,15},{20,16},{24,... | collective-permute-start | bytes 1966088 | tf_op jit(solution)/shard_map/ppermute | solution.py:399
  56.5 14.0 %collective-permute-start.14 = (bf16[640,512]{1,0:T(8,128)(2,1)S(1)}, bf16[640,512]{1,0:T(8,128)(2,1)S(1)}, u32[]{:S(2)}, u32[]{:S(2)}) collective-permute-start(bf16[640,512]{1,0:T(8,128)(2,1)S(1)} %collective-permute-done.7.refs_9_), channel_id=1, source_target_pairs={{0,16},{12,28},{16,0},{28,12},{1,17},{13,29},{17,1},{29,13},{2,18}... | collective-permute-start | bytes 1966088 | tf_op jit(solution)/shard_map/ppermute | solution.py:405
  59.9 21.8 %collective-permute-start.8 = (bf16[8,128,640]{2,1,0:T(8,128)(2,1)S(1)}, bf16[8,128,640]{2,1,0:T(8,128)(2,1)S(1)}, u32[]{:S(2)}, u32[]{:S(2)}) collective-permute-start(bf16[8,128,640]{2,1,0:T(8,128)(2,1)S(1)} %shard_map.175.refs_0_), channel_id=1, source_target_pairs={{0,1},{1,0},{2,3},{3,2},{4,5},{5,4},{6,7},{7,6},{8,9},{9,8},{10,11... | collective-permute-start | bytes 3932168 | tf_op jit(solution)/shard_map/ppermute | solution.py:50
  70.5 11.3 %collective-permute-start.15 = (bf16[8,128,640]{2,1,0:T(8,128)(2,1)S(1)}, bf16[8,128,640]{2,1,0:T(8,128)(2,1)S(1)}, u32[]{:S(2)}, u32[]{:S(2)}) collective-permute-start(bf16[8,128,640]{2,1,0:T(8,128)(2,1)S(1)} %collective-permute-done.3.refs_1_), channel_id=1, source_target_pairs={{0,1},{1,0},{2,3},{3,2},{4,5},{5,4},{6,7},{7,6},{8,9},{9,8},{10,11... | collective-permute-start | bytes 3932168 | tf_op jit(solution)/shard_map/ppermute | solution.py:50
  70.5 19.0 %collective-permute-start.17 = (bf16[640,512]{1,0:T(8,128)(2,1)S(1)}, bf16[640,512]{1,0:T(8,128)(2,1)S(1)}, u32[]{:S(2)}, u32[]{:S(2)}) collective-permute-start(bf16[640,512]{1,0:T(8,128)(2,1)S(1)} %collective-permute-done.11.refs_6_.refs_7_), channel_id=1, source_target_pairs={{0,16},{12,28},{16,0},{28,12},{1,17},{13,29},{17,1},{29,13},{2,18}... | collective-permute-start | bytes 1966088 | tf_op jit(solution)/shard_map/ppermute | solution.py:405
  73.9 15.6 %collective-permute-start.16 = (bf16[640,512]{1,0:T(8,128)(2,1)S(1)}, bf16[640,512]{1,0:T(8,128)(2,1)S(1)}, u32[]{:S(2)}, u32[]{:S(2)}) collective-permute-start(bf16[640,512]{1,0:T(8,128)(2,1)S(1)} %collective-permute-done.6.refs_4_), channel_id=1, source_target_pairs={{4,20},{8,24},{20,4},{24,8},{5,21},{9,25},{21,5},{25,9},{6,22},{10... | collective-permute-start | bytes 1966088 | tf_op jit(solution)/shard_map/ppermute | solution.py:405
  80.3 9.2 %copy-start.6 = (f32[512,128]{1,0:T(8,128)S(1)}, f32[512,128]{1,0:T(8,128)}, u32[]{:S(2)}) copy-start(f32[512,128]{1,0:T(8,128)} %constant.18.clone.refs_11_) | copy-start | bytes 786436
  80.3 9.2 %copy-start.7 = (f32[512,128]{1,0:T(8,128)S(1)}, f32[512,128]{1,0:T(8,128)}, u32[]{:S(2)}) copy-start(f32[512,128]{1,0:T(8,128)} %constant.19.clone.refs_12_) | copy-start | bytes 786436
  80.3 4.2 %collective-permute-start.18 = (f32[2,32,128]{2,1,0:T(8,128)S(1)}, f32[2,32,128]{2,1,0:T(8,128)S(1)}, u32[]{:S(2)}, u32[]{:S(2)}) collective-permute-start(f32[2,32,128]{2,1,0:T(8,128)S(1)} %get-tuple-element.57), channel_id=1, source_target_pairs={{0,8},{4,12},{1,9},{5,13},{2,10},{6,14},{3,11},{7,15},{16,24},{20,... | collective-permute-start | bytes 98312 | tf_op jit(solution)/shard_map/ppermute | solution.py:515
  (4 other events, 9.8 us)

commit v4 on v3

--- a/solution.py
+++ b/solution.py
@@ -486,21 +486,21 @@
         s1 = xor_permute(spread[1], "rep", 1)
         s2 = xor_permute(spread[2], "rep", 2)
         s3 = xor_permute(spread[3], "rep", 3)
-        from_a = line_pairs([(0, 1), (1, 0), (2, 3), (3, 2)])(after(own, s1, s2, s3))
-        from_b = line_pairs([(1, 2), (2, 1)])(after(own, s1, s2, s3))
+        from_a = line_pairs([(0, 1), (1, 0), (2, 3), (3, 2)])(own)
+        from_b = line_pairs([(1, 2), (2, 1)])(own)
         across = xor_permute(after(blocks, s1, s2, s3), "tp", 1)
         own_sums, pair, far_sums = project_new(
             [spread[0], s1, s2, s3], listed_slot, w_query, w_key, w_value, steps
         )
-        from_d = line_pairs([(1, 2), (2, 1)])(after(from_a, from_b, far_sums))
-        from_c = line_pairs([(1, 0), (2, 3)])(after(from_b, from_a, far_sums))
+        from_d = line_pairs([(1, 2), (2, 1)])(after(from_a, from_b))
+        from_c = line_pairs([(1, 0), (2, 3)])(after(from_b, from_a))
         beside = xor_permute(after(blocks, from_d, from_c), "sub", 1)
+        over_a = across_groups(after(from_a, s1, s2, s3), range(4))
+        over_b = across_groups(after(from_b, from_d, from_c), (1, 2))
         over_c = across_groups(from_c, (0, 3))
         pair_in = xor_permute(pair, "rep", 1)
-        over_a = across_groups(after(from_a, pair_in), range(4))
-        over_b = across_groups(after(from_b, pair_in), (1, 2))
         r2 = xor_permute((far_sums + pair_in[1].astype(F32)).astype(BF16), "rep", 2)
-        from_e = line_pairs([(1, 0), (2, 3)])(after(from_d, from_c, r2))
+        from_e = line_pairs([(1, 0), (2, 3)])(after(from_d, from_c, pair_in))
         over_e = across_groups(after(from_e, across, over_a, over_b, over_c), (0, 3))
         over_d = across_groups(after(from_d, from_e, over_a, over_b, over_c), (1, 2))
         corner = xor_permute(after(across, from_e, over_a, over_b, over_c), "sub", 1)
@@ -511,8 +511,8 @@
             [],
             flops=3 * depth * tokens * width * 4,
         )
-        q3, k3, v3, moved = queries(own_sums, pair_in, r2)
-        returned = lax.ppermute(after(moved, from_e), "rep", [(i, i + half) for i in range(half)])
+        q3, k3, v3, moved = queries(after(own_sums, acc), pair_in, r2)
+        returned = lax.ppermute(moved, "rep", [(i, i + half) for i in range(half)])
         num, den, rows_last = attend(q3, k3, v3)
         far = [blocks, across, beside, corner, from_d, over_d, from_e, from_e, over_e, over_e]
     else:

time: 92.9 us -> 91.4 us (0.984)
  waiting for transfers between devices: 43.1 us -> 35.2 us
  starting transfers between devices: 28.7 us -> 33.2 us
  local copies, waits for them, and re-layouts: 5.41 us -> 7.21 us
    ppermute x5, waiting for transfers between devices: 6.29 us -> 2.02 us  [across_groups(): return lax.ppermute(value, ('groups', 'rep'), pairs)]
    ppermute x5, waiting for transfers between devices: 15.5 us -> 11.3 us  [line_pairs(): return lambda value: lax.ppermute(value, axis, pairs)]
    ppermute x5, starting transfers between devices: 3.97 us -> 7.05 us  [line_pairs(): return lambda value: lax.ppermute(value, axis, pairs)]
    unnamed x34 -> x38, local copies, waits for them, and re-layouts: 4.19 us -> 5.94 us
    ppermute x8, starting transfers between devices: 13.6 us -> 15.1 us  [xor_permute(): return lax.ppermute(value, axis, [(i, i ^ distance) for i in range(count)])]
  transfers between devices with their start and end apart: 19 -> 19, of which waited for: 8 -> 7; matrix products, arithmetic and copies ran while one was open for 1% -> 0% of each run, Pallas kernels for 12% -> 12%
where the time goes in v4:
time: 91.4 us; the launch traced here: 90.9 us
  waiting for transfers between devices  35.2 us (39%)
  starting transfers between devices  33.2 us (36%)
  Pallas kernels  14.2 us (16%)
  local copies, waits for them, and re-layouts  7.21 us (8%)
  between operations  0.96 us (1%)
    ppermute x8, waiting for transfers between devices, xor_permute(): return lax.ppermute(value, axis, [(i, i ^ distance) for i in range(count)])  21.9 us
    ppermute x8, starting transfers between devices, xor_permute(): return lax.ppermute(value, axis, [(i, i ^ distance) for i in range(count)])  15.1 us
    pallas_call x7, Pallas kernels, call(): pl.pallas_call(kernel, out_shape=tuple(outs), in_specs=[SCALAR] * len(sca...  14.2 us
    ppermute x5, waiting for transfers between devices, line_pairs(): return lambda value: lax.ppermute(value, axis, pairs)  11.3 us
    ppermute x5, starting transfers between devices, across_groups(): return lax.ppermute(value, ('groups', 'rep'), pairs)  9.77 us
    ppermute x5, starting transfers between devices, line_pairs(): return lambda value: lax.ppermute(value, axis, pairs)  7.05 us
    unnamed x38, local copies, waits for them, and re-layouts  5.94 us
    ppermute x5, waiting for transfers between devices, across_groups(): return lax.ppermute(value, ('groups', 'rep'), pairs)  2.02 us
  transfers between devices with their start and end apart: 19, of which 7 were waited for; matrix products, arithmetic and copies ran while one was open for 0% of the time, Pallas kernels for 12%

profile of v4, /device:TPU:0, one launch (start us, length us, event | category | flops | bytes accessed | tf_op | source)
XLA Modules:
  0.0 90.9 jit_solution(13049444828381212606)
XLA Ops:
  0.6 1.3 %constant_dynamic-slice_fusion = (bf16[640,256]{1,0:T(8,128)(2,1)S(1)}, bf16[640,256]{1,0:T(8,128)(2,1)S(1)}) fusion(bf16[1280,256]{1,0:T(8,128)(2,1)} %refs_5_.3, s32[]{:T(128)S(6)} %select_n.4, bf16[1280,256]{1,0:T(8,128)(2,1)} %refs_4_.3), kind=kLoop, calls=%fused_computation.4 | loop fusion | bytes 1310724 | tf_op jit(solution)/shard_map/dynamic_slice | solution.py:475
  2.0 3.1 %collective-permute-start.4 = (bf16[640,512]{1,0:T(8,128)(2,1)S(1)}, bf16[640,512]{1,0:T(8,128)(2,1)S(1)}, u32[]{:S(2)}, u32[]{:S(2)}) collective-permute-start(bf16[640,512]{1,0:T(8,128)(2,1)S(1)} %pad_maximum_fusion), channel_id=1, source_target_pairs={{0,4},{4,0},{8,12},{12,8},{1,5},{5,1},{9,13},{13,9},{2,6},{6,2},{1... | collective-permute-start | bytes 1966088 | tf_op jit(solution)/shard_map/ppermute | solution.py:399
  5.8 0.9 %copy-done.10 = bf16[1,9,2,5120]{3,2,1,0:T(2,128)(2,1)S(1)} copy-done((bf16[1,9,2,5120]{3,2,1,0:T(2,128)(2,1)S(1)}, bf16[1,9,2,5120]{3,2,1,0:T(2,128)(2,1)}, u32[]{:S(2)}) %copy-start.10) | copy-done | bytes 184344
  6.7 0.7 copy-done.11
  7.8 4.4 %collective-permute-start = (bf16[18,1280]{1,0:T(8,128)(2,1)S(1)}, bf16[18,1280]{1,0:T(8,128)(2,1)S(1)}, u32[]{:S(2)}, u32[]{:S(2)}) collective-permute-start(bf16[18,1280]{1,0:T(8,128)(2,1)S(1)} %get-tuple-element.31), channel_id=1, source_target_pairs={{0,4},{4,0},{8,12},{12,8},{1,5},{5,1},{9,13},{13,9},{2,6},{6,2},{1... | collective-permute-start | bytes 138248 | tf_op jit(solution)/shard_map/ppermute | solution.py:50
  12.2 2.4 %collective-permute-start.2 = (bf16[18,1280]{1,0:T(8,128)(2,1)S(1)}, bf16[18,1280]{1,0:T(8,128)(2,1)S(1)}, u32[]{:S(2)}, u32[]{:S(2)}) collective-permute-start(bf16[18,1280]{1,0:T(8,128)(2,1)S(1)} %get-tuple-element.33), channel_id=1, source_target_pairs={{0,12},{4,8},{8,4},{12,0},{1,13},{5,9},{9,5},{13,1},{2,14},{6,10},... | collective-permute-start | bytes 138248 | tf_op jit(solution)/shard_map/ppermute | solution.py:50
  14.7 1.3 %copy-done.7 = bf16[1,128,5120]{2,1,0:T(8,128)(2,1)S(1)} copy-done((bf16[1,128,5120]{2,1,0:T(8,128)(2,1)S(1)}, bf16[1,128,5120]{2,1,0:T(8,128)(2,1)}, u32[]{:S(2)}) %copy-start.7) | copy-done | bytes 1310744
  16.0 0.7 copy-done.12
  16.7 0.7 shard_map.175.refs_0_
  17.4 3.0 %collective-permute-done.4.refs_6_ = bf16[640,512]{1,0:T(8,128)(2,1)S(1)} collective-permute-done((bf16[640,512]{1,0:T(8,128)(2,1)S(1)}, bf16[640,512]{1,0:T(8,128)(2,1)S(1)}, u32[]{:S(2)}, u32[]{:S(2)}) %collective-permute-start.4) | collective-permute-done | bytes 655392 | tf_op jit(solution)/shard_map/ppermute | solution.py:399
  21.2 1.3 %collective-permute-start.7 = (bf16[640,512]{1,0:T(8,128)(2,1)S(1)}, bf16[640,512]{1,0:T(8,128)(2,1)S(1)}, u32[]{:S(2)}, u32[]{:S(2)}) collective-permute-start(bf16[640,512]{1,0:T(8,128)(2,1)S(1)} %collective-permute-done.5.refs_8_), channel_id=1, source_target_pairs={{4,0},{8,12},{5,1},{9,13},{6,2},{10,14},{7,3},{11,15},{20,16},{24,... | collective-permute-start | bytes 1966088 | tf_op jit(solution)/shard_map/ppermute | solution.py:399
  22.5 6.1 %collective-permute-done.1.refs_2_ = bf16[18,1280]{1,0:T(8,128)(2,1)S(1)} collective-permute-done((bf16[18,1280]{1,0:T(8,128)(2,1)S(1)}, bf16[18,1280]{1,0:T(8,128)(2,1)S(1)}, u32[]{:S(2)}, u32[]{:S(2)}) %collective-permute-start.1) | collective-permute-done | bytes 46112 | tf_op jit(solution)/shard_map/ppermute | solution.py:50
  28.6 1.5 %collective-permute-start.3 = (bf16[8,128,640]{2,1,0:T(8,128)(2,1)S(1)}, bf16[8,128,640]{2,1,0:T(8,128)(2,1)S(1)}, u32[]{:S(2)}, u32[]{:S(2)}) collective-permute-start(bf16[8,128,640]{2,1,0:T(8,128)(2,1)S(1)} %shard_map.175.refs_0_), channel_id=1, source_target_pairs={{0,2},{2,0},{1,3},{3,1},{4,6},{6,4},{5,7},{7,5},{8,10},{10,8},{9,1... | collective-permute-start | bytes 3932168 | tf_op jit(solution)/shard_map/ppermute | solution.py:50
  30.1 1.1 %copy-done.3 = bf16[1280,256]{1,0:T(8,128)(2,1)S(1)} copy-done((bf16[1280,256]{1,0:T(8,128)(2,1)S(1)}, bf16[1280,256]{1,0:T(8,128)(2,1)}, u32[]{:S(2)}) %copy-start.3) | copy-done | bytes 655384
  31.2 1.1 %copy-done.5 = bf16[1280,256]{1,0:T(8,128)(2,1)S(1)} copy-done((bf16[1280,256]{1,0:T(8,128)(2,1)S(1)}, bf16[1280,256]{1,0:T(8,128)(2,1)}, u32[]{:S(2)}) %copy-start.5) | copy-done | bytes 655384
  32.3 1.7 %shard_map.177 = (f32[18,2560]{1,0:T(8,128)S(1)}, bf16[2,18,2560]{2,1,0:T(8,128)(2,1)S(1)}, f32[18,2560]{1,0:T(8,128)S(1)}) custom-call(s32[4]{0:T(128)S(1)} %copy-done.15, bf16[18,1280]{1,0:T(8,128)(2,1)S(1)} %get-tuple-element.38.refs_0_, bf16[18,1280]{1,0:T(8,128)(2,1)S(1)} %collective-permute-done.refs_1_, ...), custom_call_target="tpu_custom_call" | custom-call | flops 471859200 | bytes 7290880 | tf_op jit(solution)/shard_map/pallas_call | solution.py:25
  34.0 5.0 %collective-permute-start.9 = (bf16[2,18,2560]{2,1,0:T(8,128)(2,1)S(1)}, bf16[2,18,2560]{2,1,0:T(8,128)(2,1)S(1)}, u32[]{:S(2)}, u32[]{:S(2)}) collective-permute-start(bf16[2,18,2560]{2,1,0:T(8,128)(2,1)S(1)} %get-tuple-element.39), channel_id=1, source_target_pairs={{0,4},{4,0},{8,12},{12,8},{1,5},{5,1},{9,13},{13,9},{2,6},{6,2},{1... | collective-permute-start | bytes 552968 | tf_op jit(solution)/shard_map/ppermute | solution.py:50
  39.0 1.5 %collective-permute-start.11 = (bf16[640,512]{1,0:T(8,128)(2,1)S(1)}, bf16[640,512]{1,0:T(8,128)(2,1)S(1)}, u32[]{:S(2)}, u32[]{:S(2)}) collective-permute-start(bf16[640,512]{1,0:T(8,128)(2,1)S(1)} %collective-permute-done.4.refs_6_), channel_id=1, source_target_pairs={{0,16},{4,20},{8,24},{12,28},{16,0},{20,4},{24,8},{28,12},{1,17},{... | collective-permute-start | bytes 1966088 | tf_op jit(solution)/shard_map/ppermute | solution.py:405
  40.6 10.1 %collective-permute-done.9.refs_1_ = bf16[2,18,2560]{2,1,0:T(8,128)(2,1)S(1)} collective-permute-done((bf16[2,18,2560]{2,1,0:T(8,128)(2,1)S(1)}, bf16[2,18,2560]{2,1,0:T(8,128)(2,1)S(1)}, u32[]{:S(2)}, u32[]{:S(2)}) %collective-permute-start.9) | collective-permute-done | bytes 184352 | tf_op jit(solution)/shard_map/ppermute | solution.py:50
  50.6 1.3 %collective-permute-start.10 = (bf16[640,512]{1,0:T(8,128)(2,1)S(1)}, bf16[640,512]{1,0:T(8,128)(2,1)S(1)}, u32[]{:S(2)}, u32[]{:S(2)}) collective-permute-start(bf16[640,512]{1,0:T(8,128)(2,1)S(1)} %collective-permute-done.6.refs_4_), channel_id=1, source_target_pairs={{4,0},{8,12},{5,1},{9,13},{6,2},{10,14},{7,3},{11,15},{20,16},{24,... | collective-permute-start | bytes 1966088 | tf_op jit(solution)/shard_map/ppermute | solution.py:399
  52.6 3.4 %collective-permute-start.13 = (bf16[640,512]{1,0:T(8,128)(2,1)S(1)}, bf16[640,512]{1,0:T(8,128)(2,1)S(1)}, u32[]{:S(2)}, u32[]{:S(2)}) collective-permute-start(bf16[640,512]{1,0:T(8,128)(2,1)S(1)} %collective-permute-done.7.refs_9_), channel_id=1, source_target_pairs={{0,16},{12,28},{16,0},{28,12},{1,17},{13,29},{17,1},{29,13},{2,18}... | collective-permute-start | bytes 1966088 | tf_op jit(solution)/shard_map/ppermute | solution.py:405
  56.2 1.1 %collective-permute-done.3.refs_1_ = bf16[8,128,640]{2,1,0:T(8,128)(2,1)S(1)} collective-permute-done((bf16[8,128,640]{2,1,0:T(8,128)(2,1)S(1)}, bf16[8,128,640]{2,1,0:T(8,128)(2,1)S(1)}, u32[]{:S(2)}, u32[]{:S(2)}) %collective-permute-start.3) | collective-permute-done | bytes 1310752 | tf_op jit(solution)/shard_map/ppermute | solution.py:50
  57.3 8.3 %collective-permute-done.10.refs_6_.refs_7_ = bf16[640,512]{1,0:T(8,128)(2,1)S(1)} collective-permute-done((bf16[640,512]{1,0:T(8,128)(2,1)S(1)}, bf16[640,512]{1,0:T(8,128)(2,1)S(1)}, u32[]{:S(2)}, u32[]{:S(2)}) %collective-permute-start.10) | collective-permute-done | bytes 655392 | tf_op jit(solution)/shard_map/ppermute | solution.py:399
  65.6 2.0 %collective-permute-done.13.refs_11_ = bf16[640,512]{1,0:T(8,128)(2,1)S(1)} collective-permute-done((bf16[640,512]{1,0:T(8,128)(2,1)S(1)}, bf16[640,512]{1,0:T(8,128)(2,1)S(1)}, u32[]{:S(2)}, u32[]{:S(2)}) %collective-permute-start.13) | collective-permute-done | bytes 655392 | tf_op jit(solution)/shard_map/ppermute | solution.py:405
  67.6 3.4 %collective-permute-start.16 = (bf16[640,512]{1,0:T(8,128)(2,1)S(1)}, bf16[640,512]{1,0:T(8,128)(2,1)S(1)}, u32[]{:S(2)}, u32[]{:S(2)}) collective-permute-start(bf16[640,512]{1,0:T(8,128)(2,1)S(1)} %collective-permute-done.10.refs_6_.refs_7_), channel_id=1, source_target_pairs={{0,16},{12,28},{16,0},{28,12},{1,17},{13,29},{17,1},{29,13},{2,18}... | collective-permute-start | bytes 1966088 | tf_op jit(solution)/shard_map/ppermute | solution.py:405
  71.8 1.7 %collective-permute-start.17 = (bf16[18,2560]{1,0:T(8,128)(2,1)S(1)}, bf16[18,2560]{1,0:T(8,128)(2,1)S(1)}, u32[]{:S(2)}, u32[]{:S(2)}) collective-permute-start(bf16[18,2560]{1,0:T(8,128)(2,1)S(1)} %fusion), channel_id=1, source_target_pairs={{0,8},{4,12},{8,0},{12,4},{1,9},{5,13},{9,1},{13,5},{2,10},{6,14},... | collective-permute-start | bytes 276488 | tf_op jit(solution)/shard_map/ppermute | solution.py:50
  73.5 2.8 %shard_map.178.refs_10_ = f32[512,512]{1,0:T(8,128)S(1)} custom-call(bf16[8,128,640]{2,1,0:T(8,128)(2,1)S(1)} %shard_map.175.refs_0_, bf16[8,128,640]{2,1,0:T(8,128)(2,1)S(1)} %collective-permute-done.3.refs_1_, bf16[8,128,640]{2,1,0:T(8,128)(2,1)S(1)} %collective-permute-done.8.refs_2_, bf16[8,128,640]{2,1,0:T(8,128)(2,1)S(1)} %collective-permute-done.14.refs_3_, ...), custom_call_target="tpu_custom_call" | custom-call | flops 2013265920 | bytes 11534336 | tf_op jit(solution)/shard_map/pallas_call | solution.py:25
  76.3 4.6 %collective-permute-done.17.refs_2_ = bf16[18,2560]{1,0:T(8,128)(2,1)S(1)} collective-permute-done((bf16[18,2560]{1,0:T(8,128)(2,1)S(1)}, bf16[18,2560]{1,0:T(8,128)(2,1)S(1)}, u32[]{:S(2)}, u32[]{:S(2)}) %collective-permute-start.17) | collective-permute-done | bytes 92192 | tf_op jit(solution)/shard_map/ppermute | solution.py:50
  80.9 3.0 %shard_map.179 = (f32[18,16,128]{2,1,0:T(8,128)S(1)}, f32[18,16,128]{2,1,0:T(8,128)S(1)}, f32[18,16,128]{2,1,0:T(8,128)S(1)}, f32[2,32,128]{2,1,0:T(8,128)S(1)}) custom-call(s32[8,16]{1,0:T(8,128)S(1)} %bitcast.24, s32[4,8]{1,0:T(4,128)S(1)} %copy-done.14, s32[4]{0:T(128)S(1)} %copy-done.15, f32[18,2560]{1,0:T(8,128)S(1)} %get-tuple-element.47.refs_0_, ...), custom_call_target="tpu_custom_call" | custom-call | bytes 6180352 | tf_op jit(solution)/shard_map/pallas_call | solution.py:25
  83.9 1.3 %collective-permute-start.18 = (f32[2,32,128]{2,1,0:T(8,128)S(1)}, f32[2,32,128]{2,1,0:T(8,128)S(1)}, u32[]{:S(2)}, u32[]{:S(2)}) collective-permute-start(f32[2,32,128]{2,1,0:T(8,128)S(1)} %get-tuple-element.55), channel_id=1, source_target_pairs={{0,8},{4,12},{1,9},{5,13},{2,10},{6,14},{3,11},{7,15},{16,24},{20,... | collective-permute-start | bytes 98312 | tf_op jit(solution)/shard_map/ppermute | solution.py:515
  85.2 2.6 %shard_map.180 = (f32[18,16,128]{2,1,0:T(8,128)S(1)}, f32[18,16,128]{2,1,0:T(8,128)S(1)}, bf16[32,256]{1,0:T(8,128)(2,1)S(1)}) custom-call(s32[8,16]{1,0:T(8,128)S(1)} %bitcast.25, s32[4,8]{1,0:T(4,128)S(1)} %copy-done.14, f32[18,16,128]{2,1,0:T(8,128)S(1)} %get-tuple-element.49.refs_0_, f32[18,16,128]{2,1,0:T(8,128)S(1)} %get-tuple-element.50.refs_1_, ...), custom_call_target="tpu_custom_call" | custom-call | bytes 5996544 | tf_op jit(solution)/shard_map/pallas_call | solution.py:25
  87.9 3.0 %shard_map.181 = (bf16[512,256]{1,0:T(8,128)(2,1)}, bf16[512,256]{1,0:T(8,128)(2,1)}, bf16[9,2,2048]{2,1,0:T(2,128)(2,1)}) custom-call(s32[4]{0:T(128)S(1)} %copy-done.15, bf16[8,128,640]{2,1,0:T(8,128)(2,1)S(1)} %shard_map.175.refs_0_, bf16[8,128,640]{2,1,0:T(8,128)(2,1)S(1)} %collective-permute-done.3.refs_1_, ...), custom_call_target="tpu_custom_call" | custom-call | flops 671088640 | bytes 11690496 | tf_op jit(solution)/shard_map/pallas_call | solution.py:25
  (54 shorter events, 3.4 us)
Async XLA Ops:
  0.6 29.5 %copy-start.2 = (bf16[1280,2048]{1,0:T(8,128)(2,1)S(1)}, bf16[1280,2048]{1,0:T(8,128)(2,1)}, u32[]{:S(2)}) copy-start(bf16[1280,2048]{1,0:T(8,128)(2,1)} %refs_4_.2) | copy-start | bytes 15728644
  2.0 18.5 %collective-permute-start.4 = (bf16[640,512]{1,0:T(8,128)(2,1)S(1)}, bf16[640,512]{1,0:T(8,128)(2,1)S(1)}, u32[]{:S(2)}, u32[]{:S(2)}) collective-permute-start(bf16[640,512]{1,0:T(8,128)(2,1)S(1)} %pad_maximum_fusion), channel_id=1, source_target_pairs={{0,4},{4,0},{8,12},{12,8},{1,5},{5,1},{9,13},{13,9},{2,6},{6,2},{1... | collective-permute-start | bytes 1966088 | tf_op jit(solution)/shard_map/ppermute | solution.py:399
  5.1 15.4 %collective-permute-start.5 = (bf16[640,512]{1,0:T(8,128)(2,1)S(1)}, bf16[640,512]{1,0:T(8,128)(2,1)S(1)}, u32[]{:S(2)}, u32[]{:S(2)}) collective-permute-start(bf16[640,512]{1,0:T(8,128)(2,1)S(1)} %pad_maximum_fusion), channel_id=1, source_target_pairs={{4,8},{8,4},{5,9},{9,5},{6,10},{10,6},{7,11},{11,7},{20,24},{24,20... | collective-permute-start | bytes 1966088 | tf_op jit(solution)/shard_map/ppermute | solution.py:399
  7.8 14.7 %collective-permute-start = (bf16[18,1280]{1,0:T(8,128)(2,1)S(1)}, bf16[18,1280]{1,0:T(8,128)(2,1)S(1)}, u32[]{:S(2)}, u32[]{:S(2)}) collective-permute-start(bf16[18,1280]{1,0:T(8,128)(2,1)S(1)} %get-tuple-element.31), channel_id=1, source_target_pairs={{0,4},{4,0},{8,12},{12,8},{1,5},{5,1},{9,13},{13,9},{2,6},{6,2},{1... | collective-permute-start | bytes 138248 | tf_op jit(solution)/shard_map/ppermute | solution.py:50
  12.2 16.4 %collective-permute-start.1 = (bf16[18,1280]{1,0:T(8,128)(2,1)S(1)}, bf16[18,1280]{1,0:T(8,128)(2,1)S(1)}, u32[]{:S(2)}, u32[]{:S(2)}) collective-permute-start(bf16[18,1280]{1,0:T(8,128)(2,1)S(1)} %get-tuple-element.32), channel_id=1, source_target_pairs={{0,8},{4,12},{8,0},{12,4},{1,9},{5,13},{9,1},{13,5},{2,10},{6,14},... | collective-permute-start | bytes 138248 | tf_op jit(solution)/shard_map/ppermute | solution.py:50
  12.2 16.4 %collective-permute-start.2 = (bf16[18,1280]{1,0:T(8,128)(2,1)S(1)}, bf16[18,1280]{1,0:T(8,128)(2,1)S(1)}, u32[]{:S(2)}, u32[]{:S(2)}) collective-permute-start(bf16[18,1280]{1,0:T(8,128)(2,1)S(1)} %get-tuple-element.33), channel_id=1, source_target_pairs={{0,12},{4,8},{8,4},{12,0},{1,13},{5,9},{9,5},{13,1},{2,14},{6,10},... | collective-permute-start | bytes 138248 | tf_op jit(solution)/shard_map/ppermute | solution.py:50
  16.7 13.4 %copy-start.15 = (s32[4]{0:T(128)S(1)}, s32[4]{0:T(128)}, u32[]{:S(2)}) copy-start(s32[4]{0:T(128)} %listed_ref.5) | copy-start | bytes 52
  20.5 30.2 %collective-permute-start.6 = (bf16[640,512]{1,0:T(8,128)(2,1)S(1)}, bf16[640,512]{1,0:T(8,128)(2,1)S(1)}, u32[]{:S(2)}, u32[]{:S(2)}) collective-permute-start(bf16[640,512]{1,0:T(8,128)(2,1)S(1)} %collective-permute-done.4.refs_6_), channel_id=1, source_target_pairs={{4,8},{8,4},{5,9},{9,5},{6,10},{10,6},{7,11},{11,7},{20,24},{24,20... | collective-permute-start | bytes 1966088 | tf_op jit(solution)/shard_map/ppermute | solution.py:399
  21.2 29.5 %collective-permute-start.7 = (bf16[640,512]{1,0:T(8,128)(2,1)S(1)}, bf16[640,512]{1,0:T(8,128)(2,1)S(1)}, u32[]{:S(2)}, u32[]{:S(2)}) collective-permute-start(bf16[640,512]{1,0:T(8,128)(2,1)S(1)} %collective-permute-done.5.refs_8_), channel_id=1, source_target_pairs={{4,0},{8,12},{5,1},{9,13},{6,2},{10,14},{7,3},{11,15},{20,16},{24,... | collective-permute-start | bytes 1966088 | tf_op jit(solution)/shard_map/ppermute | solution.py:399
  28.6 28.7 %collective-permute-start.3 = (bf16[8,128,640]{2,1,0:T(8,128)(2,1)S(1)}, bf16[8,128,640]{2,1,0:T(8,128)(2,1)S(1)}, u32[]{:S(2)}, u32[]{:S(2)}) collective-permute-start(bf16[8,128,640]{2,1,0:T(8,128)(2,1)S(1)} %shard_map.175.refs_0_), channel_id=1, source_target_pairs={{0,2},{2,0},{1,3},{3,1},{4,6},{6,4},{5,7},{7,5},{8,10},{10,8},{9,1... | collective-permute-start | bytes 3932168 | tf_op jit(solution)/shard_map/ppermute | solution.py:50
  32.3 41.2 %copy-start.4 = (bf16[1280,256]{1,0:T(8,128)(2,1)S(1)}, bf16[1280,256]{1,0:T(8,128)(2,1)}, u32[]{:S(2)}) copy-start(bf16[1280,256]{1,0:T(8,128)(2,1)} %refs_5_.3) | copy-start | bytes 1966084
  32.3 41.2 %copy-start.6 = (bf16[1280,256]{1,0:T(8,128)(2,1)S(1)}, bf16[1280,256]{1,0:T(8,128)(2,1)}, u32[]{:S(2)}) copy-start(bf16[1280,256]{1,0:T(8,128)(2,1)} %refs_4_.3) | copy-start | bytes 1966084
  34.0 16.6 %collective-permute-start.9 = (bf16[2,18,2560]{2,1,0:T(8,128)(2,1)S(1)}, bf16[2,18,2560]{2,1,0:T(8,128)(2,1)S(1)}, u32[]{:S(2)}, u32[]{:S(2)}) collective-permute-start(bf16[2,18,2560]{2,1,0:T(8,128)(2,1)S(1)} %get-tuple-element.39), channel_id=1, source_target_pairs={{0,4},{4,0},{8,12},{12,8},{1,5},{5,1},{9,13},{13,9},{2,6},{6,2},{1... | collective-permute-start | bytes 552968 | tf_op jit(solution)/shard_map/ppermute | solution.py:50
  39.0 17.0 %collective-permute-start.11 = (bf16[640,512]{1,0:T(8,128)(2,1)S(1)}, bf16[640,512]{1,0:T(8,128)(2,1)S(1)}, u32[]{:S(2)}, u32[]{:S(2)}) collective-permute-start(bf16[640,512]{1,0:T(8,128)(2,1)S(1)} %collective-permute-done.4.refs_6_), channel_id=1, source_target_pairs={{0,16},{4,20},{8,24},{12,28},{16,0},{20,4},{24,8},{28,12},{1,17},{... | collective-permute-start | bytes 1966088 | tf_op jit(solution)/shard_map/ppermute | solution.py:405
  50.6 14.9 %collective-permute-start.10 = (bf16[640,512]{1,0:T(8,128)(2,1)S(1)}, bf16[640,512]{1,0:T(8,128)(2,1)S(1)}, u32[]{:S(2)}, u32[]{:S(2)}) collective-permute-start(bf16[640,512]{1,0:T(8,128)(2,1)S(1)} %collective-permute-done.6.refs_4_), channel_id=1, source_target_pairs={{4,0},{8,12},{5,1},{9,13},{6,2},{10,14},{7,3},{11,15},{20,16},{24,... | collective-permute-start | bytes 1966088 | tf_op jit(solution)/shard_map/ppermute | solution.py:399
  51.9 13.6 %collective-permute-start.12 = (bf16[640,512]{1,0:T(8,128)(2,1)S(1)}, bf16[640,512]{1,0:T(8,128)(2,1)S(1)}, u32[]{:S(2)}, u32[]{:S(2)}) collective-permute-start(bf16[640,512]{1,0:T(8,128)(2,1)S(1)} %collective-permute-done.5.refs_8_), channel_id=1, source_target_pairs={{4,20},{8,24},{20,4},{24,8},{5,21},{9,25},{21,5},{25,9},{6,22},{10... | collective-permute-start | bytes 1966088 | tf_op jit(solution)/shard_map/ppermute | solution.py:405
  52.6 14.9 %collective-permute-start.13 = (bf16[640,512]{1,0:T(8,128)(2,1)S(1)}, bf16[640,512]{1,0:T(8,128)(2,1)S(1)}, u32[]{:S(2)}, u32[]{:S(2)}) collective-permute-start(bf16[640,512]{1,0:T(8,128)(2,1)S(1)} %collective-permute-done.7.refs_9_), channel_id=1, source_target_pairs={{0,16},{12,28},{16,0},{28,12},{1,17},{13,29},{17,1},{29,13},{2,18}... | collective-permute-start | bytes 1966088 | tf_op jit(solution)/shard_map/ppermute | solution.py:405
  56.1 17.4 %collective-permute-start.8 = (bf16[8,128,640]{2,1,0:T(8,128)(2,1)S(1)}, bf16[8,128,640]{2,1,0:T(8,128)(2,1)S(1)}, u32[]{:S(2)}, u32[]{:S(2)}) collective-permute-start(bf16[8,128,640]{2,1,0:T(8,128)(2,1)S(1)} %shard_map.175.refs_0_), channel_id=1, source_target_pairs={{0,1},{1,0},{2,3},{3,2},{4,5},{5,4},{6,7},{7,6},{8,9},{9,8},{10,11... | collective-permute-start | bytes 3932168 | tf_op jit(solution)/shard_map/ppermute | solution.py:50
  67.6 5.9 %collective-permute-start.14 = (bf16[8,128,640]{2,1,0:T(8,128)(2,1)S(1)}, bf16[8,128,640]{2,1,0:T(8,128)(2,1)S(1)}, u32[]{:S(2)}, u32[]{:S(2)}) collective-permute-start(bf16[8,128,640]{2,1,0:T(8,128)(2,1)S(1)} %collective-permute-done.3.refs_1_), channel_id=1, source_target_pairs={{0,1},{1,0},{2,3},{3,2},{4,5},{5,4},{6,7},{7,6},{8,9},{9,8},{10,11... | collective-permute-start | bytes 3932168 | tf_op jit(solution)/shard_map/ppermute | solution.py:50
  67.6 20.2 %collective-permute-start.16 = (bf16[640,512]{1,0:T(8,128)(2,1)S(1)}, bf16[640,512]{1,0:T(8,128)(2,1)S(1)}, u32[]{:S(2)}, u32[]{:S(2)}) collective-permute-start(bf16[640,512]{1,0:T(8,128)(2,1)S(1)} %collective-permute-done.10.refs_6_.refs_7_), channel_id=1, source_target_pairs={{0,16},{12,28},{16,0},{28,12},{1,17},{13,29},{17,1},{29,13},{2,18}... | collective-permute-start | bytes 1966088 | tf_op jit(solution)/shard_map/ppermute | solution.py:405
  71.0 16.8 %collective-permute-start.15 = (bf16[640,512]{1,0:T(8,128)(2,1)S(1)}, bf16[640,512]{1,0:T(8,128)(2,1)S(1)}, u32[]{:S(2)}, u32[]{:S(2)}) collective-permute-start(bf16[640,512]{1,0:T(8,128)(2,1)S(1)} %collective-permute-done.6.refs_4_), channel_id=1, source_target_pairs={{4,20},{8,24},{20,4},{24,8},{5,21},{9,25},{21,5},{25,9},{6,22},{10... | collective-permute-start | bytes 1966088 | tf_op jit(solution)/shard_map/ppermute | solution.py:405
  71.7 9.1 %copy-start.13 = (s32[1,8,16]{2,1,0:T(8,128)S(1)}, s32[1,8,16]{2,1,0:T(8,128)}, u32[]{:S(2)}) copy-start(s32[1,8,16]{2,1,0:T(8,128)} %param.26) | copy-start | bytes 1540
  71.8 9.1 %copy-start.14 = (s32[4,8]{1,0:T(4,128)S(1)}, s32[4,8]{1,0:T(4,128)}, u32[]{:S(2)}) copy-start(s32[4,8]{1,0:T(4,128)} %lengths_ref.3) | copy-start | bytes 388
  71.8 9.1 %copy-start.16 = (f32[128]{0:T(128)S(1)}, f32[128]{0:T(128)}, u32[]{:S(2)}) copy-start(f32[128]{0:T(128)} %param.20) | copy-start | bytes 1540
  71.8 9.1 %copy-start.17 = (f32[128]{0:T(128)S(1)}, f32[128]{0:T(128)}, u32[]{:S(2)}) copy-start(f32[128]{0:T(128)} %param.19) | copy-start | bytes 1540
  71.8 9.1 %copy-start.18 = (f32[1,128]{1,0:T(1,128)S(1)}, f32[1,128]{1,0:T(1,128)}, u32[]{:S(2)}) copy-start(f32[1,128]{1,0:T(1,128)} %constant.20.clone.refs_3_) | copy-start | bytes 1540
  71.8 9.1 %collective-permute-start.17 = (bf16[18,2560]{1,0:T(8,128)(2,1)S(1)}, bf16[18,2560]{1,0:T(8,128)(2,1)S(1)}, u32[]{:S(2)}, u32[]{:S(2)}) collective-permute-start(bf16[18,2560]{1,0:T(8,128)(2,1)S(1)} %fusion), channel_id=1, source_target_pairs={{0,8},{4,12},{8,0},{12,4},{1,9},{5,13},{9,1},{13,5},{2,10},{6,14},... | collective-permute-start | bytes 276488 | tf_op jit(solution)/shard_map/ppermute | solution.py:50
  73.5 7.4 %copy-start = (bf16[1,40,128,256]{3,2,1,0:T(8,128)(2,1)S(1)}, bf16[1,40,128,256]{3,2,1,0:T(8,128)(2,1)}, u32[]{:S(2)}) copy-start(bf16[1,40,128,256]{3,2,1,0:T(8,128)(2,1)} %param.24) | copy-start | bytes 7864324
  73.5 7.4 %copy-start.1 = (bf16[1,40,128,256]{3,2,1,0:T(8,128)(2,1)S(1)}, bf16[1,40,128,256]{3,2,1,0:T(8,128)(2,1)}, u32[]{:S(2)}) copy-start(bf16[1,40,128,256]{3,2,1,0:T(8,128)(2,1)} %param.25) | copy-start | bytes 7864324
  83.9 3.9 %collective-permute-start.18 = (f32[2,32,128]{2,1,0:T(8,128)S(1)}, f32[2,32,128]{2,1,0:T(8,128)S(1)}, u32[]{:S(2)}, u32[]{:S(2)}) collective-permute-start(f32[2,32,128]{2,1,0:T(8,128)S(1)} %get-tuple-element.55), channel_id=1, source_target_pairs={{0,8},{4,12},{1,9},{5,13},{2,10},{6,14},{3,11},{7,15},{16,24},{20,... | collective-permute-start | bytes 98312 | tf_op jit(solution)/shard_map/ppermute | solution.py:515
  85.2 2.7 %copy-start.8 = (f32[512,128]{1,0:T(8,128)S(1)}, f32[512,128]{1,0:T(8,128)}, u32[]{:S(2)}) copy-start(f32[512,128]{1,0:T(8,128)} %constant.18.clone.refs_11_) | copy-start | bytes 786436
  85.2 2.7 %copy-start.9 = (f32[512,128]{1,0:T(8,128)S(1)}, f32[512,128]{1,0:T(8,128)}, u32[]{:S(2)}) copy-start(f32[512,128]{1,0:T(8,128)} %constant.19.clone.refs_12_) | copy-start | bytes 786436
  (6 other events, 5.9 us)

commit v5 on v4

--- a/solution.py
+++ b/solution.py
@@ -295,7 +295,7 @@
 
 def first_kernel(*refs):
     xs, (wk_ref, wv_ref), (a_ref, ya_ref, b_ref, c_ref, yb_ref, yc_ref) = refs[:4], refs[4:6], refs[6:12]
-    acc_ref = refs[12]
+    d_ref, e_ref, acc_ref = refs[12:]
     replica = lax.axis_index("rep")
     middle = (replica == 1) | (replica == 2)
     width = wk_ref.shape[1]
@@ -316,17 +316,17 @@
 
     @pl.when(middle)
     def _():
-        acc_ref[...] += dot(block(4), b_ref[...]) + dot(block(5), yb_ref[...])
+        acc_ref[...] += dot(block(4), b_ref[...]) + dot(block(5), yb_ref[...]) + dot(block(6), d_ref[...])
 
     @pl.when(jnp.logical_not(middle))
     def _():
-        acc_ref[...] += dot(block(4), c_ref[...]) + dot(block(5), yc_ref[...])
+        acc_ref[...] += dot(block(4), c_ref[...]) + dot(block(5), yc_ref[...]) + dot(block(6), e_ref[...])
 
 
 def tail_kernel(far, steps, listed_ref, *refs):
     if far:
-        xs, (d_ref, yd_ref, ek_ref, ev_ref, yek_ref, yev_ref) = refs[:4], refs[4:10]
-        refs = refs[10:]
+        xs, (yd_ref, ye_ref) = refs[:4], refs[4:6]
+        refs = refs[6:]
     acc_ref, cos_ref, sin_ref, kgain_ref, rows_ref, num_ref, den_ref, moved_ref = refs[:8]
     keys_ref, values_ref, out_ref, o3 = refs[8:12]
     replica = lax.axis_index("rep")
@@ -346,11 +346,11 @@
 
         @pl.when(middle)
         def _():
-            fresh[...] = acc_ref[...] + dot(block(6), d_ref[...]) + dot(block(7), yd_ref[...])
+            fresh[...] = acc_ref[...] + dot(block(7), yd_ref[...])
 
         @pl.when(jnp.logical_not(middle))
         def _():
-            fresh[...] = acc_ref[...] + dot(block(6), ek_ref[...]) + dot(block(7), yek_ref[...])
+            fresh[...] = acc_ref[...] + dot(block(7), ye_ref[...])
 
         tp, sub = lax.axis_index("tp"), lax.axis_index("sub")
         places = [tp * 2 + sub, (tp ^ 1) * 2 + sub, tp * 2 + (sub ^ 1), (tp ^ 1) * 2 + (sub ^ 1)]
@@ -507,14 +507,14 @@
         (acc,) = call(
             first_kernel,
             [pltpu.VMEM((tokens, 2 * width), F32)],
-            [blocks, across, beside, corner, w_key, w_value, from_a, over_a, from_b, from_c, over_b, over_c],
+            [blocks, across, beside, corner, w_key, w_value, from_a, over_a, from_b, from_c, over_b, over_c, from_d, from_e],
             [],
             flops=3 * depth * tokens * width * 4,
         )
         q3, k3, v3, moved = queries(after(own_sums, acc), pair_in, r2)
         returned = lax.ppermute(moved, "rep", [(i, i + half) for i in range(half)])
         num, den, rows_last = attend(q3, k3, v3)
-        far = [blocks, across, beside, corner, from_d, over_d, from_e, from_e, over_e, over_e]
+        far = [blocks, across, beside, corner, over_d, over_e]
     else:
         spread = lax.all_to_all(
             normalize(dec_hidden[0].reshape(per, features), norm_gain), "rep", split_axis=1, concat_axis=0, tiled=True

time: 91.4 us -> 91 us (level)
  transfers between devices with their start and end apart: 19 -> 19, of which waited for: 7 -> 7; matrix products, arithmetic and copies ran while one was open for 0% -> 0% of each run, Pallas kernels for 12% -> 13%
where the time goes in v5:
time: 91 us; the launch traced here: 90.5 us
  waiting for transfers between devices  34.8 us (38%)
  starting transfers between devices  33.2 us (36%)
  Pallas kernels  14.2 us (16%)
  local copies, waits for them, and re-layouts  7.21 us (8%)
  between operations  0.96 us (1%)
    ppermute x8, waiting for transfers between devices, xor_permute(): return lax.ppermute(value, axis, [(i, i ^ distance) for i in range(count)])  21.5 us
    ppermute x8, starting transfers between devices, xor_permute(): return lax.ppermute(value, axis, [(i, i ^ distance) for i in range(count)])  15.1 us
    pallas_call x7, Pallas kernels, call(): pl.pallas_call(kernel, out_shape=tuple(outs), in_specs=[SCALAR] * len(sca...  14.2 us
    ppermute x5, waiting for transfers between devices, line_pairs(): return lambda value: lax.ppermute(value, axis, pairs)  11.3 us
    ppermute x5, starting transfers between devices, across_groups(): return lax.ppermute(value, ('groups', 'rep'), pairs)  9.77 us
    ppermute x5, starting transfers between devices, line_pairs(): return lambda value: lax.ppermute(value, axis, pairs)  7.05 us
    unnamed x38, local copies, waits for them, and re-layouts  5.94 us
    ppermute x5, waiting for transfers between devices, across_groups(): return lax.ppermute(value, ('groups', 'rep'), pairs)  2.02 us
  transfers between devices with their start and end apart: 19, of which 7 were waited for; matrix products, arithmetic and copies ran while one was open for 0% of the time, Pallas kernels for 13%

profile of v5, /device:TPU:0, one launch (start us, length us, event | category | flops | bytes accessed | tf_op | source)
XLA Modules:
  0.0 90.5 jit_solution(16257247380051533937)
XLA Ops:
  0.6 1.3 %constant_dynamic-slice_fusion = (bf16[640,256]{1,0:T(8,128)(2,1)S(1)}, bf16[640,256]{1,0:T(8,128)(2,1)S(1)}) fusion(bf16[1280,256]{1,0:T(8,128)(2,1)} %refs_5_.3, s32[]{:T(128)S(6)} %select_n.4, bf16[1280,256]{1,0:T(8,128)(2,1)} %refs_4_.3), kind=kLoop, calls=%fused_computation.4 | loop fusion | bytes 1310724 | tf_op jit(solution)/shard_map/dynamic_slice | solution.py:475
  2.0 3.1 %collective-permute-start.4 = (bf16[640,512]{1,0:T(8,128)(2,1)S(1)}, bf16[640,512]{1,0:T(8,128)(2,1)S(1)}, u32[]{:S(2)}, u32[]{:S(2)}) collective-permute-start(bf16[640,512]{1,0:T(8,128)(2,1)S(1)} %pad_maximum_fusion), channel_id=1, source_target_pairs={{0,4},{4,0},{8,12},{12,8},{1,5},{5,1},{9,13},{13,9},{2,6},{6,2},{1... | collective-permute-start | bytes 1966088 | tf_op jit(solution)/shard_map/ppermute | solution.py:399
  5.8 0.9 %copy-done.10 = bf16[1,9,2,5120]{3,2,1,0:T(2,128)(2,1)S(1)} copy-done((bf16[1,9,2,5120]{3,2,1,0:T(2,128)(2,1)S(1)}, bf16[1,9,2,5120]{3,2,1,0:T(2,128)(2,1)}, u32[]{:S(2)}) %copy-start.10) | copy-done | bytes 184344
  6.7 0.7 copy-done.11
  7.8 4.4 %collective-permute-start = (bf16[18,1280]{1,0:T(8,128)(2,1)S(1)}, bf16[18,1280]{1,0:T(8,128)(2,1)S(1)}, u32[]{:S(2)}, u32[]{:S(2)}) collective-permute-start(bf16[18,1280]{1,0:T(8,128)(2,1)S(1)} %get-tuple-element.31), channel_id=1, source_target_pairs={{0,4},{4,0},{8,12},{12,8},{1,5},{5,1},{9,13},{13,9},{2,6},{6,2},{1... | collective-permute-start | bytes 138248 | tf_op jit(solution)/shard_map/ppermute | solution.py:50
  12.2 2.4 %collective-permute-start.2 = (bf16[18,1280]{1,0:T(8,128)(2,1)S(1)}, bf16[18,1280]{1,0:T(8,128)(2,1)S(1)}, u32[]{:S(2)}, u32[]{:S(2)}) collective-permute-start(bf16[18,1280]{1,0:T(8,128)(2,1)S(1)} %get-tuple-element.33), channel_id=1, source_target_pairs={{0,12},{4,8},{8,4},{12,0},{1,13},{5,9},{9,5},{13,1},{2,14},{6,10},... | collective-permute-start | bytes 138248 | tf_op jit(solution)/shard_map/ppermute | solution.py:50
  14.7 1.3 %copy-done.7 = bf16[1,128,5120]{2,1,0:T(8,128)(2,1)S(1)} copy-done((bf16[1,128,5120]{2,1,0:T(8,128)(2,1)S(1)}, bf16[1,128,5120]{2,1,0:T(8,128)(2,1)}, u32[]{:S(2)}) %copy-start.7) | copy-done | bytes 1310744
  16.0 0.7 copy-done.12
  16.7 0.7 shard_map.175.refs_0_
  17.4 3.0 %collective-permute-done.4.refs_6_ = bf16[640,512]{1,0:T(8,128)(2,1)S(1)} collective-permute-done((bf16[640,512]{1,0:T(8,128)(2,1)S(1)}, bf16[640,512]{1,0:T(8,128)(2,1)S(1)}, u32[]{:S(2)}, u32[]{:S(2)}) %collective-permute-start.4) | collective-permute-done | bytes 655392 | tf_op jit(solution)/shard_map/ppermute | solution.py:399
  21.2 1.3 %collective-permute-start.7 = (bf16[640,512]{1,0:T(8,128)(2,1)S(1)}, bf16[640,512]{1,0:T(8,128)(2,1)S(1)}, u32[]{:S(2)}, u32[]{:S(2)}) collective-permute-start(bf16[640,512]{1,0:T(8,128)(2,1)S(1)} %collective-permute-done.5.refs_8_), channel_id=1, source_target_pairs={{4,0},{8,12},{5,1},{9,13},{6,2},{10,14},{7,3},{11,15},{20,16},{24,... | collective-permute-start | bytes 1966088 | tf_op jit(solution)/shard_map/ppermute | solution.py:399
  22.5 6.1 %collective-permute-done.1.refs_2_ = bf16[18,1280]{1,0:T(8,128)(2,1)S(1)} collective-permute-done((bf16[18,1280]{1,0:T(8,128)(2,1)S(1)}, bf16[18,1280]{1,0:T(8,128)(2,1)S(1)}, u32[]{:S(2)}, u32[]{:S(2)}) %collective-permute-start.1) | collective-permute-done | bytes 46112 | tf_op jit(solution)/shard_map/ppermute | solution.py:50
  28.6 1.5 %collective-permute-start.3 = (bf16[8,128,640]{2,1,0:T(8,128)(2,1)S(1)}, bf16[8,128,640]{2,1,0:T(8,128)(2,1)S(1)}, u32[]{:S(2)}, u32[]{:S(2)}) collective-permute-start(bf16[8,128,640]{2,1,0:T(8,128)(2,1)S(1)} %shard_map.175.refs_0_), channel_id=1, source_target_pairs={{0,2},{2,0},{1,3},{3,1},{4,6},{6,4},{5,7},{7,5},{8,10},{10,8},{9,1... | collective-permute-start | bytes 3932168 | tf_op jit(solution)/shard_map/ppermute | solution.py:50
  30.1 1.1 %copy-done.3 = bf16[1280,256]{1,0:T(8,128)(2,1)S(1)} copy-done((bf16[1280,256]{1,0:T(8,128)(2,1)S(1)}, bf16[1280,256]{1,0:T(8,128)(2,1)}, u32[]{:S(2)}) %copy-start.3) | copy-done | bytes 655384
  31.2 1.1 %copy-done.5 = bf16[1280,256]{1,0:T(8,128)(2,1)S(1)} copy-done((bf16[1280,256]{1,0:T(8,128)(2,1)S(1)}, bf16[1280,256]{1,0:T(8,128)(2,1)}, u32[]{:S(2)}) %copy-start.5) | copy-done | bytes 655384
  32.3 1.7 %shard_map.177 = (f32[18,2560]{1,0:T(8,128)S(1)}, bf16[2,18,2560]{2,1,0:T(8,128)(2,1)S(1)}, f32[18,2560]{1,0:T(8,128)S(1)}) custom-call(s32[4]{0:T(128)S(1)} %copy-done.15, bf16[18,1280]{1,0:T(8,128)(2,1)S(1)} %get-tuple-element.38.refs_0_, bf16[18,1280]{1,0:T(8,128)(2,1)S(1)} %collective-permute-done.refs_1_, ...), custom_call_target="tpu_custom_call" | custom-call | flops 471859200 | bytes 7290880 | tf_op jit(solution)/shard_map/pallas_call | solution.py:25
  34.0 5.0 %collective-permute-start.9 = (bf16[2,18,2560]{2,1,0:T(8,128)(2,1)S(1)}, bf16[2,18,2560]{2,1,0:T(8,128)(2,1)S(1)}, u32[]{:S(2)}, u32[]{:S(2)}) collective-permute-start(bf16[2,18,2560]{2,1,0:T(8,128)(2,1)S(1)} %get-tuple-element.39), channel_id=1, source_target_pairs={{0,4},{4,0},{8,12},{12,8},{1,5},{5,1},{9,13},{13,9},{2,6},{6,2},{1... | collective-permute-start | bytes 552968 | tf_op jit(solution)/shard_map/ppermute | solution.py:50
  39.0 1.5 %collective-permute-start.11 = (bf16[640,512]{1,0:T(8,128)(2,1)S(1)}, bf16[640,512]{1,0:T(8,128)(2,1)S(1)}, u32[]{:S(2)}, u32[]{:S(2)}) collective-permute-start(bf16[640,512]{1,0:T(8,128)(2,1)S(1)} %collective-permute-done.4.refs_6_), channel_id=1, source_target_pairs={{0,16},{4,20},{8,24},{12,28},{16,0},{20,4},{24,8},{28,12},{1,17},{... | collective-permute-start | bytes 1966088 | tf_op jit(solution)/shard_map/ppermute | solution.py:405
  40.6 10.1 %collective-permute-done.9.refs_1_ = bf16[2,18,2560]{2,1,0:T(8,128)(2,1)S(1)} collective-permute-done((bf16[2,18,2560]{2,1,0:T(8,128)(2,1)S(1)}, bf16[2,18,2560]{2,1,0:T(8,128)(2,1)S(1)}, u32[]{:S(2)}, u32[]{:S(2)}) %collective-permute-start.9) | collective-permute-done | bytes 184352 | tf_op jit(solution)/shard_map/ppermute | solution.py:50
  50.6 1.3 %collective-permute-start.10 = (bf16[640,512]{1,0:T(8,128)(2,1)S(1)}, bf16[640,512]{1,0:T(8,128)(2,1)S(1)}, u32[]{:S(2)}, u32[]{:S(2)}) collective-permute-start(bf16[640,512]{1,0:T(8,128)(2,1)S(1)} %collective-permute-done.6.refs_12_), channel_id=1, source_target_pairs={{4,0},{8,12},{5,1},{9,13},{6,2},{10,14},{7,3},{11,15},{20,16},{24,... | collective-permute-start | bytes 1966088 | tf_op jit(solution)/shard_map/ppermute | solution.py:399
  52.6 3.4 %collective-permute-start.13 = (bf16[640,512]{1,0:T(8,128)(2,1)S(1)}, bf16[640,512]{1,0:T(8,128)(2,1)S(1)}, u32[]{:S(2)}, u32[]{:S(2)}) collective-permute-start(bf16[640,512]{1,0:T(8,128)(2,1)S(1)} %collective-permute-done.7.refs_9_), channel_id=1, source_target_pairs={{0,16},{12,28},{16,0},{28,12},{1,17},{13,29},{17,1},{29,13},{2,18}... | collective-permute-start | bytes 1966088 | tf_op jit(solution)/shard_map/ppermute | solution.py:405
  56.2 1.1 %collective-permute-done.3.refs_1_ = bf16[8,128,640]{2,1,0:T(8,128)(2,1)S(1)} collective-permute-done((bf16[8,128,640]{2,1,0:T(8,128)(2,1)S(1)}, bf16[8,128,640]{2,1,0:T(8,128)(2,1)S(1)}, u32[]{:S(2)}, u32[]{:S(2)}) %collective-permute-start.3) | collective-permute-done | bytes 1310752 | tf_op jit(solution)/shard_map/ppermute | solution.py:50
  57.3 8.3 %collective-permute-done.10.refs_13_ = bf16[640,512]{1,0:T(8,128)(2,1)S(1)} collective-permute-done((bf16[640,512]{1,0:T(8,128)(2,1)S(1)}, bf16[640,512]{1,0:T(8,128)(2,1)S(1)}, u32[]{:S(2)}, u32[]{:S(2)}) %collective-permute-start.10) | collective-permute-done | bytes 655392 | tf_op jit(solution)/shard_map/ppermute | solution.py:399
  65.6 2.0 %collective-permute-done.13.refs_11_ = bf16[640,512]{1,0:T(8,128)(2,1)S(1)} collective-permute-done((bf16[640,512]{1,0:T(8,128)(2,1)S(1)}, bf16[640,512]{1,0:T(8,128)(2,1)S(1)}, u32[]{:S(2)}, u32[]{:S(2)}) %collective-permute-start.13) | collective-permute-done | bytes 655392 | tf_op jit(solution)/shard_map/ppermute | solution.py:405
  67.6 3.4 %collective-permute-start.16 = (bf16[640,512]{1,0:T(8,128)(2,1)S(1)}, bf16[640,512]{1,0:T(8,128)(2,1)S(1)}, u32[]{:S(2)}, u32[]{:S(2)}) collective-permute-start(bf16[640,512]{1,0:T(8,128)(2,1)S(1)} %collective-permute-done.10.refs_13_), channel_id=1, source_target_pairs={{0,16},{12,28},{16,0},{28,12},{1,17},{13,29},{17,1},{29,13},{2,18}... | collective-permute-start | bytes 1966088 | tf_op jit(solution)/shard_map/ppermute | solution.py:405
  71.8 1.7 %collective-permute-start.17 = (bf16[18,2560]{1,0:T(8,128)(2,1)S(1)}, bf16[18,2560]{1,0:T(8,128)(2,1)S(1)}, u32[]{:S(2)}, u32[]{:S(2)}) collective-permute-start(bf16[18,2560]{1,0:T(8,128)(2,1)S(1)} %fusion), channel_id=1, source_target_pairs={{0,8},{4,12},{8,0},{12,4},{1,9},{5,13},{9,1},{13,5},{2,10},{6,14},... | collective-permute-start | bytes 276488 | tf_op jit(solution)/shard_map/ppermute | solution.py:50
  73.5 3.2 %shard_map.178.refs_6_ = f32[512,512]{1,0:T(8,128)S(1)} custom-call(bf16[8,128,640]{2,1,0:T(8,128)(2,1)S(1)} %shard_map.175.refs_0_, bf16[8,128,640]{2,1,0:T(8,128)(2,1)S(1)} %collective-permute-done.3.refs_1_, bf16[8,128,640]{2,1,0:T(8,128)(2,1)S(1)} %collective-permute-done.8.refs_2_, bf16[8,128,640]{2,1,0:T(8,128)(2,1)S(1)} %collective-permute-done.14.refs_3_, ...), custom_call_target="tpu_custom_call" | custom-call | flops 2013265920 | bytes 12845056 | tf_op jit(solution)/shard_map/pallas_call | solution.py:25
  76.7 4.2 %collective-permute-done.17.refs_2_ = bf16[18,2560]{1,0:T(8,128)(2,1)S(1)} collective-permute-done((bf16[18,2560]{1,0:T(8,128)(2,1)S(1)}, bf16[18,2560]{1,0:T(8,128)(2,1)S(1)}, u32[]{:S(2)}, u32[]{:S(2)}) %collective-permute-start.17) | collective-permute-done | bytes 92192 | tf_op jit(solution)/shard_map/ppermute | solution.py:50
  80.9 3.0 %shard_map.179 = (f32[18,16,128]{2,1,0:T(8,128)S(1)}, f32[18,16,128]{2,1,0:T(8,128)S(1)}, f32[18,16,128]{2,1,0:T(8,128)S(1)}, f32[2,32,128]{2,1,0:T(8,128)S(1)}) custom-call(s32[8,16]{1,0:T(8,128)S(1)} %bitcast.24, s32[4,8]{1,0:T(4,128)S(1)} %copy-done.14, s32[4]{0:T(128)S(1)} %copy-done.15, f32[18,2560]{1,0:T(8,128)S(1)} %get-tuple-element.47.refs_0_, ...), custom_call_target="tpu_custom_call" | custom-call | bytes 6180352 | tf_op jit(solution)/shard_map/pallas_call | solution.py:25
  83.9 1.3 %collective-permute-start.18 = (f32[2,32,128]{2,1,0:T(8,128)S(1)}, f32[2,32,128]{2,1,0:T(8,128)S(1)}, u32[]{:S(2)}, u32[]{:S(2)}) collective-permute-start(f32[2,32,128]{2,1,0:T(8,128)S(1)} %get-tuple-element.55), channel_id=1, source_target_pairs={{0,8},{4,12},{1,9},{5,13},{2,10},{6,14},{3,11},{7,15},{16,24},{20,... | collective-permute-start | bytes 98312 | tf_op jit(solution)/shard_map/ppermute | solution.py:515
  85.2 2.6 %shard_map.180 = (f32[18,16,128]{2,1,0:T(8,128)S(1)}, f32[18,16,128]{2,1,0:T(8,128)S(1)}, bf16[32,256]{1,0:T(8,128)(2,1)S(1)}) custom-call(s32[8,16]{1,0:T(8,128)S(1)} %bitcast.25, s32[4,8]{1,0:T(4,128)S(1)} %copy-done.14, f32[18,16,128]{2,1,0:T(8,128)S(1)} %get-tuple-element.49.refs_0_, f32[18,16,128]{2,1,0:T(8,128)S(1)} %get-tuple-element.50.refs_1_, ...), custom_call_target="tpu_custom_call" | custom-call | bytes 5996544 | tf_op jit(solution)/shard_map/pallas_call | solution.py:25
  87.9 2.6 %shard_map.181 = (bf16[512,256]{1,0:T(8,128)(2,1)}, bf16[512,256]{1,0:T(8,128)(2,1)}, bf16[9,2,2048]{2,1,0:T(2,128)(2,1)}) custom-call(s32[4]{0:T(128)S(1)} %copy-done.15, bf16[8,128,640]{2,1,0:T(8,128)(2,1)S(1)} %shard_map.175.refs_0_, bf16[8,128,640]{2,1,0:T(8,128)(2,1)S(1)} %collective-permute-done.3.refs_1_, ...), custom_call_target="tpu_custom_call" | custom-call | flops 671088640 | bytes 9069056 | tf_op jit(solution)/shard_map/pallas_call | solution.py:25
  (54 shorter events, 3.4 us)
Async XLA Ops:
  0.6 29.5 %copy-start.2 = (bf16[1280,2048]{1,0:T(8,128)(2,1)S(1)}, bf16[1280,2048]{1,0:T(8,128)(2,1)}, u32[]{:S(2)}) copy-start(bf16[1280,2048]{1,0:T(8,128)(2,1)} %refs_4_.2) | copy-start | bytes 15728644
  2.0 18.5 %collective-permute-start.4 = (bf16[640,512]{1,0:T(8,128)(2,1)S(1)}, bf16[640,512]{1,0:T(8,128)(2,1)S(1)}, u32[]{:S(2)}, u32[]{:S(2)}) collective-permute-start(bf16[640,512]{1,0:T(8,128)(2,1)S(1)} %pad_maximum_fusion), channel_id=1, source_target_pairs={{0,4},{4,0},{8,12},{12,8},{1,5},{5,1},{9,13},{13,9},{2,6},{6,2},{1... | collective-permute-start | bytes 1966088 | tf_op jit(solution)/shard_map/ppermute | solution.py:399
  5.1 15.4 %collective-permute-start.5 = (bf16[640,512]{1,0:T(8,128)(2,1)S(1)}, bf16[640,512]{1,0:T(8,128)(2,1)S(1)}, u32[]{:S(2)}, u32[]{:S(2)}) collective-permute-start(bf16[640,512]{1,0:T(8,128)(2,1)S(1)} %pad_maximum_fusion), channel_id=1, source_target_pairs={{4,8},{8,4},{5,9},{9,5},{6,10},{10,6},{7,11},{11,7},{20,24},{24,20... | collective-permute-start | bytes 1966088 | tf_op jit(solution)/shard_map/ppermute | solution.py:399
  7.8 14.7 %collective-permute-start = (bf16[18,1280]{1,0:T(8,128)(2,1)S(1)}, bf16[18,1280]{1,0:T(8,128)(2,1)S(1)}, u32[]{:S(2)}, u32[]{:S(2)}) collective-permute-start(bf16[18,1280]{1,0:T(8,128)(2,1)S(1)} %get-tuple-element.31), channel_id=1, source_target_pairs={{0,4},{4,0},{8,12},{12,8},{1,5},{5,1},{9,13},{13,9},{2,6},{6,2},{1... | collective-permute-start | bytes 138248 | tf_op jit(solution)/shard_map/ppermute | solution.py:50
  12.2 16.4 %collective-permute-start.1 = (bf16[18,1280]{1,0:T(8,128)(2,1)S(1)}, bf16[18,1280]{1,0:T(8,128)(2,1)S(1)}, u32[]{:S(2)}, u32[]{:S(2)}) collective-permute-start(bf16[18,1280]{1,0:T(8,128)(2,1)S(1)} %get-tuple-element.32), channel_id=1, source_target_pairs={{0,8},{4,12},{8,0},{12,4},{1,9},{5,13},{9,1},{13,5},{2,10},{6,14},... | collective-permute-start | bytes 138248 | tf_op jit(solution)/shard_map/ppermute | solution.py:50
  12.2 16.4 %collective-permute-start.2 = (bf16[18,1280]{1,0:T(8,128)(2,1)S(1)}, bf16[18,1280]{1,0:T(8,128)(2,1)S(1)}, u32[]{:S(2)}, u32[]{:S(2)}) collective-permute-start(bf16[18,1280]{1,0:T(8,128)(2,1)S(1)} %get-tuple-element.33), channel_id=1, source_target_pairs={{0,12},{4,8},{8,4},{12,0},{1,13},{5,9},{9,5},{13,1},{2,14},{6,10},... | collective-permute-start | bytes 138248 | tf_op jit(solution)/shard_map/ppermute | solution.py:50
  16.7 13.4 %copy-start.15 = (s32[4]{0:T(128)S(1)}, s32[4]{0:T(128)}, u32[]{:S(2)}) copy-start(s32[4]{0:T(128)} %listed_ref.5) | copy-start | bytes 52
  20.5 30.2 %collective-permute-start.6 = (bf16[640,512]{1,0:T(8,128)(2,1)S(1)}, bf16[640,512]{1,0:T(8,128)(2,1)S(1)}, u32[]{:S(2)}, u32[]{:S(2)}) collective-permute-start(bf16[640,512]{1,0:T(8,128)(2,1)S(1)} %collective-permute-done.4.refs_6_), channel_id=1, source_target_pairs={{4,8},{8,4},{5,9},{9,5},{6,10},{10,6},{7,11},{11,7},{20,24},{24,20... | collective-permute-start | bytes 1966088 | tf_op jit(solution)/shard_map/ppermute | solution.py:399
  21.2 29.5 %collective-permute-start.7 = (bf16[640,512]{1,0:T(8,128)(2,1)S(1)}, bf16[640,512]{1,0:T(8,128)(2,1)S(1)}, u32[]{:S(2)}, u32[]{:S(2)}) collective-permute-start(bf16[640,512]{1,0:T(8,128)(2,1)S(1)} %collective-permute-done.5.refs_8_), channel_id=1, source_target_pairs={{4,0},{8,12},{5,1},{9,13},{6,2},{10,14},{7,3},{11,15},{20,16},{24,... | collective-permute-start | bytes 1966088 | tf_op jit(solution)/shard_map/ppermute | solution.py:399
  28.6 28.7 %collective-permute-start.3 = (bf16[8,128,640]{2,1,0:T(8,128)(2,1)S(1)}, bf16[8,128,640]{2,1,0:T(8,128)(2,1)S(1)}, u32[]{:S(2)}, u32[]{:S(2)}) collective-permute-start(bf16[8,128,640]{2,1,0:T(8,128)(2,1)S(1)} %shard_map.175.refs_0_), channel_id=1, source_target_pairs={{0,2},{2,0},{1,3},{3,1},{4,6},{6,4},{5,7},{7,5},{8,10},{10,8},{9,1... | collective-permute-start | bytes 3932168 | tf_op jit(solution)/shard_map/ppermute | solution.py:50
  32.3 41.2 %copy-start.4 = (bf16[1280,256]{1,0:T(8,128)(2,1)S(1)}, bf16[1280,256]{1,0:T(8,128)(2,1)}, u32[]{:S(2)}) copy-start(bf16[1280,256]{1,0:T(8,128)(2,1)} %refs_5_.3) | copy-start | bytes 1966084
  32.3 41.2 %copy-start.6 = (bf16[1280,256]{1,0:T(8,128)(2,1)S(1)}, bf16[1280,256]{1,0:T(8,128)(2,1)}, u32[]{:S(2)}) copy-start(bf16[1280,256]{1,0:T(8,128)(2,1)} %refs_4_.3) | copy-start | bytes 1966084
  34.0 16.6 %collective-permute-start.9 = (bf16[2,18,2560]{2,1,0:T(8,128)(2,1)S(1)}, bf16[2,18,2560]{2,1,0:T(8,128)(2,1)S(1)}, u32[]{:S(2)}, u32[]{:S(2)}) collective-permute-start(bf16[2,18,2560]{2,1,0:T(8,128)(2,1)S(1)} %get-tuple-element.39), channel_id=1, source_target_pairs={{0,4},{4,0},{8,12},{12,8},{1,5},{5,1},{9,13},{13,9},{2,6},{6,2},{1... | collective-permute-start | bytes 552968 | tf_op jit(solution)/shard_map/ppermute | solution.py:50
  39.0 17.0 %collective-permute-start.11 = (bf16[640,512]{1,0:T(8,128)(2,1)S(1)}, bf16[640,512]{1,0:T(8,128)(2,1)S(1)}, u32[]{:S(2)}, u32[]{:S(2)}) collective-permute-start(bf16[640,512]{1,0:T(8,128)(2,1)S(1)} %collective-permute-done.4.refs_6_), channel_id=1, source_target_pairs={{0,16},{4,20},{8,24},{12,28},{16,0},{20,4},{24,8},{28,12},{1,17},{... | collective-permute-start | bytes 1966088 | tf_op jit(solution)/shard_map/ppermute | solution.py:405
  50.6 14.9 %collective-permute-start.10 = (bf16[640,512]{1,0:T(8,128)(2,1)S(1)}, bf16[640,512]{1,0:T(8,128)(2,1)S(1)}, u32[]{:S(2)}, u32[]{:S(2)}) collective-permute-start(bf16[640,512]{1,0:T(8,128)(2,1)S(1)} %collective-permute-done.6.refs_12_), channel_id=1, source_target_pairs={{4,0},{8,12},{5,1},{9,13},{6,2},{10,14},{7,3},{11,15},{20,16},{24,... | collective-permute-start | bytes 1966088 | tf_op jit(solution)/shard_map/ppermute | solution.py:399
  51.9 13.6 %collective-permute-start.12 = (bf16[640,512]{1,0:T(8,128)(2,1)S(1)}, bf16[640,512]{1,0:T(8,128)(2,1)S(1)}, u32[]{:S(2)}, u32[]{:S(2)}) collective-permute-start(bf16[640,512]{1,0:T(8,128)(2,1)S(1)} %collective-permute-done.5.refs_8_), channel_id=1, source_target_pairs={{4,20},{8,24},{20,4},{24,8},{5,21},{9,25},{21,5},{25,9},{6,22},{10... | collective-permute-start | bytes 1966088 | tf_op jit(solution)/shard_map/ppermute | solution.py:405
  52.6 14.9 %collective-permute-start.13 = (bf16[640,512]{1,0:T(8,128)(2,1)S(1)}, bf16[640,512]{1,0:T(8,128)(2,1)S(1)}, u32[]{:S(2)}, u32[]{:S(2)}) collective-permute-start(bf16[640,512]{1,0:T(8,128)(2,1)S(1)} %collective-permute-done.7.refs_9_), channel_id=1, source_target_pairs={{0,16},{12,28},{16,0},{28,12},{1,17},{13,29},{17,1},{29,13},{2,18}... | collective-permute-start | bytes 1966088 | tf_op jit(solution)/shard_map/ppermute | solution.py:405
  56.1 17.4 %collective-permute-start.8 = (bf16[8,128,640]{2,1,0:T(8,128)(2,1)S(1)}, bf16[8,128,640]{2,1,0:T(8,128)(2,1)S(1)}, u32[]{:S(2)}, u32[]{:S(2)}) collective-permute-start(bf16[8,128,640]{2,1,0:T(8,128)(2,1)S(1)} %shard_map.175.refs_0_), channel_id=1, source_target_pairs={{0,1},{1,0},{2,3},{3,2},{4,5},{5,4},{6,7},{7,6},{8,9},{9,8},{10,11... | collective-permute-start | bytes 3932168 | tf_op jit(solution)/shard_map/ppermute | solution.py:50
  67.6 5.9 %collective-permute-start.14 = (bf16[8,128,640]{2,1,0:T(8,128)(2,1)S(1)}, bf16[8,128,640]{2,1,0:T(8,128)(2,1)S(1)}, u32[]{:S(2)}, u32[]{:S(2)}) collective-permute-start(bf16[8,128,640]{2,1,0:T(8,128)(2,1)S(1)} %collective-permute-done.3.refs_1_), channel_id=1, source_target_pairs={{0,1},{1,0},{2,3},{3,2},{4,5},{5,4},{6,7},{7,6},{8,9},{9,8},{10,11... | collective-permute-start | bytes 3932168 | tf_op jit(solution)/shard_map/ppermute | solution.py:50
  67.6 20.2 %collective-permute-start.16 = (bf16[640,512]{1,0:T(8,128)(2,1)S(1)}, bf16[640,512]{1,0:T(8,128)(2,1)S(1)}, u32[]{:S(2)}, u32[]{:S(2)}) collective-permute-start(bf16[640,512]{1,0:T(8,128)(2,1)S(1)} %collective-permute-done.10.refs_13_), channel_id=1, source_target_pairs={{0,16},{12,28},{16,0},{28,12},{1,17},{13,29},{17,1},{29,13},{2,18}... | collective-permute-start | bytes 1966088 | tf_op jit(solution)/shard_map/ppermute | solution.py:405
  71.0 16.8 %collective-permute-start.15 = (bf16[640,512]{1,0:T(8,128)(2,1)S(1)}, bf16[640,512]{1,0:T(8,128)(2,1)S(1)}, u32[]{:S(2)}, u32[]{:S(2)}) collective-permute-start(bf16[640,512]{1,0:T(8,128)(2,1)S(1)} %collective-permute-done.6.refs_12_), channel_id=1, source_target_pairs={{4,20},{8,24},{20,4},{24,8},{5,21},{9,25},{21,5},{25,9},{6,22},{10... | collective-permute-start | bytes 1966088 | tf_op jit(solution)/shard_map/ppermute | solution.py:405
  71.7 9.1 %copy-start.13 = (s32[1,8,16]{2,1,0:T(8,128)S(1)}, s32[1,8,16]{2,1,0:T(8,128)}, u32[]{:S(2)}) copy-start(s32[1,8,16]{2,1,0:T(8,128)} %param.26) | copy-start | bytes 1540
  71.8 9.1 %copy-start.14 = (s32[4,8]{1,0:T(4,128)S(1)}, s32[4,8]{1,0:T(4,128)}, u32[]{:S(2)}) copy-start(s32[4,8]{1,0:T(4,128)} %lengths_ref.3) | copy-start | bytes 388
  71.8 9.1 %copy-start.16 = (f32[128]{0:T(128)S(1)}, f32[128]{0:T(128)}, u32[]{:S(2)}) copy-start(f32[128]{0:T(128)} %param.20) | copy-start | bytes 1540
  71.8 9.1 %copy-start.17 = (f32[128]{0:T(128)S(1)}, f32[128]{0:T(128)}, u32[]{:S(2)}) copy-start(f32[128]{0:T(128)} %param.19) | copy-start | bytes 1540
  71.8 9.1 %copy-start.18 = (f32[1,128]{1,0:T(1,128)S(1)}, f32[1,128]{1,0:T(1,128)}, u32[]{:S(2)}) copy-start(f32[1,128]{1,0:T(1,128)} %constant.20.clone.refs_3_) | copy-start | bytes 1540
  71.8 9.1 %collective-permute-start.17 = (bf16[18,2560]{1,0:T(8,128)(2,1)S(1)}, bf16[18,2560]{1,0:T(8,128)(2,1)S(1)}, u32[]{:S(2)}, u32[]{:S(2)}) collective-permute-start(bf16[18,2560]{1,0:T(8,128)(2,1)S(1)} %fusion), channel_id=1, source_target_pairs={{0,8},{4,12},{8,0},{12,4},{1,9},{5,13},{9,1},{13,5},{2,10},{6,14},... | collective-permute-start | bytes 276488 | tf_op jit(solution)/shard_map/ppermute | solution.py:50
  73.5 7.4 %copy-start = (bf16[1,40,128,256]{3,2,1,0:T(8,128)(2,1)S(1)}, bf16[1,40,128,256]{3,2,1,0:T(8,128)(2,1)}, u32[]{:S(2)}) copy-start(bf16[1,40,128,256]{3,2,1,0:T(8,128)(2,1)} %param.24) | copy-start | bytes 7864324
  73.5 7.4 %copy-start.1 = (bf16[1,40,128,256]{3,2,1,0:T(8,128)(2,1)S(1)}, bf16[1,40,128,256]{3,2,1,0:T(8,128)(2,1)}, u32[]{:S(2)}) copy-start(bf16[1,40,128,256]{3,2,1,0:T(8,128)(2,1)} %param.25) | copy-start | bytes 7864324
  83.9 3.9 %collective-permute-start.18 = (f32[2,32,128]{2,1,0:T(8,128)S(1)}, f32[2,32,128]{2,1,0:T(8,128)S(1)}, u32[]{:S(2)}, u32[]{:S(2)}) collective-permute-start(f32[2,32,128]{2,1,0:T(8,128)S(1)} %get-tuple-element.55), channel_id=1, source_target_pairs={{0,8},{4,12},{1,9},{5,13},{2,10},{6,14},{3,11},{7,15},{16,24},{20,... | collective-permute-start | bytes 98312 | tf_op jit(solution)/shard_map/ppermute | solution.py:515
  85.2 2.7 %copy-start.8 = (f32[512,128]{1,0:T(8,128)S(1)}, f32[512,128]{1,0:T(8,128)}, u32[]{:S(2)}) copy-start(f32[512,128]{1,0:T(8,128)} %constant.18.clone.refs_7_) | copy-start | bytes 786436
  85.2 2.7 %copy-start.9 = (f32[512,128]{1,0:T(8,128)S(1)}, f32[512,128]{1,0:T(8,128)}, u32[]{:S(2)}) copy-start(f32[512,128]{1,0:T(8,128)} %constant.19.clone.refs_8_) | copy-start | bytes 786436
  (6 other events, 5.9 us)

commit v6 on v5

--- a/solution.py
+++ b/solution.py
@@ -159,17 +159,12 @@
 
 def old_terms(rows, keys_ref, values_ref, page_of, length, pages, first):
     page = keys_ref.shape[1]
-    num, den = None, None
-    for i in range(pages):
-        at = first + i
-        scores = dot_rows(rows, keys_ref[page_of(at)])
-        ids = lax.broadcasted_iota(jnp.int32, scores.shape, 1) + at * page
-        weights = jnp.where(ids < length, jnp.exp(scores), 0.0)
-        part = jnp.sum(weights, axis=-1, keepdims=True)
-        mixed = dot(weights.astype(BF16), values_ref[page_of(at)])
-        num = mixed if num is None else num + mixed
-        den = part if den is None else den + part
-    return num, den
+    keys = jnp.concatenate([keys_ref[page_of(first + i)] for i in range(pages)], axis=0)
+    values = jnp.concatenate([values_ref[page_of(first + i)] for i in range(pages)], axis=0)
+    scores = dot_rows(rows, keys)
+    ids = lax.broadcasted_iota(jnp.int32, scores.shape, 1) + first * page
+    weights = jnp.where(ids < length, jnp.exp(scores), 0.0)
+    return dot(weights.astype(BF16), values), jnp.sum(weights, axis=-1, keepdims=True)
 
 
 def queries_kernel(parts, seq_count, steps, tokens, table_ref, lengths_ref, listed_ref, *refs):

time: 91 us -> 90.4 us (level)
  transfers between devices with their start and end apart: 19 -> 19, of which waited for: 7 -> 7; matrix products, arithmetic and copies ran while one was open for 0% -> 0% of each run, Pallas kernels for 13% -> 12%
where the time goes in v6:
time: 90.4 us; the launch traced here: 89.9 us
  waiting for transfers between devices  34.8 us (38%)
  starting transfers between devices  33.2 us (37%)
  Pallas kernels  13.6 us (15%)
  local copies, waits for them, and re-layouts  7.21 us (8%)
  between operations  0.96 us (1%)
    ppermute x8, waiting for transfers between devices, xor_permute(): return lax.ppermute(value, axis, [(i, i ^ distance) for i in range(count)])  21.5 us
    ppermute x8, starting transfers between devices, xor_permute(): return lax.ppermute(value, axis, [(i, i ^ distance) for i in range(count)])  15.1 us
    pallas_call x7, Pallas kernels, call(): pl.pallas_call(kernel, out_shape=tuple(outs), in_specs=[SCALAR] * len(sca...  13.6 us
    ppermute x5, waiting for transfers between devices, line_pairs(): return lambda value: lax.ppermute(value, axis, pairs)  11.3 us
    ppermute x5, starting transfers between devices, across_groups(): return lax.ppermute(value, ('groups', 'rep'), pairs)  9.77 us
    ppermute x5, starting transfers between devices, line_pairs(): return lambda value: lax.ppermute(value, axis, pairs)  7.05 us
    unnamed x38, local copies, waits for them, and re-layouts  5.94 us
    ppermute x5, waiting for transfers between devices, across_groups(): return lax.ppermute(value, ('groups', 'rep'), pairs)  2.02 us
  transfers between devices with their start and end apart: 19, of which 7 were waited for; matrix products, arithmetic and copies ran while one was open for 0% of the time, Pallas kernels for 12%

profile of v6, /device:TPU:0, one launch (start us, length us, event | category | flops | bytes accessed | tf_op | source)
XLA Modules:
  0.0 89.9 jit_solution(15085882268929176079)
XLA Ops:
  0.6 1.3 %constant_dynamic-slice_fusion = (bf16[640,256]{1,0:T(8,128)(2,1)S(1)}, bf16[640,256]{1,0:T(8,128)(2,1)S(1)}) fusion(bf16[1280,256]{1,0:T(8,128)(2,1)} %refs_5_.3, s32[]{:T(128)S(6)} %select_n.4, bf16[1280,256]{1,0:T(8,128)(2,1)} %refs_4_.3), kind=kLoop, calls=%fused_computation.4 | loop fusion | bytes 1310724 | tf_op jit(solution)/shard_map/dynamic_slice | solution.py:470
  2.0 3.1 %collective-permute-start.4 = (bf16[640,512]{1,0:T(8,128)(2,1)S(1)}, bf16[640,512]{1,0:T(8,128)(2,1)S(1)}, u32[]{:S(2)}, u32[]{:S(2)}) collective-permute-start(bf16[640,512]{1,0:T(8,128)(2,1)S(1)} %pad_maximum_fusion), channel_id=1, source_target_pairs={{0,4},{4,0},{8,12},{12,8},{1,5},{5,1},{9,13},{13,9},{2,6},{6,2},{1... | collective-permute-start | bytes 1966088 | tf_op jit(solution)/shard_map/ppermute | solution.py:394
  5.8 0.9 %copy-done.10 = bf16[1,9,2,5120]{3,2,1,0:T(2,128)(2,1)S(1)} copy-done((bf16[1,9,2,5120]{3,2,1,0:T(2,128)(2,1)S(1)}, bf16[1,9,2,5120]{3,2,1,0:T(2,128)(2,1)}, u32[]{:S(2)}) %copy-start.10) | copy-done | bytes 184344
  6.7 0.7 copy-done.11
  7.8 4.4 %collective-permute-start = (bf16[18,1280]{1,0:T(8,128)(2,1)S(1)}, bf16[18,1280]{1,0:T(8,128)(2,1)S(1)}, u32[]{:S(2)}, u32[]{:S(2)}) collective-permute-start(bf16[18,1280]{1,0:T(8,128)(2,1)S(1)} %get-tuple-element.31), channel_id=1, source_target_pairs={{0,4},{4,0},{8,12},{12,8},{1,5},{5,1},{9,13},{13,9},{2,6},{6,2},{1... | collective-permute-start | bytes 138248 | tf_op jit(solution)/shard_map/ppermute | solution.py:50
  12.2 2.4 %collective-permute-start.2 = (bf16[18,1280]{1,0:T(8,128)(2,1)S(1)}, bf16[18,1280]{1,0:T(8,128)(2,1)S(1)}, u32[]{:S(2)}, u32[]{:S(2)}) collective-permute-start(bf16[18,1280]{1,0:T(8,128)(2,1)S(1)} %get-tuple-element.33), channel_id=1, source_target_pairs={{0,12},{4,8},{8,4},{12,0},{1,13},{5,9},{9,5},{13,1},{2,14},{6,10},... | collective-permute-start | bytes 138248 | tf_op jit(solution)/shard_map/ppermute | solution.py:50
  14.7 1.3 %copy-done.7 = bf16[1,128,5120]{2,1,0:T(8,128)(2,1)S(1)} copy-done((bf16[1,128,5120]{2,1,0:T(8,128)(2,1)S(1)}, bf16[1,128,5120]{2,1,0:T(8,128)(2,1)}, u32[]{:S(2)}) %copy-start.7) | copy-done | bytes 1310744
  16.0 0.7 copy-done.12
  16.7 0.7 shard_map.175.refs_0_
  17.4 3.0 %collective-permute-done.4.refs_6_ = bf16[640,512]{1,0:T(8,128)(2,1)S(1)} collective-permute-done((bf16[640,512]{1,0:T(8,128)(2,1)S(1)}, bf16[640,512]{1,0:T(8,128)(2,1)S(1)}, u32[]{:S(2)}, u32[]{:S(2)}) %collective-permute-start.4) | collective-permute-done | bytes 655392 | tf_op jit(solution)/shard_map/ppermute | solution.py:394
  21.2 1.3 %collective-permute-start.7 = (bf16[640,512]{1,0:T(8,128)(2,1)S(1)}, bf16[640,512]{1,0:T(8,128)(2,1)S(1)}, u32[]{:S(2)}, u32[]{:S(2)}) collective-permute-start(bf16[640,512]{1,0:T(8,128)(2,1)S(1)} %collective-permute-done.5.refs_8_), channel_id=1, source_target_pairs={{4,0},{8,12},{5,1},{9,13},{6,2},{10,14},{7,3},{11,15},{20,16},{24,... | collective-permute-start | bytes 1966088 | tf_op jit(solution)/shard_map/ppermute | solution.py:394
  22.5 6.1 %collective-permute-done.1.refs_2_ = bf16[18,1280]{1,0:T(8,128)(2,1)S(1)} collective-permute-done((bf16[18,1280]{1,0:T(8,128)(2,1)S(1)}, bf16[18,1280]{1,0:T(8,128)(2,1)S(1)}, u32[]{:S(2)}, u32[]{:S(2)}) %collective-permute-start.1) | collective-permute-done | bytes 46112 | tf_op jit(solution)/shard_map/ppermute | solution.py:50
  28.6 1.5 %collective-permute-start.3 = (bf16[8,128,640]{2,1,0:T(8,128)(2,1)S(1)}, bf16[8,128,640]{2,1,0:T(8,128)(2,1)S(1)}, u32[]{:S(2)}, u32[]{:S(2)}) collective-permute-start(bf16[8,128,640]{2,1,0:T(8,128)(2,1)S(1)} %shard_map.175.refs_0_), channel_id=1, source_target_pairs={{0,2},{2,0},{1,3},{3,1},{4,6},{6,4},{5,7},{7,5},{8,10},{10,8},{9,1... | collective-permute-start | bytes 3932168 | tf_op jit(solution)/shard_map/ppermute | solution.py:50
  30.1 1.1 %copy-done.3 = bf16[1280,256]{1,0:T(8,128)(2,1)S(1)} copy-done((bf16[1280,256]{1,0:T(8,128)(2,1)S(1)}, bf16[1280,256]{1,0:T(8,128)(2,1)}, u32[]{:S(2)}) %copy-start.3) | copy-done | bytes 655384
  31.2 1.1 %copy-done.5 = bf16[1280,256]{1,0:T(8,128)(2,1)S(1)} copy-done((bf16[1280,256]{1,0:T(8,128)(2,1)S(1)}, bf16[1280,256]{1,0:T(8,128)(2,1)}, u32[]{:S(2)}) %copy-start.5) | copy-done | bytes 655384
  32.3 1.7 %shard_map.177 = (f32[18,2560]{1,0:T(8,128)S(1)}, bf16[2,18,2560]{2,1,0:T(8,128)(2,1)S(1)}, f32[18,2560]{1,0:T(8,128)S(1)}) custom-call(s32[4]{0:T(128)S(1)} %copy-done.15, bf16[18,1280]{1,0:T(8,128)(2,1)S(1)} %get-tuple-element.38.refs_0_, bf16[18,1280]{1,0:T(8,128)(2,1)S(1)} %collective-permute-done.refs_1_, ...), custom_call_target="tpu_custom_call" | custom-call | flops 471859200 | bytes 7290880 | tf_op jit(solution)/shard_map/pallas_call | solution.py:25
  34.0 5.0 %collective-permute-start.9 = (bf16[2,18,2560]{2,1,0:T(8,128)(2,1)S(1)}, bf16[2,18,2560]{2,1,0:T(8,128)(2,1)S(1)}, u32[]{:S(2)}, u32[]{:S(2)}) collective-permute-start(bf16[2,18,2560]{2,1,0:T(8,128)(2,1)S(1)} %get-tuple-element.39), channel_id=1, source_target_pairs={{0,4},{4,0},{8,12},{12,8},{1,5},{5,1},{9,13},{13,9},{2,6},{6,2},{1... | collective-permute-start | bytes 552968 | tf_op jit(solution)/shard_map/ppermute | solution.py:50
  39.0 1.5 %collective-permute-start.11 = (bf16[640,512]{1,0:T(8,128)(2,1)S(1)}, bf16[640,512]{1,0:T(8,128)(2,1)S(1)}, u32[]{:S(2)}, u32[]{:S(2)}) collective-permute-start(bf16[640,512]{1,0:T(8,128)(2,1)S(1)} %collective-permute-done.4.refs_6_), channel_id=1, source_target_pairs={{0,16},{4,20},{8,24},{12,28},{16,0},{20,4},{24,8},{28,12},{1,17},{... | collective-permute-start | bytes 1966088 | tf_op jit(solution)/shard_map/ppermute | solution.py:400
  40.6 10.1 %collective-permute-done.9.refs_1_ = bf16[2,18,2560]{2,1,0:T(8,128)(2,1)S(1)} collective-permute-done((bf16[2,18,2560]{2,1,0:T(8,128)(2,1)S(1)}, bf16[2,18,2560]{2,1,0:T(8,128)(2,1)S(1)}, u32[]{:S(2)}, u32[]{:S(2)}) %collective-permute-start.9) | collective-permute-done | bytes 184352 | tf_op jit(solution)/shard_map/ppermute | solution.py:50
  50.6 1.3 %collective-permute-start.10 = (bf16[640,512]{1,0:T(8,128)(2,1)S(1)}, bf16[640,512]{1,0:T(8,128)(2,1)S(1)}, u32[]{:S(2)}, u32[]{:S(2)}) collective-permute-start(bf16[640,512]{1,0:T(8,128)(2,1)S(1)} %collective-permute-done.6.refs_12_), channel_id=1, source_target_pairs={{4,0},{8,12},{5,1},{9,13},{6,2},{10,14},{7,3},{11,15},{20,16},{24,... | collective-permute-start | bytes 1966088 | tf_op jit(solution)/shard_map/ppermute | solution.py:394
  52.6 3.4 %collective-permute-start.13 = (bf16[640,512]{1,0:T(8,128)(2,1)S(1)}, bf16[640,512]{1,0:T(8,128)(2,1)S(1)}, u32[]{:S(2)}, u32[]{:S(2)}) collective-permute-start(bf16[640,512]{1,0:T(8,128)(2,1)S(1)} %collective-permute-done.7.refs_9_), channel_id=1, source_target_pairs={{0,16},{12,28},{16,0},{28,12},{1,17},{13,29},{17,1},{29,13},{2,18}... | collective-permute-start | bytes 1966088 | tf_op jit(solution)/shard_map/ppermute | solution.py:400
  56.2 1.1 %collective-permute-done.3.refs_1_ = bf16[8,128,640]{2,1,0:T(8,128)(2,1)S(1)} collective-permute-done((bf16[8,128,640]{2,1,0:T(8,128)(2,1)S(1)}, bf16[8,128,640]{2,1,0:T(8,128)(2,1)S(1)}, u32[]{:S(2)}, u32[]{:S(2)}) %collective-permute-start.3) | collective-permute-done | bytes 1310752 | tf_op jit(solution)/shard_map/ppermute | solution.py:50
  57.3 8.3 %collective-permute-done.10.refs_13_ = bf16[640,512]{1,0:T(8,128)(2,1)S(1)} collective-permute-done((bf16[640,512]{1,0:T(8,128)(2,1)S(1)}, bf16[640,512]{1,0:T(8,128)(2,1)S(1)}, u32[]{:S(2)}, u32[]{:S(2)}) %collective-permute-start.10) | collective-permute-done | bytes 655392 | tf_op jit(solution)/shard_map/ppermute | solution.py:394
  65.6 2.0 %collective-permute-done.13.refs_11_ = bf16[640,512]{1,0:T(8,128)(2,1)S(1)} collective-permute-done((bf16[640,512]{1,0:T(8,128)(2,1)S(1)}, bf16[640,512]{1,0:T(8,128)(2,1)S(1)}, u32[]{:S(2)}, u32[]{:S(2)}) %collective-permute-start.13) | collective-permute-done | bytes 655392 | tf_op jit(solution)/shard_map/ppermute | solution.py:400
  67.6 3.4 %collective-permute-start.16 = (bf16[640,512]{1,0:T(8,128)(2,1)S(1)}, bf16[640,512]{1,0:T(8,128)(2,1)S(1)}, u32[]{:S(2)}, u32[]{:S(2)}) collective-permute-start(bf16[640,512]{1,0:T(8,128)(2,1)S(1)} %collective-permute-done.10.refs_13_), channel_id=1, source_target_pairs={{0,16},{12,28},{16,0},{28,12},{1,17},{13,29},{17,1},{29,13},{2,18}... | collective-permute-start | bytes 1966088 | tf_op jit(solution)/shard_map/ppermute | solution.py:400
  71.8 1.7 %collective-permute-start.17 = (bf16[18,2560]{1,0:T(8,128)(2,1)S(1)}, bf16[18,2560]{1,0:T(8,128)(2,1)S(1)}, u32[]{:S(2)}, u32[]{:S(2)}) collective-permute-start(bf16[18,2560]{1,0:T(8,128)(2,1)S(1)} %fusion), channel_id=1, source_target_pairs={{0,8},{4,12},{8,0},{12,4},{1,9},{5,13},{9,1},{13,5},{2,10},{6,14},... | collective-permute-start | bytes 276488 | tf_op jit(solution)/shard_map/ppermute | solution.py:50
  73.5 3.2 %shard_map.178.refs_6_ = f32[512,512]{1,0:T(8,128)S(1)} custom-call(bf16[8,128,640]{2,1,0:T(8,128)(2,1)S(1)} %shard_map.175.refs_0_, bf16[8,128,640]{2,1,0:T(8,128)(2,1)S(1)} %collective-permute-done.3.refs_1_, bf16[8,128,640]{2,1,0:T(8,128)(2,1)S(1)} %collective-permute-done.8.refs_2_, bf16[8,128,640]{2,1,0:T(8,128)(2,1)S(1)} %collective-permute-done.14.refs_3_, ...), custom_call_target="tpu_custom_call" | custom-call | flops 2013265920 | bytes 12845056 | tf_op jit(solution)/shard_map/pallas_call | solution.py:25
  76.7 4.2 %collective-permute-done.17.refs_2_ = bf16[18,2560]{1,0:T(8,128)(2,1)S(1)} collective-permute-done((bf16[18,2560]{1,0:T(8,128)(2,1)S(1)}, bf16[18,2560]{1,0:T(8,128)(2,1)S(1)}, u32[]{:S(2)}, u32[]{:S(2)}) %collective-permute-start.17) | collective-permute-done | bytes 92192 | tf_op jit(solution)/shard_map/ppermute | solution.py:50
  80.9 2.7 %shard_map.179 = (f32[18,16,128]{2,1,0:T(8,128)S(1)}, f32[18,16,128]{2,1,0:T(8,128)S(1)}, f32[18,16,128]{2,1,0:T(8,128)S(1)}, f32[2,32,128]{2,1,0:T(8,128)S(1)}) custom-call(s32[8,16]{1,0:T(8,128)S(1)} %bitcast.24, s32[4,8]{1,0:T(4,128)S(1)} %copy-done.14, s32[4]{0:T(128)S(1)} %copy-done.15, f32[18,2560]{1,0:T(8,128)S(1)} %get-tuple-element.47.refs_0_, ...), custom_call_target="tpu_custom_call" | custom-call | bytes 6180352 | tf_op jit(solution)/shard_map/pallas_call | solution.py:25
  83.6 1.3 %collective-permute-start.18 = (f32[2,32,128]{2,1,0:T(8,128)S(1)}, f32[2,32,128]{2,1,0:T(8,128)S(1)}, u32[]{:S(2)}, u32[]{:S(2)}) collective-permute-start(f32[2,32,128]{2,1,0:T(8,128)S(1)} %get-tuple-element.55), channel_id=1, source_target_pairs={{0,8},{4,12},{1,9},{5,13},{2,10},{6,14},{3,11},{7,15},{16,24},{20,... | collective-permute-start | bytes 98312 | tf_op jit(solution)/shard_map/ppermute | solution.py:510
  84.9 2.4 %shard_map.180 = (f32[18,16,128]{2,1,0:T(8,128)S(1)}, f32[18,16,128]{2,1,0:T(8,128)S(1)}, bf16[32,256]{1,0:T(8,128)(2,1)S(1)}) custom-call(s32[8,16]{1,0:T(8,128)S(1)} %bitcast.25, s32[4,8]{1,0:T(4,128)S(1)} %copy-done.14, f32[18,16,128]{2,1,0:T(8,128)S(1)} %get-tuple-element.49.refs_0_, f32[18,16,128]{2,1,0:T(8,128)S(1)} %get-tuple-element.50.refs_1_, ...), custom_call_target="tpu_custom_call" | custom-call | bytes 5996544 | tf_op jit(solution)/shard_map/pallas_call | solution.py:25
  87.3 2.6 %shard_map.181 = (bf16[512,256]{1,0:T(8,128)(2,1)}, bf16[512,256]{1,0:T(8,128)(2,1)}, bf16[9,2,2048]{2,1,0:T(2,128)(2,1)}) custom-call(s32[4]{0:T(128)S(1)} %copy-done.15, bf16[8,128,640]{2,1,0:T(8,128)(2,1)S(1)} %shard_map.175.refs_0_, bf16[8,128,640]{2,1,0:T(8,128)(2,1)S(1)} %collective-permute-done.3.refs_1_, ...), custom_call_target="tpu_custom_call" | custom-call | flops 671088640 | bytes 9069056 | tf_op jit(solution)/shard_map/pallas_call | solution.py:25
  (54 shorter events, 3.4 us)
Async XLA Ops:
  0.6 29.5 %copy-start.2 = (bf16[1280,2048]{1,0:T(8,128)(2,1)S(1)}, bf16[1280,2048]{1,0:T(8,128)(2,1)}, u32[]{:S(2)}) copy-start(bf16[1280,2048]{1,0:T(8,128)(2,1)} %refs_4_.2) | copy-start | bytes 15728644
  2.0 18.5 %collective-permute-start.4 = (bf16[640,512]{1,0:T(8,128)(2,1)S(1)}, bf16[640,512]{1,0:T(8,128)(2,1)S(1)}, u32[]{:S(2)}, u32[]{:S(2)}) collective-permute-start(bf16[640,512]{1,0:T(8,128)(2,1)S(1)} %pad_maximum_fusion), channel_id=1, source_target_pairs={{0,4},{4,0},{8,12},{12,8},{1,5},{5,1},{9,13},{13,9},{2,6},{6,2},{1... | collective-permute-start | bytes 1966088 | tf_op jit(solution)/shard_map/ppermute | solution.py:394
  5.1 15.4 %collective-permute-start.5 = (bf16[640,512]{1,0:T(8,128)(2,1)S(1)}, bf16[640,512]{1,0:T(8,128)(2,1)S(1)}, u32[]{:S(2)}, u32[]{:S(2)}) collective-permute-start(bf16[640,512]{1,0:T(8,128)(2,1)S(1)} %pad_maximum_fusion), channel_id=1, source_target_pairs={{4,8},{8,4},{5,9},{9,5},{6,10},{10,6},{7,11},{11,7},{20,24},{24,20... | collective-permute-start | bytes 1966088 | tf_op jit(solution)/shard_map/ppermute | solution.py:394
  7.8 14.7 %collective-permute-start = (bf16[18,1280]{1,0:T(8,128)(2,1)S(1)}, bf16[18,1280]{1,0:T(8,128)(2,1)S(1)}, u32[]{:S(2)}, u32[]{:S(2)}) collective-permute-start(bf16[18,1280]{1,0:T(8,128)(2,1)S(1)} %get-tuple-element.31), channel_id=1, source_target_pairs={{0,4},{4,0},{8,12},{12,8},{1,5},{5,1},{9,13},{13,9},{2,6},{6,2},{1... | collective-permute-start | bytes 138248 | tf_op jit(solution)/shard_map/ppermute | solution.py:50
  12.2 16.4 %collective-permute-start.1 = (bf16[18,1280]{1,0:T(8,128)(2,1)S(1)}, bf16[18,1280]{1,0:T(8,128)(2,1)S(1)}, u32[]{:S(2)}, u32[]{:S(2)}) collective-permute-start(bf16[18,1280]{1,0:T(8,128)(2,1)S(1)} %get-tuple-element.32), channel_id=1, source_target_pairs={{0,8},{4,12},{8,0},{12,4},{1,9},{5,13},{9,1},{13,5},{2,10},{6,14},... | collective-permute-start | bytes 138248 | tf_op jit(solution)/shard_map/ppermute | solution.py:50
  12.2 16.4 %collective-permute-start.2 = (bf16[18,1280]{1,0:T(8,128)(2,1)S(1)}, bf16[18,1280]{1,0:T(8,128)(2,1)S(1)}, u32[]{:S(2)}, u32[]{:S(2)}) collective-permute-start(bf16[18,1280]{1,0:T(8,128)(2,1)S(1)} %get-tuple-element.33), channel_id=1, source_target_pairs={{0,12},{4,8},{8,4},{12,0},{1,13},{5,9},{9,5},{13,1},{2,14},{6,10},... | collective-permute-start | bytes 138248 | tf_op jit(solution)/shard_map/ppermute | solution.py:50
  16.7 13.4 %copy-start.15 = (s32[4]{0:T(128)S(1)}, s32[4]{0:T(128)}, u32[]{:S(2)}) copy-start(s32[4]{0:T(128)} %listed_ref.5) | copy-start | bytes 52
  20.5 30.2 %collective-permute-start.6 = (bf16[640,512]{1,0:T(8,128)(2,1)S(1)}, bf16[640,512]{1,0:T(8,128)(2,1)S(1)}, u32[]{:S(2)}, u32[]{:S(2)}) collective-permute-start(bf16[640,512]{1,0:T(8,128)(2,1)S(1)} %collective-permute-done.4.refs_6_), channel_id=1, source_target_pairs={{4,8},{8,4},{5,9},{9,5},{6,10},{10,6},{7,11},{11,7},{20,24},{24,20... | collective-permute-start | bytes 1966088 | tf_op jit(solution)/shard_map/ppermute | solution.py:394
  21.2 29.5 %collective-permute-start.7 = (bf16[640,512]{1,0:T(8,128)(2,1)S(1)}, bf16[640,512]{1,0:T(8,128)(2,1)S(1)}, u32[]{:S(2)}, u32[]{:S(2)}) collective-permute-start(bf16[640,512]{1,0:T(8,128)(2,1)S(1)} %collective-permute-done.5.refs_8_), channel_id=1, source_target_pairs={{4,0},{8,12},{5,1},{9,13},{6,2},{10,14},{7,3},{11,15},{20,16},{24,... | collective-permute-start | bytes 1966088 | tf_op jit(solution)/shard_map/ppermute | solution.py:394
  28.6 28.7 %collective-permute-start.3 = (bf16[8,128,640]{2,1,0:T(8,128)(2,1)S(1)}, bf16[8,128,640]{2,1,0:T(8,128)(2,1)S(1)}, u32[]{:S(2)}, u32[]{:S(2)}) collective-permute-start(bf16[8,128,640]{2,1,0:T(8,128)(2,1)S(1)} %shard_map.175.refs_0_), channel_id=1, source_target_pairs={{0,2},{2,0},{1,3},{3,1},{4,6},{6,4},{5,7},{7,5},{8,10},{10,8},{9,1... | collective-permute-start | bytes 3932168 | tf_op jit(solution)/shard_map/ppermute | solution.py:50
  32.3 41.2 %copy-start.4 = (bf16[1280,256]{1,0:T(8,128)(2,1)S(1)}, bf16[1280,256]{1,0:T(8,128)(2,1)}, u32[]{:S(2)}) copy-start(bf16[1280,256]{1,0:T(8,128)(2,1)} %refs_5_.3) | copy-start | bytes 1966084
  32.3 41.2 %copy-start.6 = (bf16[1280,256]{1,0:T(8,128)(2,1)S(1)}, bf16[1280,256]{1,0:T(8,128)(2,1)}, u32[]{:S(2)}) copy-start(bf16[1280,256]{1,0:T(8,128)(2,1)} %refs_4_.3) | copy-start | bytes 1966084
  34.0 16.6 %collective-permute-start.9 = (bf16[2,18,2560]{2,1,0:T(8,128)(2,1)S(1)}, bf16[2,18,2560]{2,1,0:T(8,128)(2,1)S(1)}, u32[]{:S(2)}, u32[]{:S(2)}) collective-permute-start(bf16[2,18,2560]{2,1,0:T(8,128)(2,1)S(1)} %get-tuple-element.39), channel_id=1, source_target_pairs={{0,4},{4,0},{8,12},{12,8},{1,5},{5,1},{9,13},{13,9},{2,6},{6,2},{1... | collective-permute-start | bytes 552968 | tf_op jit(solution)/shard_map/ppermute | solution.py:50
  39.0 17.0 %collective-permute-start.11 = (bf16[640,512]{1,0:T(8,128)(2,1)S(1)}, bf16[640,512]{1,0:T(8,128)(2,1)S(1)}, u32[]{:S(2)}, u32[]{:S(2)}) collective-permute-start(bf16[640,512]{1,0:T(8,128)(2,1)S(1)} %collective-permute-done.4.refs_6_), channel_id=1, source_target_pairs={{0,16},{4,20},{8,24},{12,28},{16,0},{20,4},{24,8},{28,12},{1,17},{... | collective-permute-start | bytes 1966088 | tf_op jit(solution)/shard_map/ppermute | solution.py:400
  50.6 14.9 %collective-permute-start.10 = (bf16[640,512]{1,0:T(8,128)(2,1)S(1)}, bf16[640,512]{1,0:T(8,128)(2,1)S(1)}, u32[]{:S(2)}, u32[]{:S(2)}) collective-permute-start(bf16[640,512]{1,0:T(8,128)(2,1)S(1)} %collective-permute-done.6.refs_12_), channel_id=1, source_target_pairs={{4,0},{8,12},{5,1},{9,13},{6,2},{10,14},{7,3},{11,15},{20,16},{24,... | collective-permute-start | bytes 1966088 | tf_op jit(solution)/shard_map/ppermute | solution.py:394
  51.9 13.6 %collective-permute-start.12 = (bf16[640,512]{1,0:T(8,128)(2,1)S(1)}, bf16[640,512]{1,0:T(8,128)(2,1)S(1)}, u32[]{:S(2)}, u32[]{:S(2)}) collective-permute-start(bf16[640,512]{1,0:T(8,128)(2,1)S(1)} %collective-permute-done.5.refs_8_), channel_id=1, source_target_pairs={{4,20},{8,24},{20,4},{24,8},{5,21},{9,25},{21,5},{25,9},{6,22},{10... | collective-permute-start | bytes 1966088 | tf_op jit(solution)/shard_map/ppermute | solution.py:400
  52.6 14.9 %collective-permute-start.13 = (bf16[640,512]{1,0:T(8,128)(2,1)S(1)}, bf16[640,512]{1,0:T(8,128)(2,1)S(1)}, u32[]{:S(2)}, u32[]{:S(2)}) collective-permute-start(bf16[640,512]{1,0:T(8,128)(2,1)S(1)} %collective-permute-done.7.refs_9_), channel_id=1, source_target_pairs={{0,16},{12,28},{16,0},{28,12},{1,17},{13,29},{17,1},{29,13},{2,18}... | collective-permute-start | bytes 1966088 | tf_op jit(solution)/shard_map/ppermute | solution.py:400
  56.1 17.4 %collective-permute-start.8 = (bf16[8,128,640]{2,1,0:T(8,128)(2,1)S(1)}, bf16[8,128,640]{2,1,0:T(8,128)(2,1)S(1)}, u32[]{:S(2)}, u32[]{:S(2)}) collective-permute-start(bf16[8,128,640]{2,1,0:T(8,128)(2,1)S(1)} %shard_map.175.refs_0_), channel_id=1, source_target_pairs={{0,1},{1,0},{2,3},{3,2},{4,5},{5,4},{6,7},{7,6},{8,9},{9,8},{10,11... | collective-permute-start | bytes 3932168 | tf_op jit(solution)/shard_map/ppermute | solution.py:50
  67.6 5.9 %collective-permute-start.14 = (bf16[8,128,640]{2,1,0:T(8,128)(2,1)S(1)}, bf16[8,128,640]{2,1,0:T(8,128)(2,1)S(1)}, u32[]{:S(2)}, u32[]{:S(2)}) collective-permute-start(bf16[8,128,640]{2,1,0:T(8,128)(2,1)S(1)} %collective-permute-done.3.refs_1_), channel_id=1, source_target_pairs={{0,1},{1,0},{2,3},{3,2},{4,5},{5,4},{6,7},{7,6},{8,9},{9,8},{10,11... | collective-permute-start | bytes 3932168 | tf_op jit(solution)/shard_map/ppermute | solution.py:50
  67.6 19.7 %collective-permute-start.16 = (bf16[640,512]{1,0:T(8,128)(2,1)S(1)}, bf16[640,512]{1,0:T(8,128)(2,1)S(1)}, u32[]{:S(2)}, u32[]{:S(2)}) collective-permute-start(bf16[640,512]{1,0:T(8,128)(2,1)S(1)} %collective-permute-done.10.refs_13_), channel_id=1, source_target_pairs={{0,16},{12,28},{16,0},{28,12},{1,17},{13,29},{17,1},{29,13},{2,18}... | collective-permute-start | bytes 1966088 | tf_op jit(solution)/shard_map/ppermute | solution.py:400
  71.0 16.2 %collective-permute-start.15 = (bf16[640,512]{1,0:T(8,128)(2,1)S(1)}, bf16[640,512]{1,0:T(8,128)(2,1)S(1)}, u32[]{:S(2)}, u32[]{:S(2)}) collective-permute-start(bf16[640,512]{1,0:T(8,128)(2,1)S(1)} %collective-permute-done.6.refs_12_), channel_id=1, source_target_pairs={{4,20},{8,24},{20,4},{24,8},{5,21},{9,25},{21,5},{25,9},{6,22},{10... | collective-permute-start | bytes 1966088 | tf_op jit(solution)/shard_map/ppermute | solution.py:400
  71.7 9.1 %copy-start.13 = (s32[1,8,16]{2,1,0:T(8,128)S(1)}, s32[1,8,16]{2,1,0:T(8,128)}, u32[]{:S(2)}) copy-start(s32[1,8,16]{2,1,0:T(8,128)} %param.26) | copy-start | bytes 1540
  71.8 9.1 %copy-start.14 = (s32[4,8]{1,0:T(4,128)S(1)}, s32[4,8]{1,0:T(4,128)}, u32[]{:S(2)}) copy-start(s32[4,8]{1,0:T(4,128)} %lengths_ref.3) | copy-start | bytes 388
  71.8 9.1 %copy-start.16 = (f32[128]{0:T(128)S(1)}, f32[128]{0:T(128)}, u32[]{:S(2)}) copy-start(f32[128]{0:T(128)} %param.20) | copy-start | bytes 1540
  71.8 9.1 %copy-start.17 = (f32[128]{0:T(128)S(1)}, f32[128]{0:T(128)}, u32[]{:S(2)}) copy-start(f32[128]{0:T(128)} %param.19) | copy-start | bytes 1540
  71.8 9.1 %copy-start.18 = (f32[1,128]{1,0:T(1,128)S(1)}, f32[1,128]{1,0:T(1,128)}, u32[]{:S(2)}) copy-start(f32[1,128]{1,0:T(1,128)} %constant.20.clone.refs_3_) | copy-start | bytes 1540
  71.8 9.1 %collective-permute-start.17 = (bf16[18,2560]{1,0:T(8,128)(2,1)S(1)}, bf16[18,2560]{1,0:T(8,128)(2,1)S(1)}, u32[]{:S(2)}, u32[]{:S(2)}) collective-permute-start(bf16[18,2560]{1,0:T(8,128)(2,1)S(1)} %fusion), channel_id=1, source_target_pairs={{0,8},{4,12},{8,0},{12,4},{1,9},{5,13},{9,1},{13,5},{2,10},{6,14},... | collective-permute-start | bytes 276488 | tf_op jit(solution)/shard_map/ppermute | solution.py:50
  73.5 7.4 %copy-start = (bf16[1,40,128,256]{3,2,1,0:T(8,128)(2,1)S(1)}, bf16[1,40,128,256]{3,2,1,0:T(8,128)(2,1)}, u32[]{:S(2)}) copy-start(bf16[1,40,128,256]{3,2,1,0:T(8,128)(2,1)} %param.24) | copy-start | bytes 7864324
  73.5 7.4 %copy-start.1 = (bf16[1,40,128,256]{3,2,1,0:T(8,128)(2,1)S(1)}, bf16[1,40,128,256]{3,2,1,0:T(8,128)(2,1)}, u32[]{:S(2)}) copy-start(bf16[1,40,128,256]{3,2,1,0:T(8,128)(2,1)} %param.25) | copy-start | bytes 7864324
  83.6 3.7 %collective-permute-start.18 = (f32[2,32,128]{2,1,0:T(8,128)S(1)}, f32[2,32,128]{2,1,0:T(8,128)S(1)}, u32[]{:S(2)}, u32[]{:S(2)}) collective-permute-start(f32[2,32,128]{2,1,0:T(8,128)S(1)} %get-tuple-element.55), channel_id=1, source_target_pairs={{0,8},{4,12},{1,9},{5,13},{2,10},{6,14},{3,11},{7,15},{16,24},{20,... | collective-permute-start | bytes 98312 | tf_op jit(solution)/shard_map/ppermute | solution.py:510
  84.9 2.4 %copy-start.8 = (f32[512,128]{1,0:T(8,128)S(1)}, f32[512,128]{1,0:T(8,128)}, u32[]{:S(2)}) copy-start(f32[512,128]{1,0:T(8,128)} %constant.18.clone.refs_7_) | copy-start | bytes 786436
  84.9 2.4 %copy-start.9 = (f32[512,128]{1,0:T(8,128)S(1)}, f32[512,128]{1,0:T(8,128)}, u32[]{:S(2)}) copy-start(f32[512,128]{1,0:T(8,128)} %constant.19.clone.refs_8_) | copy-start | bytes 786436
  (6 other events, 5.9 us)
